TPU v7x, 32 devices: a whole 2x2x4 slice. The times are simulated.
32 devices in a mesh: seq: 8 (over y, x, core), head: 4 (over z).
Axes of the slice: x: 2, y: 2, z: 4, core: 2. Of those that a mesh axis runs over, the one named last changes fastest.
Arguments:
- queries: bfloat16 [8192, 2048], P(('seq', 'head')), may hold values from -6 to 6
- keys_in: bfloat16 [8192, 2048], P(('seq', 'head')), may hold values from -6 to 6
- values_in: bfloat16 [8192, 2048], P(('seq', 'head')), may hold values from -6 to 6
- cotangent: bfloat16 [8192, 2048], P(('seq', 'head')), may hold values from -6 to 6
Outputs:
- attended: bfloat16 [8192, 2048], P(('seq', 'head'))
- grad_queries: bfloat16 [8192, 2048], P(('seq', 'head'))
- grad_keys: bfloat16 [8192, 2048], P(('seq', 'head'))
- grad_values: bfloat16 [8192, 2048], P(('seq', 'head'))
All inputs are finite; a program needn't handle non-finite values.
Results may differ from a plain program's by a relative error of at most 0.029.
Values may be sent and summed in bfloat16 or wider, within the bound.
No kernel may reach another device: no remote copies, remote signals or barrier semaphores. Data moves between devices by JAX's collectives and lax.ppermute only.
A program may use at most 128 MiB of HBM per device.

v0:
```python
import math

import jax
import jax.numpy as jnp
from jax import lax
from jax.sharding import PartitionSpec as P

HEADS = 16
HEAD_DIM = 128
BLOCK = 128
SUMMARY = 8


neg_fill = -1e30
tile_limit = 512


def block_view(matrix):
    return matrix.reshape(matrix.shape[0] // BLOCK, BLOCK, HEADS, HEAD_DIM)


def summary_rows_of(matrix):
    row_count = matrix.shape[0]
    picked = matrix.reshape(row_count // BLOCK, BLOCK, matrix.shape[1])[:, BLOCK - SUMMARY :, :]
    return picked.reshape(row_count // BLOCK * SUMMARY, matrix.shape[1])


def head_view(matrix):
    return matrix.reshape(matrix.shape[0], matrix.shape[1] // HEAD_DIM, HEAD_DIM)


def key_mask(query_block, row_start, tile_len):
    key_block = (row_start + lax.iota(jnp.int32, tile_len)) // SUMMARY
    return key_block[None, :] < query_block[:, None]


def tile_scores(query_rows, key_tile, scaling):
    return (
        jnp.einsum("ihe,jhe->hij", query_rows, key_tile, preferred_element_type=jnp.float32)
        * scaling
    )


def summary_stats(query_rows, query_block, key_all, tile_count, tile_len, scaling):
    group_heads = query_rows.shape[1]
    row_count = query_rows.shape[0]

    def stats_turn(step, carried):
        highest, norm_sum = carried
        row_start = step * tile_len
        key_tile = lax.dynamic_slice_in_dim(key_all, row_start, tile_len, 0)
        visible = key_mask(query_block, row_start, tile_len)[None]
        scores = jnp.where(visible, tile_scores(query_rows, key_tile, scaling), neg_fill)
        new_high = jnp.maximum(highest, jnp.max(scores, axis=-1))
        weights = jnp.where(visible, jnp.exp(scores - new_high[..., None]), 0.0)
        return (new_high, norm_sum * jnp.exp(highest - new_high) + jnp.sum(weights, axis=-1))

    start_state = (
        jnp.full((group_heads, row_count), neg_fill, jnp.float32),
        jnp.zeros((group_heads, row_count), jnp.float32),
    )
    return lax.fori_loop(0, tile_count, stats_turn, start_state)


def summary_output(
    query_rows, query_block, log_norm, key_all, value_all, tile_count, tile_len, scaling
):

    def output_turn(step, summed):
        row_start = step * tile_len
        key_tile = lax.dynamic_slice_in_dim(key_all, row_start, tile_len, 0)
        value_tile = lax.dynamic_slice_in_dim(value_all, row_start, tile_len, 0)
        visible = key_mask(query_block, row_start, tile_len)[None]
        weights = jnp.where(
            visible, jnp.exp(tile_scores(query_rows, key_tile, scaling) - log_norm[..., None]), 0.0
        )
        return summed + jnp.einsum(
            "hij,jhe->ihe",
            weights.astype(jnp.bfloat16),
            value_tile,
            preferred_element_type=jnp.float32,
        )

    return lax.fori_loop(0, tile_count, output_turn, jnp.zeros(query_rows.shape, jnp.float32))


def group_forward(
    query_rows, high_rows, norm_rows, query_block, key_all, value_all, tile_count, tile_len, scaling
):
    summary_high, summary_norm = summary_stats(
        query_rows, query_block, key_all, tile_count, tile_len, scaling
    )
    local_part_high = high_rows.T
    local_part_norm = norm_rows.T
    highest = jnp.maximum(local_part_high, summary_high)
    log_norm = highest + jnp.log(
        local_part_norm * jnp.exp(local_part_high - highest)
        + summary_norm * jnp.exp(summary_high - highest)
    )
    partial_value = summary_output(
        query_rows, query_block, log_norm, key_all, value_all, tile_count, tile_len, scaling
    )
    return (partial_value.reshape(query_rows.shape[0], -1), log_norm)


def summary_grads(
    query_rows,
    grad_rows,
    query_block,
    log_norm,
    delta,
    key_all,
    value_all,
    buffers,
    tile_count,
    tile_len,
    scaling,
):

    def grads_turn(step, carried):
        grad_query, key_grads, value_grads = carried
        row_start = step * tile_len
        key_tile = lax.dynamic_slice_in_dim(key_all, row_start, tile_len, 0)
        value_tile = lax.dynamic_slice_in_dim(value_all, row_start, tile_len, 0)
        visible = key_mask(query_block, row_start, tile_len)[None]
        probs = jnp.where(
            visible, jnp.exp(tile_scores(query_rows, key_tile, scaling) - log_norm[..., None]), 0.0
        )
        dprob = jnp.einsum(
            "ihe,jhe->hij", grad_rows, value_tile, preferred_element_type=jnp.float32
        )
        dscore = (probs * (dprob - delta[..., None])).astype(jnp.bfloat16)
        grad_query = grad_query + jnp.einsum(
            "hij,jhe->ihe", dscore, key_tile, preferred_element_type=jnp.float32
        )
        key_part = (
            jnp.einsum("hij,ihe->jhe", dscore, query_rows, preferred_element_type=jnp.float32)
            * scaling
        )
        value_part = jnp.einsum(
            "hij,ihe->jhe",
            probs.astype(jnp.bfloat16),
            grad_rows,
            preferred_element_type=jnp.float32,
        )
        key_grads = lax.dynamic_update_slice_in_dim(
            key_grads,
            lax.dynamic_slice_in_dim(key_grads, row_start, tile_len, 0) + key_part,
            row_start,
            0,
        )
        value_grads = lax.dynamic_update_slice_in_dim(
            value_grads,
            lax.dynamic_slice_in_dim(value_grads, row_start, tile_len, 0) + value_part,
            row_start,
            0,
        )
        return (grad_query, key_grads, value_grads)

    start_state = (jnp.zeros(query_rows.shape, jnp.float32), buffers[0], buffers[1])
    grad_query, key_grads, value_grads = lax.fori_loop(0, tile_count, grads_turn, start_state)
    return (grad_query, (key_grads, value_grads))


def on_device(queries, keys_in, values_in, cotangent):
    tokens = queries.shape[0]
    nblocks = tokens // BLOCK
    scaling = 1.0 / math.sqrt(HEAD_DIM)
    query_blocks = block_view(queries)
    key_blocks = block_view(keys_in)
    value_blocks = block_view(values_in)
    grad_blocks = block_view(cotangent)
    causal = lax.iota(jnp.int32, BLOCK)[:, None] >= lax.iota(jnp.int32, BLOCK)[None, :]
    local_scores = (
        jnp.einsum("bihe,bjhe->bhij", query_blocks, key_blocks, preferred_element_type=jnp.float32)
        * scaling
    )
    local_scores = jnp.where(causal, local_scores, neg_fill)
    local_high = jnp.max(local_scores, axis=-1)
    local_norm = jnp.sum(
        jnp.where(causal, jnp.exp(local_scores - local_high[..., None]), 0.0), axis=-1
    )
    high_tok = local_high.transpose(0, 2, 1).reshape(tokens, HEADS)
    norm_tok = local_norm.transpose(0, 2, 1).reshape(tokens, HEADS)
    query_h, grad_h, key_h, value_h, high_h, norm_h = (
        lax.all_to_all(
            queries.astype(jnp.float32), "head", split_axis=1, concat_axis=0, tiled=True
        ).astype(queries.dtype),
        lax.all_to_all(
            cotangent.astype(jnp.float32), "head", split_axis=1, concat_axis=0, tiled=True
        ).astype(cotangent.dtype),
        lax.all_to_all(
            keys_in.astype(jnp.float32), "head", split_axis=1, concat_axis=0, tiled=True
        ).astype(keys_in.dtype),
        lax.all_to_all(
            values_in.astype(jnp.float32), "head", split_axis=1, concat_axis=0, tiled=True
        ).astype(values_in.dtype),
        lax.all_to_all(high_tok, "head", split_axis=1, concat_axis=0, tiled=True),
        lax.all_to_all(norm_tok, "head", split_axis=1, concat_axis=0, tiled=True),
    )
    key_rows = summary_rows_of(key_h)
    value_rows = summary_rows_of(value_h)
    key_all, value_all = (
        lax.all_gather(key_rows, "seq", axis=0, tiled=True),
        lax.all_gather(value_rows, "seq", axis=0, tiled=True),
    )
    key_all = head_view(key_all)
    value_all = head_view(value_all)
    nkeys = key_all.shape[0]
    tile_len = min(tile_limit, nkeys)
    tile_total = nkeys // tile_len
    rows_here = query_h.shape[0]
    seq_pos = lax.axis_index("seq")
    query_d, grad_d, high_d, norm_d = (query_h, grad_h, high_h, norm_h)
    positions = seq_pos * rows_here + lax.iota(jnp.int32, rows_here)
    half_rows = rows_here // 2
    group_plans = [(0, half_rows, tile_total), (half_rows, half_rows, tile_total)]
    query_heads = head_view(query_d)
    grad_heads = head_view(grad_d)
    query_block = positions // BLOCK
    out_pieces = []
    lse_pieces = []
    for row_start, row_count, tile_count in group_plans:
        row_stop = row_start + row_count
        part_out, part_lse = group_forward(
            query_heads[row_start:row_stop],
            high_d[row_start:row_stop],
            norm_d[row_start:row_stop],
            query_block[row_start:row_stop],
            key_all,
            value_all,
            tile_count,
            tile_len,
            scaling,
        )
        out_pieces.append(part_out)
        lse_pieces.append(part_lse)
    out_heads = jnp.concatenate(out_pieces, axis=0)
    lse_heads = jnp.concatenate([lse_part.T for lse_part in lse_pieces], axis=0)
    out_summary, lse_tok = (
        lax.all_to_all(out_heads, "head", split_axis=0, concat_axis=1, tiled=True),
        lax.all_to_all(lse_heads, "head", split_axis=0, concat_axis=1, tiled=True),
    )
    lse_blocks = lse_tok.reshape(nblocks, BLOCK, HEADS).transpose(0, 2, 1)
    local_probs = jnp.where(causal, jnp.exp(local_scores - lse_blocks[..., None]), 0.0)
    local_pb = local_probs.astype(jnp.bfloat16)
    local_out = jnp.einsum(
        "bhij,bjhe->bihe", local_pb, value_blocks, preferred_element_type=jnp.float32
    )
    attended = (local_out.reshape(tokens, -1) + out_summary).astype(jnp.bfloat16)
    delta_blocks = jnp.sum(
        grad_blocks.astype(jnp.float32) * block_view(attended).astype(jnp.float32), axis=-1
    )
    delta_tok = delta_blocks.reshape(tokens, HEADS)
    local_dprob = jnp.einsum(
        "bihe,bjhe->bhij", grad_blocks, value_blocks, preferred_element_type=jnp.float32
    )
    local_ds = (local_probs * (local_dprob - delta_blocks.transpose(0, 2, 1)[..., None])).astype(
        jnp.bfloat16
    )
    local_dq = jnp.einsum(
        "bhij,bjhe->bihe", local_ds, key_blocks, preferred_element_type=jnp.float32
    )
    local_dk = (
        jnp.einsum("bhij,bihe->bjhe", local_ds, query_blocks, preferred_element_type=jnp.float32)
        * scaling
    )
    local_dv = jnp.einsum(
        "bhij,bihe->bjhe", local_pb, grad_blocks, preferred_element_type=jnp.float32
    )
    delta_h = lax.all_to_all(delta_tok, "head", split_axis=1, concat_axis=0, tiled=True)
    group_heads = key_all.shape[1]
    buffers = (
        jnp.zeros((nkeys, group_heads, HEAD_DIM), jnp.float32),
        jnp.zeros((nkeys, group_heads, HEAD_DIM), jnp.float32),
    )
    dq_pieces = []
    for plan, part_lse in zip(group_plans, lse_pieces):
        row_start, row_count, tile_count = plan
        row_stop = row_start + row_count
        part_dq, buffers = summary_grads(
            query_heads[row_start:row_stop],
            grad_heads[row_start:row_stop],
            query_block[row_start:row_stop],
            part_lse,
            delta_h[row_start:row_stop].T,
            key_all,
            value_all,
            buffers,
            tile_count,
            tile_len,
            scaling,
        )
        dq_pieces.append(part_dq.reshape(row_count, -1))
    dq_heads = jnp.concatenate(dq_pieces, axis=0)
    key_grad_rows, value_grad_rows = (
        lax.psum_scatter(buffers[0].reshape(nkeys, -1), "seq", scatter_dimension=0, tiled=True),
        lax.psum_scatter(buffers[1].reshape(nkeys, -1), "seq", scatter_dimension=0, tiled=True),
    )
    dq_tok, key_tok_rows, value_tok_rows = (
        lax.all_to_all(dq_heads, "head", split_axis=0, concat_axis=1, tiled=True),
        lax.all_to_all(key_grad_rows, "head", split_axis=0, concat_axis=1, tiled=True),
        lax.all_to_all(value_grad_rows, "head", split_axis=0, concat_axis=1, tiled=True),
    )
    grad_queries = ((local_dq.reshape(tokens, -1) + dq_tok) * scaling).astype(jnp.bfloat16)
    key_grads = local_dk.reshape(nblocks, BLOCK, -1)
    key_extra = key_tok_rows.reshape(nblocks, SUMMARY, -1)
    grad_keys = jnp.concatenate(
        [key_grads[:, : BLOCK - SUMMARY], key_grads[:, BLOCK - SUMMARY :] + key_extra], axis=1
    )
    grad_keys = grad_keys.reshape(tokens, -1).astype(jnp.bfloat16)
    value_grads = local_dv.reshape(nblocks, BLOCK, -1)
    value_extra = value_tok_rows.reshape(nblocks, SUMMARY, -1)
    grad_values = jnp.concatenate(
        [value_grads[:, : BLOCK - SUMMARY], value_grads[:, BLOCK - SUMMARY :] + value_extra], axis=1
    )
    grad_values = grad_values.reshape(tokens, -1).astype(jnp.bfloat16)
    return (attended, grad_queries, grad_keys, grad_values)


def solution(mesh):
    return jax.shard_map(
        on_device,
        mesh=mesh,
        in_specs=(
            P(("seq", "head"), None),
            P(("seq", "head"), None),
            P(("seq", "head"), None),
            P(("seq", "head"), None),
        ),
        out_specs=(
            P(("seq", "head"), None),
            P(("seq", "head"), None),
            P(("seq", "head"), None),
            P(("seq", "head"), None),
        ),
        check_vma=False,
    )
```

profile of v0, /device:TPU:0, one launch (start us, length us, event | category | flops | bytes accessed | tf_op | source)
XLA Modules:
  0.0 395.2 jit_solution(18367277619202601298)
XLA Ops:
  14.5 6.3 %all-to-all-start = ((f32[256,4,4]{0,2,1:T(4,128)}), f32[256,4,4]{0,2,1:T(4,128)S(1)}, u32[]{:S(2)}, u32[]{:S(2)}) async-start(f32[256,4,4]{0,2,1:T(4,128)} %all_to_all.150), calls=%async_computation | async-start | bytes 32768 | tf_op jit(solution)/shard_map/all_to_all | solution.py:198
  21.9 4.6 %all-to-all-done = f32[256,4,4]{0,2,1:T(4,128)S(1)} async-done(((f32[256,4,4]{0,2,1:T(4,128)}), f32[256,4,4]{0,2,1:T(4,128)S(1)}, u32[]{:S(2)}, u32[]{:S(2)}) %all-to-all-start) | async-done | bytes 16416 | tf_op jit(solution)/shard_map/all_to_all | solution.py:198
  30.8 4.5 %all-to-all-done.3 = f32[256,4,4]{0,2,1:T(4,128)S(1)} async-done(((f32[256,4,4]{0,2,1:T(4,128)}), f32[256,4,4]{0,2,1:T(4,128)S(1)}, u32[]{:S(2)}, u32[]{:S(2)}) %all-to-all-start.3) | async-done | bytes 16416 | tf_op jit(solution)/shard_map/all_to_all | solution.py:199
  40.1 22.1 %all-to-all-done.1 = bf16[256,4,512]{2,0,1:T(8,128)(2,1)S(1)} async-done(((bf16[256,4,512]{2,0,1:T(8,128)(2,1)}), bf16[256,4,512]{2,0,1:T(8,128)(2,1)S(1)}, u32[]{:S(2)}, u32[]{:S(2)}) %all-to-all-start.1) | async-done | bytes 1048608 | tf_op jit(solution)/shard_map/all_to_all | solution.py:186
  62.2 3.5 all-to-all-start.2
  67.1 23.8 %all-to-all-done.2 = bf16[256,4,512]{0,2,1:T(8,128)(2,1)S(1)} async-done(((bf16[256,4,512]{0,2,1:T(8,128)(2,1)}), bf16[256,4,512]{0,2,1:T(8,128)(2,1)S(1)}, u32[]{:S(2)}, u32[]{:S(2)}) %all-to-all-start.2) | async-done | bytes 1048608 | tf_op jit(solution)/shard_map/all_to_all | solution.py:192
  90.9 4.4 %all-to-all-start.5 = ((bf16[256,4,512]{0,2,1:T(8,128)(2,1)}), bf16[256,4,512]{0,2,1:T(8,128)(2,1)}, u32[]{:S(2)}, u32[]{:S(2)}) async-start(bf16[256,4,512]{0,2,1:T(8,128)(2,1)} %bitcast.254), calls=%async_computation.5 | async-start | bytes 2097152 | tf_op jit(solution)/shard_map/all_to_all | solution.py:195
  100.3 9.8 %all_gather.6 = bf16[512,512]{1,0:T(8,128)(2,1)S(1)} all-gather(bf16[64,512]{1,0:T(8,128)(2,1)S(1)} %slice_bitcast_fusion.1), channel_id=1, replica_groups=mesh['seq'=8,'head'=4] {'seq'}, dimensions={0}, use_global_device_ids=true | all-gather | bytes 589824 | tf_op jit(solution)/shard_map/all_gather | solution.py:204
  110.4 10.2 %all-to-all-done.5 = bf16[256,4,512]{0,2,1:T(8,128)(2,1)} async-done(((bf16[256,4,512]{0,2,1:T(8,128)(2,1)}), bf16[256,4,512]{0,2,1:T(8,128)(2,1)}, u32[]{:S(2)}, u32[]{:S(2)}) %all-to-all-start.5) | async-done | bytes 1048608 | tf_op jit(solution)/shard_map/all_to_all | solution.py:195
  127.2 11.1 %all_gather.7 = bf16[512,512]{1,0:T(8,128)(2,1)} all-gather(bf16[64,512]{1,0:T(8,128)(2,1)S(1)} %slice_bitcast_fusion), channel_id=1, replica_groups=mesh['seq'=8,'head'=4] {'seq'}, dimensions={0}, use_global_device_ids=true | all-gather | bytes 589824 | tf_op jit(solution)/shard_map/all_gather | solution.py:205
  149.3 4.2 %fusion.47 = f32[4,512,128]{1,2,0:T(8,128)} fusion(bf16[512,4,128]{0,2,1:T(8,128)(2,1)S(1)} %bitcast.275, f32[4,512,512]{1,2,0:T(8,128)} %copy-done.1, f32[4,512]{1,0:T(4,128)S(1)} %log_add_fusion, pred[512,512]{0,1:T(8,128)(4,1)S(1)} %get-tuple-element.131), kind=kOutput, calls=%fused_computation.109 | convolution fusion | flops 272629760 | bytes 6037504 | tf_op jit(solution)/shard_map/while/body/eval_jaxpr/hij,jhe->ihe/dot_general | solution.py:77
  156.7 5.1 %all-to-all-start.4 = ((f32[4,256,4]{1,2,0:T(4,128)}), f32[4,256,4]{1,2,0:T(4,128)S(1)}, u32[]{:S(2)}, u32[]{:S(2)}) async-start(f32[4,256,4]{1,2,0:T(4,128)} %bitcast.18), calls=%async_computation.4 | async-start | bytes 32768 | tf_op jit(solution)/shard_map/all_to_all | solution.py:242
  167.4 3.8 all-to-all-start.6
  188.0 4.4 %fusion.49 = f32[4,512,128]{1,2,0:T(8,128)} fusion(bf16[512,4,128]{0,2,1:T(8,128)(2,1)} %copy.224, f32[4,512,512]{1,2,0:T(8,128)} %copy-done.3, f32[4,512]{1,0:T(4,128)S(1)} %log_add_fusion.1, pred[512,512]{0,1:T(8,128)(4,1)} %copy-done.24), kind=kOutput, calls=%fused_computation.110 | convolution fusion | flops 272629760 | bytes 6037504 | tf_op jit(solution)/shard_map/while/body/eval_jaxpr/hij,ihe->jhe/dot_general | solution.py:140
  192.4 26.3 %all-to-all-done.6 = f32[4,256,512]{2,1,0:T(8,128)S(1)} async-done(((f32[4,256,512]{2,1,0:T(8,128)}), f32[4,256,512]{2,1,0:T(8,128)S(1)}, u32[]{:S(2)}, u32[]{:S(2)}) %all-to-all-start.6) | async-done | bytes 2097184 | tf_op jit(solution)/shard_map/all_to_all | solution.py:241
  227.4 4.9 %multiply_reduce_fusion = (f32[2,128,16]{1,2,0:T(8,128)S(1)}, f32[2,128,16,128]{1,3,2,0:T(8,128)}) fusion(bf16[2,128,16,128]{1,3,2,0:T(8,128)(2,1)} %copy.190, f32[2,128,16,128]{1,3,2,0:T(8,128)} %copy.192, f32[2,16,128,128]{2,3,1,0:T(8,128)} %copy-done, f32[2,16,128]{2,1,0:T(8,128)S(1)} %copy.176, pred[128,128]{0,1:T(8,128)(4,1)S(1)} %iota_compare_fusion, ...), kind=kOutput, calls=%fused_computation.22 | convolution fusion | flops 138932224 | bytes 8437760 | tf_op jit(solution)/shard_map/bhij,bjhe->bihe/dot_general | solution.py:247
  236.3 4.7 %convolution_add_fusion = f32[4,512,128]{1,2,0:T(8,128)} fusion(f32[4,512,128]{1,2,0:T(8,128)} %fusion.49, bf16[512,4,128]{0,2,1:T(8,128)(2,1)} %copy.226, f32[4,512,512]{1,2,0:T(8,128)} %copy-done.1, f32[4,512]{1,0:T(4,128)S(1)} %log_add_fusion, pred[512,512]{0,1:T(8,128)(4,1)S(1)} %get-tuple-element.131), kind=kOutput, calls=%fused_computation.31 | convolution fusion | flops 272891904 | bytes 7086080 | tf_op jit(solution)/shard_map/while/body/eval_jaxpr/hij,ihe->jhe/dot_general | solution.py:140
  243.7 4.3 %multiply_convert_fusion.1 = bf16[4,512,512]{1,2,0:T(8,128)(2,1)S(1)} fusion(f32[4,512,512]{1,2,0:T(8,128)} %copy-done.3, bf16[512,4,128]{0,2,1:T(8,128)(2,1)} %copy.224, bf16[512,4,128]{0,2,1:T(8,128)(2,1)} %bitcast.273, f32[4,512]{1,0:T(4,128)S(1)} %bitcast.298, f32[4,512]{1,0:T(4,128)S(1)} %log_add_fusion.1, pred[512,512]{0,1:T(8,128)(4,1)} %copy-done.24), kind=kOutput, calls=%fused_computation.1 | convolution fusion | flops 274726912 | bytes 7618560 | tf_op jit(solution)/shard_map/while/body/eval_jaxpr/ihe,jhe->hij/dot_general | solution.py:129
  256.1 24.2 %reduce-scatter.5.cloned.1.call-done = f32[64,512]{1,0:T(8,128)} async-done(((f32[512,512]{1,0:T(8,128)}), f32[64,512]{1,0:T(8,128)}) %reduce-scatter.5.cloned.1.call-update) | async-done | bytes 131088 | tf_op jit(solution)/shard_map/reduce_scatter | solution.py:298
  280.3 4.6 %all-to-all-start.11 = ((f32[4,16,512]{2,1,0:T(8,128)}), f32[4,16,512]{2,1,0:T(8,128)S(1)}, u32[]{:S(2)}, u32[]{:S(2)}) async-start(f32[4,16,512]{2,1,0:T(8,128)} %bitcast.279), calls=%async_computation.13 | async-start | bytes 262144 | tf_op jit(solution)/shard_map/all_to_all | solution.py:303
  290.9 28.5 %reduce-scatter.3.cloned.1.call-done = f32[64,512]{1,0:T(8,128)} async-done(((f32[512,512]{1,0:T(8,128)}), f32[64,512]{1,0:T(8,128)}) %reduce-scatter.3.cloned.1.call-update) | async-done | bytes 131088 | tf_op jit(solution)/shard_map/reduce_scatter | solution.py:297
  319.5 4.9 %all-to-all-start.10 = ((f32[4,16,512]{2,1,0:T(8,128)}), f32[4,16,512]{2,1,0:T(8,128)S(1)}, u32[]{:S(2)}, u32[]{:S(2)}) async-start(f32[4,16,512]{2,1,0:T(8,128)} %bitcast.280), calls=%async_computation.11 | async-start | bytes 262144 | tf_op jit(solution)/shard_map/all_to_all | solution.py:302
  330.9 5.1 %all-to-all-start.9 = ((f32[4,256,512]{2,1,0:T(8,128)}), f32[4,256,512]{2,1,0:T(8,128)}, u32[]{:S(2)}, u32[]{:S(2)}) async-start(f32[4,256,512]{2,1,0:T(8,128)} %bitcast.239), calls=%async_computation.9 | async-start | bytes 4194304 | tf_op jit(solution)/shard_map/all_to_all | solution.py:301
  374.2 9.5 %all-to-all-done.9 = f32[4,256,512]{2,1,0:T(8,128)} async-done(((f32[4,256,512]{2,1,0:T(8,128)}), f32[4,256,512]{2,1,0:T(8,128)}, u32[]{:S(2)}, u32[]{:S(2)}) %all-to-all-start.9) | async-done | bytes 2097184 | tf_op jit(solution)/shard_map/all_to_all | solution.py:301
  (167 shorter events, 145.4 us)
Async XLA Ops:
  13.8 17.0 %copy-start = (f32[2,16,128,128]{2,3,1,0:T(8,128)}, f32[2,16,128,128]{2,3,1,0:T(8,128)S(1)}, u32[]{:S(2)}) copy-start(f32[2,16,128,128]{2,3,1,0:T(8,128)S(1)} %get-tuple-element.145) | copy-start | bytes 6291460
  14.5 11.9 %all-to-all-start = ((f32[256,4,4]{0,2,1:T(4,128)}), f32[256,4,4]{0,2,1:T(4,128)S(1)}, u32[]{:S(2)}, u32[]{:S(2)}) async-start(f32[256,4,4]{0,2,1:T(4,128)} %all_to_all.150), calls=%async_computation | async-start | bytes 32768 | tf_op jit(solution)/shard_map/all_to_all | solution.py:198
  26.4 8.8 %all-to-all-start.3 = ((f32[256,4,4]{0,2,1:T(4,128)}), f32[256,4,4]{0,2,1:T(4,128)S(1)}, u32[]{:S(2)}, u32[]{:S(2)}) async-start(f32[256,4,4]{0,2,1:T(4,128)} %all_to_all.159), calls=%async_computation.3 | async-start | bytes 32768 | tf_op jit(solution)/shard_map/all_to_all | solution.py:199
  30.8 8.0 %copy-start.12 = (bf16[256,2048]{1,0:T(8,128)(2,1)S(1)}, bf16[256,2048]{1,0:T(8,128)(2,1)}, u32[]{:S(2)}) copy-start(bf16[256,2048]{1,0:T(8,128)(2,1)} %param.5) | copy-start | bytes 3145732
  35.3 26.9 %all-to-all-start.1 = ((bf16[256,4,512]{2,0,1:T(8,128)(2,1)}), bf16[256,4,512]{2,0,1:T(8,128)(2,1)S(1)}, u32[]{:S(2)}, u32[]{:S(2)}) async-start(bf16[256,4,512]{2,0,1:T(8,128)(2,1)} %bitcast.257), calls=%async_computation.1 | async-start | bytes 2097152 | tf_op jit(solution)/shard_map/all_to_all | solution.py:186
  38.8 26.9 %copy-start.14 = (bf16[256,2048]{1,0:T(8,128)(2,1)S(1)}, bf16[256,2048]{1,0:T(8,128)(2,1)}, u32[]{:S(2)}) copy-start(bf16[256,2048]{1,0:T(8,128)(2,1)} %param.6) | copy-start | bytes 3145732
  62.2 28.7 %all-to-all-start.2 = ((bf16[256,4,512]{0,2,1:T(8,128)(2,1)}), bf16[256,4,512]{0,2,1:T(8,128)(2,1)S(1)}, u32[]{:S(2)}, u32[]{:S(2)}) async-start(bf16[256,4,512]{0,2,1:T(8,128)(2,1)} %bitcast.255), calls=%async_computation.2 | async-start | bytes 2097152 | tf_op jit(solution)/shard_map/all_to_all | solution.py:192
  65.7 29.6 %copy-start.13 = (bf16[256,2048]{1,0:T(8,128)(2,1)S(1)}, bf16[256,2048]{1,0:T(8,128)(2,1)}, u32[]{:S(2)}) copy-start(bf16[256,2048]{1,0:T(8,128)(2,1)} %param.7) | copy-start | bytes 3145732
  90.9 5.5 %copy-start.19 = (bf16[256,4,512]{0,2,1:T(8,128)(2,1)}, bf16[256,4,512]{0,2,1:T(8,128)(2,1)S(1)}, u32[]{:S(2)}) copy-start(bf16[256,4,512]{0,2,1:T(8,128)(2,1)S(1)} %all-to-all-done.2) | copy-start | bytes 3145732
  90.9 5.9 %copy-start.18 = (bf16[256,4,512]{2,0,1:T(8,128)(2,1)S(1)}, bf16[256,4,512]{2,0,1:T(8,128)(2,1)}, u32[]{:S(2)}) copy-start(bf16[256,4,512]{2,0,1:T(8,128)(2,1)} %copy-done.17) | copy-start | bytes 3145732
  90.9 29.7 %all-to-all-start.5 = ((bf16[256,4,512]{0,2,1:T(8,128)(2,1)}), bf16[256,4,512]{0,2,1:T(8,128)(2,1)}, u32[]{:S(2)}, u32[]{:S(2)}) async-start(bf16[256,4,512]{0,2,1:T(8,128)(2,1)} %bitcast.254), calls=%async_computation.5 | async-start | bytes 2097152 | tf_op jit(solution)/shard_map/all_to_all | solution.py:195
  96.8 47.9 %copy-start.24 = (pred[512,512]{0,1:T(8,128)(4,1)}, pred[512,512]{0,1:T(8,128)(4,1)S(1)}, u32[]{:S(2)}) copy-start(pred[512,512]{0,1:T(8,128)(4,1)S(1)} %get-tuple-element.130) | copy-start | bytes 786436
  97.4 42.9 %copy-start.8 = (bf16[512,4,128]{0,2,1:T(8,128)(2,1)}, bf16[512,4,128]{0,2,1:T(8,128)(2,1)S(1)}, u32[]{:S(2)}) copy-start(bf16[512,4,128]{0,2,1:T(8,128)(2,1)S(1)} %copy.213) | copy-start | bytes 1572868
  120.6 36.1 %all-to-all-start.7 = ((bf16[256,4,512]{2,0,1:T(8,128)(2,1)}), bf16[256,4,512]{2,0,1:T(8,128)(2,1)S(1)}, u32[]{:S(2)}, u32[]{:S(2)}) async-start(bf16[256,4,512]{2,0,1:T(8,128)(2,1)} %bitcast.227), calls=%async_computation.7 | async-start | bytes 2097152 | tf_op jit(solution)/shard_map/all_to_all | solution.py:189
  156.7 8.1 %copy-start.15 = (bf16[256,4,512]{2,0,1:T(8,128)(2,1)}, bf16[256,4,512]{2,0,1:T(8,128)(2,1)S(1)}, u32[]{:S(2)}) copy-start(bf16[256,4,512]{2,0,1:T(8,128)(2,1)S(1)} %all-to-all-done.7) | copy-start | bytes 3145732
  156.7 10.7 %all-to-all-start.4 = ((f32[4,256,4]{1,2,0:T(4,128)}), f32[4,256,4]{1,2,0:T(4,128)S(1)}, u32[]{:S(2)}, u32[]{:S(2)}) async-start(f32[4,256,4]{1,2,0:T(4,128)} %bitcast.18), calls=%async_computation.4 | async-start | bytes 32768 | tf_op jit(solution)/shard_map/all_to_all | solution.py:242
  167.4 51.3 %all-to-all-start.6 = ((f32[4,256,512]{2,1,0:T(8,128)}), f32[4,256,512]{2,1,0:T(8,128)S(1)}, u32[]{:S(2)}, u32[]{:S(2)}) async-start(f32[4,256,512]{2,1,0:T(8,128)} %bitcast.240), calls=%async_computation.6 | async-start | bytes 4194304 | tf_op jit(solution)/shard_map/all_to_all | solution.py:241
  233.0 10.6 %all-to-all-start.8 = ((f32[256,4,4]{0,2,1:T(4,128)}), f32[256,4,4]{0,2,1:T(4,128)S(1)}, u32[]{:S(2)}, u32[]{:S(2)}) async-start(f32[256,4,4]{0,2,1:T(4,128)} %all_to_all.176), calls=%async_computation.8 | async-start | bytes 32768 | tf_op jit(solution)/shard_map/all_to_all | solution.py:271
  236.3 44.0 %reduce-scatter.5.cloned.1.call-start = ((), (), s32[]{:S(2)}) async-start(), calls=%async_computation.15 | async-start | bytes 1179648 | tf_op jit(solution)/shard_map/reduce_scatter | solution.py:298
  243.6 75.9 %reduce-scatter.3.cloned.1.call-start = ((), (), s32[]{:S(2)}) async-start(), calls=%async_computation.14 | async-start | bytes 1179648 | tf_op jit(solution)/shard_map/reduce_scatter | solution.py:297
  243.7 5.1 %copy-start.2 = (f32[4,512,512]{1,2,0:T(8,128)S(1)}, f32[4,512,512]{1,2,0:T(8,128)}, u32[]{:S(2)}) copy-start(f32[4,512,512]{1,2,0:T(8,128)} %copy-done.1) | copy-start | bytes 12582916
  280.3 10.7 %all-to-all-start.11 = ((f32[4,16,512]{2,1,0:T(8,128)}), f32[4,16,512]{2,1,0:T(8,128)S(1)}, u32[]{:S(2)}, u32[]{:S(2)}) async-start(f32[4,16,512]{2,1,0:T(8,128)} %bitcast.279), calls=%async_computation.13 | async-start | bytes 262144 | tf_op jit(solution)/shard_map/all_to_all | solution.py:303
  319.5 11.4 %all-to-all-start.10 = ((f32[4,16,512]{2,1,0:T(8,128)}), f32[4,16,512]{2,1,0:T(8,128)S(1)}, u32[]{:S(2)}, u32[]{:S(2)}) async-start(f32[4,16,512]{2,1,0:T(8,128)} %bitcast.280), calls=%async_computation.11 | async-start | bytes 262144 | tf_op jit(solution)/shard_map/all_to_all | solution.py:302
  330.9 52.7 %all-to-all-start.9 = ((f32[4,256,512]{2,1,0:T(8,128)}), f32[4,256,512]{2,1,0:T(8,128)}, u32[]{:S(2)}, u32[]{:S(2)}) async-start(f32[4,256,512]{2,1,0:T(8,128)} %bitcast.239), calls=%async_computation.9 | async-start | bytes 4194304 | tf_op jit(solution)/shard_map/all_to_all | solution.py:301
  (18 other events, 42.4 us)
Sparse Core Ops, SparseCore 0:
  243.7 36.4 reduce-scatter.4
  283.4 35.9 reduce-scatter.2
where the time goes:
time: 402 us; the launch traced here: 395 us
  waiting for transfers between devices  159 us (40%)
  local copies, waits for them, and re-layouts  86.3 us (21%)
  starting transfers between devices  51.3 us (13%)
  matrix products  46.7 us (12%)
  blocking collectives  20.9 us (5%)
  other arithmetic  15.7 us (4%)
  between operations  15.1 us (4%)
    reduce_scatter x1, waiting for transfers between devices, on_device(): lax.psum_scatter(buffers[0].reshape(nkeys, -1), 'seq', scatter_dimension=...  28.5 us
    all_to_all x1, waiting for transfers between devices, on_device(): lax.all_to_all(out_heads, 'head', split_axis=0, concat_axis=1, tiled=True)  26.3 us
    reduce_scatter x1, waiting for transfers between devices, on_device(): lax.psum_scatter(buffers[1].reshape(nkeys, -1), 'seq', scatter_dimension=...  24.2 us
    all_to_all x1, waiting for transfers between devices, on_device(): lax.all_to_all(keys_in.astype(jnp.float32), 'head', split_axis=1, concat_...  23.8 us
    all_to_all x1, waiting for transfers between devices, on_device(): lax.all_to_all(queries.astype(jnp.float32), 'head', split_axis=1, concat_...  22.1 us
    unnamed x64, local copies, waits for them, and re-layouts  18.7 us
    all_gather x1, blocking collectives, on_device(): lax.all_gather(value_rows, 'seq', axis=0, tiled=True)  11.1 us
    all_to_all x1, waiting for transfers between devices, on_device(): lax.all_to_all(values_in.astype(jnp.float32), 'head', split_axis=1, conca...  10.2 us
  transfers between devices with their start and end apart: 14, of which 11 were waited for; matrix products, arithmetic and copies ran while one was open for 30% of the time, Pallas kernels for 0%

commit v1 on v0

v1 whole, which is shorter than its diff:
```python
import functools
import math

import jax
import jax.numpy as jnp
from jax import lax
from jax.experimental import pallas as pl
from jax.experimental.pallas import tpu as pltpu
from jax.sharding import PartitionSpec as P

HEADS = 16
HEAD_DIM = 128
BLOCK = 128
SUMMARY = 8

neg_fill = -1e30
scaling = 1.0 / math.sqrt(HEAD_DIM)
chunk_heads = (8, 8)
vmem_bytes = 48 * 1024 * 1024


def dot(left, right, left_dim, right_dim):
    return lax.dot_general(
        left, right, (((left_dim,), (right_dim,)), ((), ())), preferred_element_type=jnp.float32
    )


def summary_rows(matrix, start, width):
    rows = [
        lax.slice(matrix, (b * BLOCK + BLOCK - SUMMARY, start), ((b + 1) * BLOCK, start + width))
        for b in range(matrix.shape[0] // BLOCK)
    ]
    return jnp.concatenate(rows, axis=0)


def attention_body(n_sum, n_cols, n_alias, *refs):
    q_ref, k_ref, v_ref, g_ref, local_bias, far_bias = refs[:6]
    col_refs = refs[6 : 6 + n_cols]
    out_refs = refs[6 + n_cols + n_alias :]
    o_ref, dq_ref, dk_ref, dv_ref, near_ref, own_ref, other_ref = out_refs
    q = q_ref[...]
    g = g_ref[...]
    k_loc = k_ref[...]
    v_loc = v_ref[...]
    n_loc = k_loc.shape[0]
    k_far = jnp.concatenate(
        [ref[j, :n_sum, :] for ref in col_refs for j in range(ref.shape[0])], axis=0
    )
    v_far = jnp.concatenate(
        [ref[j, n_sum:, :] for ref in col_refs for j in range(ref.shape[0])], axis=0
    )
    bias_far = far_bias[...]
    bias_far = jnp.concatenate([bias_far] * (q.shape[0] // bias_far.shape[1]), axis=1)
    s_loc = dot(k_loc, q, 1, 1) + local_bias[...]
    s_far = dot(k_far, q, 1, 1) + bias_far
    high = jnp.maximum(
        jnp.max(s_loc, axis=0, keepdims=True), jnp.max(s_far, axis=0, keepdims=True)
    )
    e_loc = jnp.exp((s_loc - high) * scaling)
    e_far = jnp.exp((s_far - high) * scaling)
    norm = jnp.sum(e_loc, axis=0, keepdims=True) + jnp.sum(e_far, axis=0, keepdims=True)
    inv = 1.0 / norm
    p_loc = e_loc * inv
    p_far = e_far * inv
    pb_loc = p_loc.astype(jnp.bfloat16)
    pb_far = p_far.astype(jnp.bfloat16)
    out_t = dot(v_loc, pb_loc, 0, 0) + dot(v_far, pb_far, 0, 0)
    out = out_t.T.astype(jnp.bfloat16)
    o_ref[...] = out
    g_t = g.astype(jnp.float32).T
    delta = jnp.sum(g_t * out_t.astype(jnp.bfloat16).astype(jnp.float32), axis=0, keepdims=True)
    ds_loc = (p_loc * (dot(v_loc, g, 1, 1) - delta)).astype(jnp.bfloat16)
    ds_far = (p_far * (dot(v_far, g, 1, 1) - delta)).astype(jnp.bfloat16)
    dq_t = dot(k_loc, ds_loc, 0, 0) + dot(k_far, ds_far, 0, 0)
    dq_ref[...] = (dq_t * scaling).T.astype(jnp.bfloat16)
    dk_loc = dot(ds_loc, q, 1, 0) * scaling
    dv_loc = dot(pb_loc, g, 1, 0)
    dk_ref[...] = dk_loc.astype(jnp.bfloat16)
    dv_ref[...] = dv_loc.astype(jnp.bfloat16)
    near = []
    for part in (dk_loc, dv_loc):
        for b in range(n_loc // BLOCK):
            near.append(part[(b + 1) * BLOCK - SUMMARY : (b + 1) * BLOCK, :])
    near_ref[...] = jnp.concatenate(near, axis=0)
    dk_far = (dot(ds_far, q, 1, 0) * scaling).astype(jnp.bfloat16)
    dv_far = dot(pb_far, g, 1, 0).astype(jnp.bfloat16)
    row = 0
    for half in (own_ref, other_ref):
        for c in range(half.shape[0]):
            for j in range(half.shape[1]):
                half[c, j, :n_sum, :] = dk_far[row : row + n_sum]
                half[c, j, n_sum:, :] = dv_far[row : row + n_sum]
                row += n_sum


def attention(q, k, v, g, local_bias, far_bias, cols, earlier, first, heads):
    tokens, width = q.shape
    n_cols = len(cols)
    nz, rows, chunk_width = cols[0].shape
    nkeys = far_bias.shape[0]
    head_spec = pl.BlockSpec((tokens, HEAD_DIM), lambda h: (0, first + h))
    col_spec = pl.BlockSpec((nz, rows, HEAD_DIM), lambda h: (0, 0, h))
    grads_shape = jax.ShapeDtypeStruct((n_cols // 2, nz, rows, chunk_width), jnp.bfloat16)
    grads_spec = pl.BlockSpec((n_cols // 2, nz, rows, HEAD_DIM), lambda h: (0, 0, 0, h))
    full = jax.ShapeDtypeStruct((tokens, width), jnp.bfloat16)
    return pl.pallas_call(
        functools.partial(attention_body, rows // 2, n_cols, len(earlier)),
        grid=(heads,),
        in_specs=[head_spec] * 4
        + [
            pl.BlockSpec(local_bias.shape, lambda h: (0, 0)),
            pl.BlockSpec(far_bias.shape, lambda h: (0, 0)),
        ]
        + [col_spec] * n_cols
        + [pl.BlockSpec(memory_space=pl.ANY)] * len(earlier),
        out_specs=[head_spec] * 4
        + [pl.BlockSpec((rows, HEAD_DIM), lambda h: (0, h)), grads_spec, grads_spec],
        out_shape=[full] * 4
        + [jax.ShapeDtypeStruct((rows, chunk_width), jnp.float32), grads_shape, grads_shape],
        input_output_aliases={6 + n_cols + i: i for i in range(len(earlier))},
        compiler_params=pltpu.CompilerParams(vmem_limit_bytes=vmem_bytes),
        cost_estimate=pl.CostEstimate(
            flops=heads * 12 * tokens * (tokens + nkeys) * HEAD_DIM,
            bytes_accessed=heads * HEAD_DIM * (16 * tokens + 8 * nkeys),
            transcendentals=heads * tokens * (tokens + nkeys),
        ),
        name="attention",
    )(q, k, v, g, local_bias, far_bias, *cols, *earlier)


def core_sum_body(own_ref, came_ref, *out_refs):
    for c, ref in enumerate(out_refs):
        total = own_ref[c].astype(jnp.float32) + came_ref[c].astype(jnp.float32)
        ref[...] = total.astype(ref.dtype)


def core_sum(own, came):
    n_cols = own.shape[0]
    shapes = [
        jax.ShapeDtypeStruct(own.shape[1:], jnp.float32 if c == 0 else jnp.bfloat16)
        for c in range(n_cols)
    ]
    return pl.pallas_call(
        core_sum_body,
        out_shape=shapes,
        compiler_params=pltpu.CompilerParams(vmem_limit_bytes=vmem_bytes),
        name="core_sum",
    )(own, came)


def column_sum_body(n_in, *refs):
    in_refs, out_refs = refs[:n_in], refs[n_in:]
    for j, ref in enumerate(out_refs):
        total = in_refs[0][j].astype(jnp.float32)
        for came in in_refs[1:]:
            total = total + came[j].astype(jnp.float32)
        ref[...] = total.astype(ref.dtype)


def column_sum(parts):
    nz = parts[0].shape[0]
    shapes = [
        jax.ShapeDtypeStruct(parts[0].shape[1:], jnp.float32 if j == 0 else jnp.bfloat16)
        for j in range(nz)
    ]
    return pl.pallas_call(
        functools.partial(column_sum_body, len(parts)),
        out_shape=shapes,
        compiler_params=pltpu.CompilerParams(vmem_limit_bytes=vmem_bytes),
        name="column_sum",
    )(*parts)


def finish_body(n_chunks, n_terms, n_blocks, *refs):
    dk_in, dv_in = refs[0], refs[1]
    terms = refs[2 : 2 + n_chunks * n_terms]
    dk_ref, dv_ref = refs[2 + n_chunks * n_terms :]
    totals = []
    for c in range(n_chunks):
        mine = terms[c * n_terms : (c + 1) * n_terms]
        total = mine[0][...]
        for term in mine[1:]:
            total = total + term[...].astype(jnp.float32)
        totals.append(total)
    total = jnp.concatenate(totals, axis=1)
    n_sum = total.shape[0] // 2
    block = pl.program_id(0)
    for half, (source, target) in enumerate(((dk_in, dk_ref), (dv_in, dv_ref))):
        fresh = total[half * n_sum : (half + 1) * n_sum]
        picked = fresh[:SUMMARY]
        for b in range(1, n_blocks):
            picked = jnp.where(block == b, fresh[b * SUMMARY : (b + 1) * SUMMARY], picked)
        kept = source[...].astype(jnp.float32)[: 16 - SUMMARY]
        target[...] = jnp.concatenate([kept, picked], axis=0).astype(jnp.bfloat16)


def finish(dk, dv, chunks):
    tokens, width = dk.shape
    n_blocks = tokens // BLOCK
    n_terms = len(chunks[0])
    edge = pl.BlockSpec((16, width), lambda b: (b * (BLOCK // 16) + BLOCK // 16 - 1, 0))
    terms = [term for chunk in chunks for term in chunk]
    return pl.pallas_call(
        functools.partial(finish_body, len(chunks), n_terms, n_blocks),
        grid=(n_blocks,),
        in_specs=[edge, edge] + [pl.BlockSpec(term.shape, lambda b: (0, 0)) for term in terms],
        out_specs=[edge, edge],
        out_shape=[jax.ShapeDtypeStruct(dk.shape, dk.dtype)] * 2,
        input_output_aliases={0: 0, 1: 1},
        compiler_params=pltpu.CompilerParams(vmem_limit_bytes=vmem_bytes),
        name="finish",
    )(dk, dv, *terms)


def on_device(n_seq, nz, queries, keys_in, values_in, cotangent):
    tokens = queries.shape[0]
    n_blocks = tokens // BLOCK
    n_sum = n_blocks * SUMMARY
    n_cols = n_seq // 2

    def flips(size, bits, keep):
        return [(i, i ^ bits) for i in range(size) if keep(i, i ^ bits)]

    def over_z(array, bits):
        return lax.ppermute(array, "head", flips(nz, bits, lambda a, b: True))

    def over_columns(array, bits, keep):
        return lax.ppermute(array, "seq", flips(n_seq, 2 * bits, keep))

    def over_core(array):
        return lax.ppermute(array, "seq", flips(n_seq, 1, lambda a, b: True))

    seq_pos = lax.axis_index("seq")
    z_pos = lax.axis_index("head")
    here = seq_pos * nz + z_pos
    sources = []
    for core in range(2):
        for c in range(n_cols):
            for j in range(nz):
                sources.append((seq_pos ^ (2 * c + core)) * nz + (z_pos ^ j))
    seen = jnp.stack(sources) < here
    far_bias = jnp.where(jnp.repeat(seen, n_sum), 0.0, neg_fill).astype(jnp.float32)
    far_bias = jnp.broadcast_to(far_bias[:, None], (far_bias.shape[0], 128))
    key_row = lax.broadcasted_iota(jnp.int32, (tokens, tokens), 0)
    query_row = lax.broadcasted_iota(jnp.int32, (tokens, tokens), 1)
    same = (key_row // BLOCK == query_row // BLOCK) & (key_row <= query_row)
    earlier_block = (key_row // BLOCK < query_row // BLOCK) & (key_row % BLOCK >= BLOCK - SUMMARY)
    local_bias = jnp.where(same | earlier_block, 0.0, neg_fill).astype(jnp.float32)

    firsts = [sum(chunk_heads[:c]) for c in range(len(chunk_heads))]
    gathered = []
    for first, heads in zip(firsts, chunk_heads):
        width = heads * HEAD_DIM
        start = first * HEAD_DIM
        mine = jnp.concatenate(
            [summary_rows(keys_in, start, width), summary_rows(values_in, start, width)], axis=0
        )
        line = jnp.stack([mine] + [over_z(mine, j) for j in range(1, nz)])
        cols = [line] + [over_columns(line, c, lambda a, b: a < b) for c in range(1, n_cols)]
        cols = cols + [over_core(col) for col in cols]
        gathered.append(cols)

    results = ()
    chunks = []
    for cols, first, heads in zip(gathered, firsts, chunk_heads):
        *results, near, own, other = attention(
            queries, keys_in, values_in, cotangent, local_bias, far_bias, cols, results, first, heads
        )
        sums = core_sum(own, over_core(other))
        sums = [sums[0]] + [
            over_columns(sums[c], c, lambda a, b: a > b) for c in range(1, n_cols)
        ]
        sums = column_sum(sums)
        sums = [sums[0]] + [over_z(sums[j], j) for j in range(1, nz)]
        chunks.append([near] + sums)
    attended, grad_queries, dk, dv = results
    grad_keys, grad_values = finish(dk, dv, chunks)
    return (attended, grad_queries, grad_keys, grad_values)


def solution(mesh):
    spec = P(("seq", "head"), None)
    return jax.shard_map(
        functools.partial(on_device, mesh.shape["seq"], mesh.shape["head"]),
        mesh=mesh,
        in_specs=(spec,) * 4,
        out_specs=(spec,) * 4,
        check_vma=False,
    )
```

time: 402 us -> 115 us (0.29); the launches traced: 395 us -> 114 us
  waiting for transfers between devices: 159 us -> 32.5 us
  local copies, waits for them, and re-layouts: 86.3 us -> 5.36 us
  matrix products: 46.7 us -> 0 us
  Pallas kernels: 0 us -> 28.7 us
  blocking collectives: 20.9 us -> 0 us
  other arithmetic: 15.7 us -> 0.38 us
  between operations: 15.1 us -> 0.96 us
  starting transfers between devices: 51.3 us -> 46.5 us
    all_to_all x12 -> x0, waiting for transfers between devices: 107 us -> none  [the longest x1 26.3 us: on_device(): lax.all_to_all(out_heads, 'head', split_axis=0, concat_axis=1, tiled=True)]
    reduce_scatter x2 -> x0, waiting for transfers between devices: 52.7 us -> none  [the longest x1 28.5 us: on_device(): lax.psum_scatter(buffers[0].reshape(nkeys, -1), 'seq', scatter_dimension=...]
    all_to_all x12 -> x0, starting transfers between devices: 51.2 us -> none  [the longest x1 6.31 us: on_device(): lax.all_to_all(high_tok, 'head', split_axis=1, concat_axis=0, tiled=True)]
    dot_general x18 -> x0, matrix products: 46.7 us -> none  [the longest x2 9.11 us: grads_turn(): jnp.einsum('hij,ihe->jhe', probs.astype(jnp.bfloat16), grad_rows, preferr...]
    ppermute x0 -> x34, starting transfers between devices: none -> 46.5 us  [the longest x12 23 us: over_z(): return lax.ppermute(array, 'head', flips(nz, bits, lambda a, b: True))]
    ppermute x0 -> x34, waiting for transfers between devices: none -> 32.5 us  [the longest x12 25.6 us: over_columns(): return lax.ppermute(array, 'seq', flips(n_seq, 2 * bits, keep))]
    pallas_call x0 -> x7, Pallas kernels: none -> 28.7 us  [the longest x2 26.4 us: attention(): pl.pallas_call(functools.partial(attention_body, rows // 2, n_cols, len(e...]
    all_gather x2 -> x0, blocking collectives: 20.9 us -> none  [the longest x1 11.1 us: on_device(): lax.all_gather(value_rows, 'seq', axis=0, tiled=True)]
  transfers between devices with their start and end apart: 14 -> 34, of which waited for: 11 -> 9; matrix products, arithmetic and copies ran while one was open for 30% -> 1% of each run, Pallas kernels for 0% -> 12%
where the time goes in v1:
time: 115 us; the launch traced here: 114 us
  starting transfers between devices  46.5 us (40%)
  waiting for transfers between devices  32.5 us (28%)
  Pallas kernels  28.7 us (25%)
  local copies, waits for them, and re-layouts  5.36 us (5%)
    pallas_call x2, Pallas kernels, attention(): pl.pallas_call(functools.partial(attention_body, rows // 2, n_cols, len(e...  26.4 us
    ppermute x12, waiting for transfers between devices, over_columns(): return lax.ppermute(array, 'seq', flips(n_seq, 2 * bits, keep))  25.6 us
    ppermute x12, starting transfers between devices, over_z(): return lax.ppermute(array, 'head', flips(nz, bits, lambda a, b: True))  23 us
    ppermute x12, starting transfers between devices, over_columns(): return lax.ppermute(array, 'seq', flips(n_seq, 2 * bits, keep))  20.8 us
    ppermute x12, waiting for transfers between devices, over_z(): return lax.ppermute(array, 'head', flips(nz, bits, lambda a, b: True))  4.75 us
    unnamed x14, local copies, waits for them, and re-layouts  4.12 us
    ppermute x10, starting transfers between devices, over_core(): return lax.ppermute(array, 'seq', flips(n_seq, 1, lambda a, b: True))  2.71 us
  transfers between devices with their start and end apart: 34, of which 9 were waited for; matrix products, arithmetic and copies ran while one was open for 1% of the time, Pallas kernels for 12%

profile of v1, /device:TPU:0, one launch (start us, length us, event | category | flops | bytes accessed | tf_op | source)
XLA Modules:
  0.0 114.5 jit_solution(7910999891805392071)
XLA Ops:
  1.5 4.1 %collective-permute-start.1 = (bf16[32,1024]{1,0:T(8,128)(2,1)S(1)}, bf16[32,1024]{1,0:T(8,128)(2,1)S(1)}, u32[]{:S(2)}, u32[]{:S(2)}) collective-permute-start(bf16[32,1024]{1,0:T(8,128)(2,1)S(1)} %get-tuple-element.79), channel_id=1, source_target_pairs={{0,2},{1,3},{2,0},{3,1},{4,6},{5,7},{6,4},{7,5},{8,10},{9,11},{10,... | collective-permute-start | bytes 196616 | tf_op jit(solution)/shard_map/ppermute | solution.py:225
  5.6 1.6 %collective-permute-start = (bf16[32,1024]{1,0:T(8,128)(2,1)S(1)}, bf16[32,1024]{1,0:T(8,128)(2,1)S(1)}, u32[]{:S(2)}, u32[]{:S(2)}) collective-permute-start(bf16[32,1024]{1,0:T(8,128)(2,1)S(1)} %get-tuple-element.79), channel_id=1, source_target_pairs={{0,1},{1,0},{2,3},{3,2},{4,5},{5,4},{6,7},{7,6},{8,9},{9,8},{10,11... | collective-permute-start | bytes 196616 | tf_op jit(solution)/shard_map/ppermute | solution.py:225
  7.2 2.0 %collective-permute-start.11 = (bf16[32,1024]{1,0:T(8,128)(2,1)S(1)}, bf16[32,1024]{1,0:T(8,128)(2,1)S(1)}, u32[]{:S(2)}, u32[]{:S(2)}) collective-permute-start(bf16[32,1024]{1,0:T(8,128)(2,1)S(1)} %get-tuple-element.77), channel_id=1, source_target_pairs={{0,2},{1,3},{2,0},{3,1},{4,6},{5,7},{6,4},{7,5},{8,10},{9,11},{10,... | collective-permute-start | bytes 196616 | tf_op jit(solution)/shard_map/ppermute | solution.py:225
  9.2 2.5 %collective-permute-start.10 = (bf16[32,1024]{1,0:T(8,128)(2,1)S(1)}, bf16[32,1024]{1,0:T(8,128)(2,1)S(1)}, u32[]{:S(2)}, u32[]{:S(2)}) collective-permute-start(bf16[32,1024]{1,0:T(8,128)(2,1)S(1)} %get-tuple-element.77), channel_id=1, source_target_pairs={{0,1},{1,0},{2,3},{3,2},{4,5},{5,4},{6,7},{7,6},{8,9},{9,8},{10,11... | collective-permute-start | bytes 196616 | tf_op jit(solution)/shard_map/ppermute | solution.py:225
  11.7 3.3 %collective-permute-start.12 = (bf16[32,1024]{1,0:T(8,128)(2,1)S(1)}, bf16[32,1024]{1,0:T(8,128)(2,1)S(1)}, u32[]{:S(2)}, u32[]{:S(2)}) collective-permute-start(bf16[32,1024]{1,0:T(8,128)(2,1)S(1)} %get-tuple-element.77), channel_id=1, source_target_pairs={{0,3},{1,2},{2,1},{3,0},{4,7},{5,6},{6,5},{7,4},{8,11},{9,10},{10,... | collective-permute-start | bytes 196616 | tf_op jit(solution)/shard_map/ppermute | solution.py:225
  15.0 4.4 %collective-permute-start.5 = (bf16[4,32,1024]{2,1,0:T(8,128)(2,1)S(1)}, bf16[4,32,1024]{2,1,0:T(8,128)(2,1)S(1)}, u32[]{:S(2)}, u32[]{:S(2)}) collective-permute-start(bf16[4,32,1024]{2,1,0:T(8,128)(2,1)S(1)} %pad_maximum_fusion.refs_6_), channel_id=1, source_target_pairs={{0,24},{4,28},{8,16},{12,20},{1,25},{5,29},{9,17},{13,21},{2,26},{... | collective-permute-start | bytes 786440 | tf_op jit(solution)/shard_map/ppermute | solution.py:228
  20.8 1.4 %collective-permute-start.15 = (bf16[4,32,1024]{2,1,0:T(8,128)(2,1)S(1)}, bf16[4,32,1024]{2,1,0:T(8,128)(2,1)S(1)}, u32[]{:S(2)}, u32[]{:S(2)}) collective-permute-start(bf16[4,32,1024]{2,1,0:T(8,128)(2,1)S(1)} %pad_maximum_fusion.1.refs_6_), channel_id=1, source_target_pairs={{0,24},{4,28},{8,16},{12,20},{1,25},{5,29},{9,17},{13,21},{2,26},{... | collective-permute-start | bytes 786440 | tf_op jit(solution)/shard_map/ppermute | solution.py:228
  22.3 1.3 %collective-permute-start.14 = (bf16[4,32,1024]{2,1,0:T(8,128)(2,1)S(1)}, bf16[4,32,1024]{2,1,0:T(8,128)(2,1)S(1)}, u32[]{:S(2)}, u32[]{:S(2)}) collective-permute-start(bf16[4,32,1024]{2,1,0:T(8,128)(2,1)S(1)} %pad_maximum_fusion.1.refs_6_), channel_id=1, source_target_pairs={{0,16},{4,20},{8,24},{12,28},{1,17},{5,21},{9,25},{13,29},{2,18},{... | collective-permute-start | bytes 786440 | tf_op jit(solution)/shard_map/ppermute | solution.py:228
  23.6 3.2 %collective-permute-start.13 = (bf16[4,32,1024]{2,1,0:T(8,128)(2,1)S(1)}, bf16[4,32,1024]{2,1,0:T(8,128)(2,1)}, u32[]{:S(2)}, u32[]{:S(2)}) collective-permute-start(bf16[4,32,1024]{2,1,0:T(8,128)(2,1)S(1)} %pad_maximum_fusion.1.refs_6_), channel_id=1, source_target_pairs={{0,8},{4,12},{16,24},{20,28},{1,9},{5,13},{17,25},{21,29},{2,10},{... | collective-permute-start | bytes 786440 | tf_op jit(solution)/shard_map/ppermute | solution.py:228
  26.8 1.5 %collective-permute-start.3 = (bf16[4,32,1024]{2,1,0:T(8,128)(2,1)S(1)}, bf16[4,32,1024]{2,1,0:T(8,128)(2,1)S(1)}, u32[]{:S(2)}, u32[]{:S(2)}) collective-permute-start(bf16[4,32,1024]{2,1,0:T(8,128)(2,1)S(1)} %pad_maximum_fusion.refs_6_), channel_id=1, source_target_pairs={{0,8},{4,12},{16,24},{20,28},{1,9},{5,13},{17,25},{21,29},{2,10},{... | collective-permute-start | bytes 786440 | tf_op jit(solution)/shard_map/ppermute | solution.py:228
  28.3 6.1 %collective-permute-done.4.refs_8_ = bf16[4,32,1024]{2,1,0:T(8,128)(2,1)S(1)} collective-permute-done((bf16[4,32,1024]{2,1,0:T(8,128)(2,1)S(1)}, bf16[4,32,1024]{2,1,0:T(8,128)(2,1)S(1)}, u32[]{:S(2)}, u32[]{:S(2)}) %collective-permute-start.4) | collective-permute-done | bytes 262176 | tf_op jit(solution)/shard_map/ppermute | solution.py:228
  35.5 3.4 %collective-permute-done.14.refs_8_ = bf16[4,32,1024]{2,1,0:T(8,128)(2,1)S(1)} collective-permute-done((bf16[4,32,1024]{2,1,0:T(8,128)(2,1)S(1)}, bf16[4,32,1024]{2,1,0:T(8,128)(2,1)S(1)}, u32[]{:S(2)}, u32[]{:S(2)}) %collective-permute-start.14) | collective-permute-done | bytes 262176 | tf_op jit(solution)/shard_map/ppermute | solution.py:228
  44.8 13.0 %attention.2 = (bf16[256,2048]{1,0:T(8,128)(2,1)}, bf16[256,2048]{1,0:T(8,128)(2,1)}, bf16[256,2048]{1,0:T(8,128)(2,1)}, bf16[256,2048]{1,0:T(8,128)(2,1)}, f32[...) custom-call(bf16[256,2048]{1,0:T(8,128)(2,1)S(1)} %copy-done, ...), custom_call_target="tpu_custom_call" | custom-call | flops 2415919104 | bytes 8388608 | tf_op jit(solution)/shard_map/attention/pallas_call | solution.py:106
  57.9 13.3 %attention.3 = (bf16[256,2048]{1,0:T(8,128)(2,1)}, bf16[256,2048]{1,0:T(8,128)(2,1)}, bf16[256,2048]{1,0:T(8,128)(2,1)}, bf16[256,2048]{1,0:T(8,128)(2,1)}, f32[...) custom-call(bf16[256,2048]{1,0:T(8,128)(2,1)S(1)} %copy-done, ...), custom_call_target="tpu_custom_call", output_to_operand_aliasing={{0}: (14, {}), {1}: (15, {}), {2}: (16, {}), {3}: (17, {})} | custom-call | flops 2415919104 | bytes 8388608 | tf_op jit(solution)/shard_map/attention/pallas_call | solution.py:106
  71.8 2.1 %collective-permute-done.27.came_ref = bf16[4,4,32,1024]{3,2,1,0:T(8,128)(2,1)S(1)} collective-permute-done((bf16[4,4,32,1024]{3,2,1,0:T(8,128)(2,1)S(1)}, bf16[4,4,32,1024]{3,2,1,0:T(8,128)(2,1)S(1)}, u32[]{:S(2)}, u32[]{:S(2)}) %collective-permute-start.27) | collective-permute-done | bytes 1048608 | tf_op jit(solution)/shard_map/ppermute | solution.py:231
  80.9 4.3 %collective-permute-done.28.refs_1_ = bf16[4,32,1024]{2,1,0:T(8,128)(2,1)S(1)} collective-permute-done((bf16[4,32,1024]{2,1,0:T(8,128)(2,1)S(1)}, bf16[4,32,1024]{2,1,0:T(8,128)(2,1)S(1)}, u32[]{:S(2)}, u32[]{:S(2)}) %collective-permute-start.28) | collective-permute-done | bytes 262176 | tf_op jit(solution)/shard_map/ppermute | solution.py:228
  86.5 6.3 %collective-permute-done.30.refs_3_ = bf16[4,32,1024]{2,1,0:T(8,128)(2,1)S(1)} collective-permute-done((bf16[4,32,1024]{2,1,0:T(8,128)(2,1)S(1)}, bf16[4,32,1024]{2,1,0:T(8,128)(2,1)S(1)}, u32[]{:S(2)}, u32[]{:S(2)}) %collective-permute-start.30) | collective-permute-done | bytes 262176 | tf_op jit(solution)/shard_map/ppermute | solution.py:228
  93.7 2.5 %collective-permute-start.32 = (bf16[32,1024]{1,0:T(8,128)(2,1)S(1)}, bf16[32,1024]{1,0:T(8,128)(2,1)S(1)}, u32[]{:S(2)}, u32[]{:S(2)}) collective-permute-start(bf16[32,1024]{1,0:T(8,128)(2,1)S(1)} %get-tuple-element.64), channel_id=1, source_target_pairs={{0,2},{1,3},{2,0},{3,1},{4,6},{5,7},{6,4},{7,5},{8,10},{9,11},{10,... | collective-permute-start | bytes 196616 | tf_op jit(solution)/shard_map/ppermute | solution.py:225
  96.2 1.4 %collective-permute-start.33 = (bf16[32,1024]{1,0:T(8,128)(2,1)S(1)}, bf16[32,1024]{1,0:T(8,128)(2,1)S(1)}, u32[]{:S(2)}, u32[]{:S(2)}) collective-permute-start(bf16[32,1024]{1,0:T(8,128)(2,1)S(1)} %get-tuple-element.65), channel_id=1, source_target_pairs={{0,3},{1,2},{2,1},{3,0},{4,7},{5,6},{6,5},{7,4},{8,11},{9,10},{10,... | collective-permute-start | bytes 196616 | tf_op jit(solution)/shard_map/ppermute | solution.py:225
  97.6 5.6 %collective-permute-done.23.refs_3_ = bf16[4,32,1024]{2,1,0:T(8,128)(2,1)S(1)} collective-permute-done((bf16[4,32,1024]{2,1,0:T(8,128)(2,1)S(1)}, bf16[4,32,1024]{2,1,0:T(8,128)(2,1)S(1)}, u32[]{:S(2)}, u32[]{:S(2)}) %collective-permute-start.23) | collective-permute-done | bytes 262176 | tf_op jit(solution)/shard_map/ppermute | solution.py:228
  104.2 2.5 %collective-permute-start.25 = (bf16[32,1024]{1,0:T(8,128)(2,1)S(1)}, bf16[32,1024]{1,0:T(8,128)(2,1)S(1)}, u32[]{:S(2)}, u32[]{:S(2)}) collective-permute-start(bf16[32,1024]{1,0:T(8,128)(2,1)S(1)} %get-tuple-element.53), channel_id=1, source_target_pairs={{0,2},{1,3},{2,0},{3,1},{4,6},{5,7},{6,4},{7,5},{8,10},{9,11},{10,... | collective-permute-start | bytes 196616 | tf_op jit(solution)/shard_map/ppermute | solution.py:225
  106.7 1.4 %collective-permute-start.26 = (bf16[32,1024]{1,0:T(8,128)(2,1)S(1)}, bf16[32,1024]{1,0:T(8,128)(2,1)S(1)}, u32[]{:S(2)}, u32[]{:S(2)}) collective-permute-start(bf16[32,1024]{1,0:T(8,128)(2,1)S(1)} %get-tuple-element.54), channel_id=1, source_target_pairs={{0,3},{1,2},{2,1},{3,0},{4,7},{5,6},{6,5},{7,4},{8,11},{9,10},{10,... | collective-permute-start | bytes 196616 | tf_op jit(solution)/shard_map/ppermute | solution.py:225
  108.2 3.8 %collective-permute-done.25.refs_5_ = bf16[32,1024]{1,0:T(8,128)(2,1)S(1)} collective-permute-done((bf16[32,1024]{1,0:T(8,128)(2,1)S(1)}, bf16[32,1024]{1,0:T(8,128)(2,1)S(1)}, u32[]{:S(2)}, u32[]{:S(2)}) %collective-permute-start.25) | collective-permute-done | bytes 65568 | tf_op jit(solution)/shard_map/ppermute | solution.py:225
  112.8 1.7 %finish.1 = (bf16[256,2048]{1,0:T(8,128)(2,1)}, bf16[256,2048]{1,0:T(8,128)(2,1)}) custom-call(bf16[256,2048]{1,0:T(8,128)(2,1)} %get-tuple-element.42.refs_0_, bf16[256,2048]{1,0:T(8,128)(2,1)} %get-tuple-element.43.refs_1_, f32[32,1024]{1,0:T(8,128)S(1)} %get-tuple-element.44.refs_2_, ...), custom_call_target="tpu_custom_call", output_to_operand_aliasing={{0}: (0, {}), {1}: (1, {})} | custom-call | tf_op jit(solution)/shard_map/finish/pallas_call | solution.py:203
  (79 shorter events, 20.9 us)
Async XLA Ops:
  1.5 10.1 %collective-permute-start.1 = (bf16[32,1024]{1,0:T(8,128)(2,1)S(1)}, bf16[32,1024]{1,0:T(8,128)(2,1)S(1)}, u32[]{:S(2)}, u32[]{:S(2)}) collective-permute-start(bf16[32,1024]{1,0:T(8,128)(2,1)S(1)} %get-tuple-element.79), channel_id=1, source_target_pairs={{0,2},{1,3},{2,0},{3,1},{4,6},{5,7},{6,4},{7,5},{8,10},{9,11},{10,... | collective-permute-start | bytes 196616 | tf_op jit(solution)/shard_map/ppermute | solution.py:225
  5.6 9.4 %collective-permute-start = (bf16[32,1024]{1,0:T(8,128)(2,1)S(1)}, bf16[32,1024]{1,0:T(8,128)(2,1)S(1)}, u32[]{:S(2)}, u32[]{:S(2)}) collective-permute-start(bf16[32,1024]{1,0:T(8,128)(2,1)S(1)} %get-tuple-element.79), channel_id=1, source_target_pairs={{0,1},{1,0},{2,3},{3,2},{4,5},{5,4},{6,7},{7,6},{8,9},{9,8},{10,11... | collective-permute-start | bytes 196616 | tf_op jit(solution)/shard_map/ppermute | solution.py:225
  7.2 13.5 %collective-permute-start.11 = (bf16[32,1024]{1,0:T(8,128)(2,1)S(1)}, bf16[32,1024]{1,0:T(8,128)(2,1)S(1)}, u32[]{:S(2)}, u32[]{:S(2)}) collective-permute-start(bf16[32,1024]{1,0:T(8,128)(2,1)S(1)} %get-tuple-element.77), channel_id=1, source_target_pairs={{0,2},{1,3},{2,0},{3,1},{4,6},{5,7},{6,4},{7,5},{8,10},{9,11},{10,... | collective-permute-start | bytes 196616 | tf_op jit(solution)/shard_map/ppermute | solution.py:225
  9.2 11.6 %collective-permute-start.10 = (bf16[32,1024]{1,0:T(8,128)(2,1)S(1)}, bf16[32,1024]{1,0:T(8,128)(2,1)S(1)}, u32[]{:S(2)}, u32[]{:S(2)}) collective-permute-start(bf16[32,1024]{1,0:T(8,128)(2,1)S(1)} %get-tuple-element.77), channel_id=1, source_target_pairs={{0,1},{1,0},{2,3},{3,2},{4,5},{5,4},{6,7},{7,6},{8,9},{9,8},{10,11... | collective-permute-start | bytes 196616 | tf_op jit(solution)/shard_map/ppermute | solution.py:225
  11.7 9.1 %collective-permute-start.12 = (bf16[32,1024]{1,0:T(8,128)(2,1)S(1)}, bf16[32,1024]{1,0:T(8,128)(2,1)S(1)}, u32[]{:S(2)}, u32[]{:S(2)}) collective-permute-start(bf16[32,1024]{1,0:T(8,128)(2,1)S(1)} %get-tuple-element.77), channel_id=1, source_target_pairs={{0,3},{1,2},{2,1},{3,0},{4,7},{5,6},{6,5},{7,4},{8,11},{9,10},{10,... | collective-permute-start | bytes 196616 | tf_op jit(solution)/shard_map/ppermute | solution.py:225
  15.0 11.7 %collective-permute-start.5 = (bf16[4,32,1024]{2,1,0:T(8,128)(2,1)S(1)}, bf16[4,32,1024]{2,1,0:T(8,128)(2,1)S(1)}, u32[]{:S(2)}, u32[]{:S(2)}) collective-permute-start(bf16[4,32,1024]{2,1,0:T(8,128)(2,1)S(1)} %pad_maximum_fusion.refs_6_), channel_id=1, source_target_pairs={{0,24},{4,28},{8,16},{12,20},{1,25},{5,29},{9,17},{13,21},{2,26},{... | collective-permute-start | bytes 786440 | tf_op jit(solution)/shard_map/ppermute | solution.py:228
  19.4 14.9 %collective-permute-start.4 = (bf16[4,32,1024]{2,1,0:T(8,128)(2,1)S(1)}, bf16[4,32,1024]{2,1,0:T(8,128)(2,1)S(1)}, u32[]{:S(2)}, u32[]{:S(2)}) collective-permute-start(bf16[4,32,1024]{2,1,0:T(8,128)(2,1)S(1)} %pad_maximum_fusion.refs_6_), channel_id=1, source_target_pairs={{0,16},{4,20},{8,24},{12,28},{1,17},{5,21},{9,25},{13,29},{2,18},{... | collective-permute-start | bytes 786440 | tf_op jit(solution)/shard_map/ppermute | solution.py:228
  20.8 13.5 %collective-permute-start.15 = (bf16[4,32,1024]{2,1,0:T(8,128)(2,1)S(1)}, bf16[4,32,1024]{2,1,0:T(8,128)(2,1)S(1)}, u32[]{:S(2)}, u32[]{:S(2)}) collective-permute-start(bf16[4,32,1024]{2,1,0:T(8,128)(2,1)S(1)} %pad_maximum_fusion.1.refs_6_), channel_id=1, source_target_pairs={{0,24},{4,28},{8,16},{12,20},{1,25},{5,29},{9,17},{13,21},{2,26},{... | collective-permute-start | bytes 786440 | tf_op jit(solution)/shard_map/ppermute | solution.py:228
  22.3 16.7 %collective-permute-start.14 = (bf16[4,32,1024]{2,1,0:T(8,128)(2,1)S(1)}, bf16[4,32,1024]{2,1,0:T(8,128)(2,1)S(1)}, u32[]{:S(2)}, u32[]{:S(2)}) collective-permute-start(bf16[4,32,1024]{2,1,0:T(8,128)(2,1)S(1)} %pad_maximum_fusion.1.refs_6_), channel_id=1, source_target_pairs={{0,16},{4,20},{8,24},{12,28},{1,17},{5,21},{9,25},{13,29},{2,18},{... | collective-permute-start | bytes 786440 | tf_op jit(solution)/shard_map/ppermute | solution.py:228
  23.6 16.1 %collective-permute-start.13 = (bf16[4,32,1024]{2,1,0:T(8,128)(2,1)S(1)}, bf16[4,32,1024]{2,1,0:T(8,128)(2,1)}, u32[]{:S(2)}, u32[]{:S(2)}) collective-permute-start(bf16[4,32,1024]{2,1,0:T(8,128)(2,1)S(1)} %pad_maximum_fusion.1.refs_6_), channel_id=1, source_target_pairs={{0,8},{4,12},{16,24},{20,28},{1,9},{5,13},{17,25},{21,29},{2,10},{... | collective-permute-start | bytes 786440 | tf_op jit(solution)/shard_map/ppermute | solution.py:228
  26.8 13.9 %collective-permute-start.3 = (bf16[4,32,1024]{2,1,0:T(8,128)(2,1)S(1)}, bf16[4,32,1024]{2,1,0:T(8,128)(2,1)S(1)}, u32[]{:S(2)}, u32[]{:S(2)}) collective-permute-start(bf16[4,32,1024]{2,1,0:T(8,128)(2,1)S(1)} %pad_maximum_fusion.refs_6_), channel_id=1, source_target_pairs={{0,8},{4,12},{16,24},{20,28},{1,9},{5,13},{17,25},{21,29},{2,10},{... | collective-permute-start | bytes 786440 | tf_op jit(solution)/shard_map/ppermute | solution.py:228
  40.7 17.2 %collective-permute-start.6 = (bf16[4,32,1024]{2,1,0:T(8,128)(2,1)S(1)}, bf16[4,32,1024]{2,1,0:T(8,128)(2,1)S(1)}, u32[]{:S(2)}, u32[]{:S(2)}) collective-permute-start(bf16[4,32,1024]{2,1,0:T(8,128)(2,1)S(1)} %pad_maximum_fusion.refs_6_), channel_id=1, source_target_pairs={{0,4},{4,0},{8,12},{12,8},{16,20},{20,16},{24,28},{28,24},{1,5},{5... | collective-permute-start | bytes 786440 | tf_op jit(solution)/shard_map/ppermute | solution.py:231
  40.8 17.1 %collective-permute-start.9 = (bf16[4,32,1024]{2,1,0:T(8,128)(2,1)S(1)}, bf16[4,32,1024]{2,1,0:T(8,128)(2,1)S(1)}, u32[]{:S(2)}, u32[]{:S(2)}) collective-permute-start(bf16[4,32,1024]{2,1,0:T(8,128)(2,1)S(1)} %collective-permute-done.5.refs_9_), channel_id=1, source_target_pairs={{0,4},{4,0},{8,12},{12,8},{16,20},{20,16},{24,28},{28,24},{1,5},{5... | collective-permute-start | bytes 786440 | tf_op jit(solution)/shard_map/ppermute | solution.py:231
  41.3 16.6 %collective-permute-start.8 = (bf16[4,32,1024]{2,1,0:T(8,128)(2,1)S(1)}, bf16[4,32,1024]{2,1,0:T(8,128)(2,1)S(1)}, u32[]{:S(2)}, u32[]{:S(2)}) collective-permute-start(bf16[4,32,1024]{2,1,0:T(8,128)(2,1)S(1)} %collective-permute-done.4.refs_8_), channel_id=1, source_target_pairs={{0,4},{4,0},{8,12},{12,8},{16,20},{20,16},{24,28},{28,24},{1,5},{5... | collective-permute-start | bytes 786440 | tf_op jit(solution)/shard_map/ppermute | solution.py:231
  41.4 16.5 %collective-permute-start.7 = (bf16[4,32,1024]{2,1,0:T(8,128)(2,1)S(1)}, bf16[4,32,1024]{2,1,0:T(8,128)(2,1)S(1)}, u32[]{:S(2)}, u32[]{:S(2)}) collective-permute-start(bf16[4,32,1024]{2,1,0:T(8,128)(2,1)S(1)} %collective-permute-done.3.refs_7_), channel_id=1, source_target_pairs={{0,4},{4,0},{8,12},{12,8},{16,20},{20,16},{24,28},{28,24},{1,5},{5... | collective-permute-start | bytes 786440 | tf_op jit(solution)/shard_map/ppermute | solution.py:231
  74.1 11.0 %collective-permute-start.28 = (bf16[4,32,1024]{2,1,0:T(8,128)(2,1)S(1)}, bf16[4,32,1024]{2,1,0:T(8,128)(2,1)S(1)}, u32[]{:S(2)}, u32[]{:S(2)}) collective-permute-start(bf16[4,32,1024]{2,1,0:T(8,128)(2,1)S(1)} %get-tuple-element.59), channel_id=1, source_target_pairs={{8,0},{12,4},{24,16},{28,20},{9,1},{13,5},{25,17},{29,21},{10,2},{... | collective-permute-start | bytes 786440 | tf_op jit(solution)/shard_map/ppermute | solution.py:228
  75.4 11.0 %collective-permute-start.29 = (bf16[4,32,1024]{2,1,0:T(8,128)(2,1)S(1)}, bf16[4,32,1024]{2,1,0:T(8,128)(2,1)S(1)}, u32[]{:S(2)}, u32[]{:S(2)}) collective-permute-start(bf16[4,32,1024]{2,1,0:T(8,128)(2,1)S(1)} %get-tuple-element.60), channel_id=1, source_target_pairs={{16,0},{20,4},{24,8},{28,12},{17,1},{21,5},{25,9},{29,13},{18,2},{... | collective-permute-start | bytes 786440 | tf_op jit(solution)/shard_map/ppermute | solution.py:228
  76.7 16.0 %collective-permute-start.30 = (bf16[4,32,1024]{2,1,0:T(8,128)(2,1)S(1)}, bf16[4,32,1024]{2,1,0:T(8,128)(2,1)S(1)}, u32[]{:S(2)}, u32[]{:S(2)}) collective-permute-start(bf16[4,32,1024]{2,1,0:T(8,128)(2,1)S(1)} %get-tuple-element.61), channel_id=1, source_target_pairs={{16,8},{20,12},{24,0},{28,4},{17,9},{21,13},{25,1},{29,5},{18,10},... | collective-permute-start | bytes 786440 | tf_op jit(solution)/shard_map/ppermute | solution.py:228
  78.3 17.9 %collective-permute-start.21 = (bf16[4,32,1024]{2,1,0:T(8,128)(2,1)S(1)}, bf16[4,32,1024]{2,1,0:T(8,128)(2,1)S(1)}, u32[]{:S(2)}, u32[]{:S(2)}) collective-permute-start(bf16[4,32,1024]{2,1,0:T(8,128)(2,1)S(1)} %get-tuple-element.48), channel_id=1, source_target_pairs={{8,0},{12,4},{24,16},{28,20},{9,1},{13,5},{25,17},{29,21},{10,2},{... | collective-permute-start | bytes 786440 | tf_op jit(solution)/shard_map/ppermute | solution.py:228
  79.6 18.0 %collective-permute-start.22 = (bf16[4,32,1024]{2,1,0:T(8,128)(2,1)S(1)}, bf16[4,32,1024]{2,1,0:T(8,128)(2,1)S(1)}, u32[]{:S(2)}, u32[]{:S(2)}) collective-permute-start(bf16[4,32,1024]{2,1,0:T(8,128)(2,1)S(1)} %get-tuple-element.49), channel_id=1, source_target_pairs={{16,0},{20,4},{24,8},{28,12},{17,1},{21,5},{25,9},{29,13},{18,2},{... | collective-permute-start | bytes 786440 | tf_op jit(solution)/shard_map/ppermute | solution.py:228
  85.2 18.0 %collective-permute-start.23 = (bf16[4,32,1024]{2,1,0:T(8,128)(2,1)S(1)}, bf16[4,32,1024]{2,1,0:T(8,128)(2,1)S(1)}, u32[]{:S(2)}, u32[]{:S(2)}) collective-permute-start(bf16[4,32,1024]{2,1,0:T(8,128)(2,1)S(1)} %get-tuple-element.50), channel_id=1, source_target_pairs={{16,8},{20,12},{24,0},{28,4},{17,9},{21,13},{25,1},{29,5},{18,10},... | collective-permute-start | bytes 786440 | tf_op jit(solution)/shard_map/ppermute | solution.py:228
  92.9 13.8 %collective-permute-start.31 = (bf16[32,1024]{1,0:T(8,128)(2,1)S(1)}, bf16[32,1024]{1,0:T(8,128)(2,1)S(1)}, u32[]{:S(2)}, u32[]{:S(2)}) collective-permute-start(bf16[32,1024]{1,0:T(8,128)(2,1)S(1)} %get-tuple-element.63), channel_id=1, source_target_pairs={{0,1},{1,0},{2,3},{3,2},{4,5},{5,4},{6,7},{7,6},{8,9},{9,8},{10,11... | collective-permute-start | bytes 196616 | tf_op jit(solution)/shard_map/ppermute | solution.py:225
  93.7 14.3 %collective-permute-start.32 = (bf16[32,1024]{1,0:T(8,128)(2,1)S(1)}, bf16[32,1024]{1,0:T(8,128)(2,1)S(1)}, u32[]{:S(2)}, u32[]{:S(2)}) collective-permute-start(bf16[32,1024]{1,0:T(8,128)(2,1)S(1)} %get-tuple-element.64), channel_id=1, source_target_pairs={{0,2},{1,3},{2,0},{3,1},{4,6},{5,7},{6,4},{7,5},{8,10},{9,11},{10,... | collective-permute-start | bytes 196616 | tf_op jit(solution)/shard_map/ppermute | solution.py:225
  96.2 11.8 %collective-permute-start.33 = (bf16[32,1024]{1,0:T(8,128)(2,1)S(1)}, bf16[32,1024]{1,0:T(8,128)(2,1)S(1)}, u32[]{:S(2)}, u32[]{:S(2)}) collective-permute-start(bf16[32,1024]{1,0:T(8,128)(2,1)S(1)} %get-tuple-element.65), channel_id=1, source_target_pairs={{0,3},{1,2},{2,1},{3,0},{4,7},{5,6},{6,5},{7,4},{8,11},{9,10},{10,... | collective-permute-start | bytes 196616 | tf_op jit(solution)/shard_map/ppermute | solution.py:225
  (17 other events, 118.9 us)

commit v2 on v1

v2 whole, which is shorter than its diff:
```python
import functools
import math

import jax
import jax.numpy as jnp
from jax import lax
from jax.experimental import pallas as pl
from jax.experimental.pallas import tpu as pltpu
from jax.sharding import PartitionSpec as P

HEADS = 16
HEAD_DIM = 128
BLOCK = 128
SUMMARY = 8
EDGE = 16

neg_fill = -1e30
scaling = 1.0 / math.sqrt(HEAD_DIM)
exponent = scaling / math.log(2.0)
chunk_heads = (8, 8)
unroll = 4
vmem_bytes = 40 * 1024 * 1024
in_vmem = pl.BlockSpec(memory_space=pltpu.VMEM)
in_hbm = pl.BlockSpec(memory_space=pltpu.HBM)
in_smem = pl.BlockSpec(memory_space=pltpu.SMEM)
token_shape = jax.ShapeDtypeStruct((8, 128), jnp.float32)
params = pltpu.CompilerParams(vmem_limit_bytes=vmem_bytes)


def dot(left, right, left_dim, right_dim):
    return lax.dot_general(
        left, right, (((left_dim,), (right_dim,)), ((), ())), preferred_element_type=jnp.float32
    )


def summary_rows(matrix, start, width):
    rows = [
        lax.slice(matrix, (b * BLOCK + BLOCK - SUMMARY, start), ((b + 1) * BLOCK, start + width))
        for b in range(matrix.shape[0] // BLOCK)
    ]
    return jnp.concatenate(rows, axis=0)


def block_mask():
    key = lax.broadcasted_iota(jnp.int32, (BLOCK, BLOCK), 1)
    query = lax.broadcasted_iota(jnp.int32, (BLOCK, BLOCK), 0)
    return jnp.where(key <= query, 0.0, neg_fill)


def far_mask(seq_pos, z_pos, n_cols, nz, n_sum, tokens):
    shape = (tokens, 2 * n_cols * nz * n_sum)
    row = lax.broadcasted_iota(jnp.int32, shape, 1)
    query = lax.broadcasted_iota(jnp.int32, shape, 0)
    piece = row // n_sum
    core = piece // (n_cols * nz)
    column = (piece // nz) % n_cols
    source = (seq_pos ^ (2 * column + core)) * nz + (z_pos ^ (piece % nz))
    mine = (piece == 0) & (row // SUMMARY < query // BLOCK)
    return jnp.where((source < seq_pos * nz + z_pos) | mine, 0.0, neg_fill)


def attention_body(n_sum, n_cols, n_skip, first, heads, *refs):
    place_ref = refs[0]
    sources = refs[1:5]
    col_refs = refs[5 : 5 + n_cols]
    targets = refs[5 + n_cols + n_skip : 9 + n_cols + n_skip]
    near_ref, own_ref, other_ref, token_ref = refs[9 + n_cols + n_skip : 13 + n_cols + n_skip]
    near_mask, away_mask, loads, stores, load_sem, store_sem = refs[13 + n_cols + n_skip :]
    tokens = sources[0].shape[0]
    nz = col_refs[0].shape[0]
    steps = heads // unroll
    span = unroll * HEAD_DIM

    def window(step):
        return pl.ds(pl.multiple_of(first * HEAD_DIM + step * span, HEAD_DIM), span)

    def load(step, i):
        return pltpu.make_async_copy(
            sources[i].at[:, window(step)], loads.at[step, i], load_sem.at[step, i]
        )

    def store(step, i):
        return pltpu.make_async_copy(
            stores.at[step, i], targets[i].at[:, window(step)], store_sem.at[step, i]
        )

    for step in range(steps):
        for i in range(4):
            load(step, i).start()
    blocks = [slice(b * BLOCK, (b + 1) * BLOCK) for b in range(tokens // BLOCK)]
    token_ref[...] = jnp.zeros(token_ref.shape, token_ref.dtype)
    near_mask[...] = jnp.concatenate([block_mask()] * len(blocks), axis=0)
    away_mask[...] = far_mask(place_ref[0], place_ref[1], n_cols // 2, nz, n_sum, tokens)

    def beside(parts):
        return jnp.concatenate(parts, axis=1)

    def head(step, at, to):
        q, k_loc, v_loc, g = (loads[step, i, :, at] for i in range(4))
        k_far = jnp.concatenate([ref[j, :n_sum, to] for ref in col_refs for j in range(nz)], axis=0)
        v_far = jnp.concatenate([ref[j, n_sum:, to] for ref in col_refs for j in range(nz)], axis=0)
        s_loc = jnp.concatenate([dot(q[b], k_loc[b], 1, 1) for b in blocks], axis=0) + near_mask[...]
        s_far = dot(q, k_far, 1, 1) + away_mask[...]
        high = jnp.maximum(
            jnp.max(s_loc, axis=1, keepdims=True), jnp.max(s_far, axis=1, keepdims=True)
        )
        e_loc = jnp.exp2((s_loc - high) * exponent)
        e_far = jnp.exp2((s_far - high) * exponent)
        norm = jnp.sum(e_loc, axis=1, keepdims=True) + jnp.sum(e_far, axis=1, keepdims=True)
        inv = 1.0 / norm
        eb_loc = e_loc.astype(jnp.bfloat16)
        eb_far = e_far.astype(jnp.bfloat16)
        out = jnp.concatenate([dot(eb_loc[b], v_loc[b], 1, 0) for b in blocks], axis=0) + dot(
            eb_far, v_far, 1, 0
        )
        out = (out * inv).astype(jnp.bfloat16)
        stores[step, 0, :, at] = out
        gf = g.astype(jnp.float32)
        delta = jnp.sum(gf * out.astype(jnp.float32), axis=1, keepdims=True)
        factor = inv * scaling
        t_loc = (jnp.concatenate([dot(g[b], v_loc[b], 1, 1) for b in blocks], axis=0) - delta) * factor
        t_far = (dot(g, v_far, 1, 1) - delta) * factor
        ds_loc = (eb_loc.astype(jnp.float32) * t_loc).astype(jnp.bfloat16)
        ds_far = (eb_far.astype(jnp.float32) * t_far).astype(jnp.bfloat16)
        dq = jnp.concatenate([dot(ds_loc[b], k_loc[b], 1, 0) for b in blocks], axis=0) + dot(
            ds_far, k_far, 1, 0
        )
        stores[step, 1, :, at] = dq.astype(jnp.bfloat16)
        gi = (gf * inv).astype(jnp.bfloat16)
        row = 0
        for target, left, right in ((2, ds_loc, q), (3, eb_loc, gi)):
            for b in blocks:
                part = dot(left[b], right[b], 0, 0)
                stores[step, target, b, at] = part.astype(jnp.bfloat16)
                near_ref[row : row + EDGE, to] = part[BLOCK - EDGE :, :]
                row += EDGE
        dk_far = dot(q, ds_far, 0, 0).astype(jnp.bfloat16).T
        dv_far = dot(gi, eb_far, 0, 0).astype(jnp.bfloat16).T
        row = 0
        for half in (own_ref, other_ref):
            for c in range(n_cols // 2):
                for j in range(nz):
                    half[c, j, :n_sum, to] = dk_far[row : row + n_sum]
                    half[c, j, n_sum:, to] = dv_far[row : row + n_sum]
                    row += n_sum

    def turn(step, carried):
        for i in range(4):
            load(step, i).wait()
        for u in range(unroll):
            to = pl.ds(pl.multiple_of(step * span + u * HEAD_DIM, HEAD_DIM), HEAD_DIM)
            head(step, slice(u * HEAD_DIM, (u + 1) * HEAD_DIM), to)
        for i in range(4):
            store(step, i).start()
        return carried

    lax.fori_loop(0, steps, turn, 0)
    for step in range(steps):
        for i in range(4):
            store(step, i).wait()


def attention(place, q, k, v, g, cols, earlier, after, first, heads):
    tokens, width = q.shape
    n_cols = len(cols)
    nz, rows, chunk_width = cols[0].shape
    nkeys = n_cols * nz * rows // 2
    n_blocks = tokens // BLOCK
    grads_shape = jax.ShapeDtypeStruct((n_cols // 2, nz, rows, chunk_width), jnp.bfloat16)
    full = jax.ShapeDtypeStruct((tokens, width), jnp.bfloat16)
    n_skip = len(earlier) + len(after)
    return pl.pallas_call(
        functools.partial(attention_body, rows // 2, n_cols, n_skip, first, heads),
        in_specs=[in_smem]
        + [in_hbm] * 4
        + [in_vmem] * n_cols
        + [in_hbm] * len(earlier)
        + [in_vmem] * len(after),
        out_specs=[in_hbm] * 4 + [in_vmem] * 4,
        out_shape=[full] * 4
        + [
            jax.ShapeDtypeStruct((2 * n_blocks * EDGE, chunk_width), jnp.float32),
            grads_shape,
            grads_shape,
            token_shape,
        ],
        scratch_shapes=[
            pltpu.VMEM((tokens, BLOCK), jnp.float32),
            pltpu.VMEM((tokens, nkeys), jnp.float32),
            pltpu.VMEM((heads // unroll, 4, tokens, unroll * HEAD_DIM), jnp.bfloat16),
            pltpu.VMEM((heads // unroll, 4, tokens, unroll * HEAD_DIM), jnp.bfloat16),
            pltpu.SemaphoreType.DMA((heads // unroll, 4)),
            pltpu.SemaphoreType.DMA((heads // unroll, 4)),
        ],
        input_output_aliases={5 + n_cols + i: i for i in range(len(earlier))},
        compiler_params=params,
        cost_estimate=pl.CostEstimate(
            flops=heads * 12 * tokens * (tokens + nkeys) * HEAD_DIM,
            bytes_accessed=heads * HEAD_DIM * (16 * tokens + 8 * nkeys),
            transcendentals=heads * tokens * (tokens + nkeys),
        ),
        name="attention",
    )(place, *[pltpu.with_memory_space_constraint(x, pltpu.HBM) for x in (q, k, v, g)], *cols, *earlier, *after)


def hold_body(*refs):
    pass


def hold(arrays, *after):
    return pl.pallas_call(
        hold_body,
        in_specs=[in_vmem] * (len(arrays) + len(after)),
        out_specs=[in_vmem] * len(arrays),
        out_shape=[jax.ShapeDtypeStruct(a.shape, a.dtype) for a in arrays],
        input_output_aliases={i: i for i in range(len(arrays))},
        compiler_params=params,
        name="hold",
    )(*arrays, *after)


def line_body(n_in, *refs):
    line_ref, token_ref = refs[-2:]
    for j in range(n_in):
        line_ref[j] = refs[j][...]
    token_ref[...] = jnp.zeros(token_ref.shape, token_ref.dtype)


def stack_line(pieces, *after):
    shape = (len(pieces),) + pieces[0].shape
    return pl.pallas_call(
        functools.partial(line_body, len(pieces)),
        in_specs=[in_vmem] * (len(pieces) + len(after)),
        out_specs=[in_vmem] * 2,
        out_shape=[jax.ShapeDtypeStruct(shape, pieces[0].dtype), token_shape],
        compiler_params=params,
        name="line",
    )(*pieces, *after)


def core_sum_body(own_ref, came_ref, *out_refs):
    token_ref = out_refs[-1]
    for c, ref in enumerate(out_refs[:-1]):
        total = own_ref[c].astype(jnp.float32) + came_ref[c].astype(jnp.float32)
        ref[...] = total.astype(ref.dtype)
    token_ref[...] = jnp.zeros(token_ref.shape, token_ref.dtype)


def core_sum(own, came):
    n_cols = own.shape[0]
    shapes = [
        jax.ShapeDtypeStruct(own.shape[1:], jnp.float32 if c == 0 else jnp.bfloat16)
        for c in range(n_cols)
    ]
    return pl.pallas_call(
        core_sum_body,
        in_specs=[in_vmem] * 2,
        out_specs=[in_vmem] * (n_cols + 1),
        out_shape=shapes + [token_shape],
        compiler_params=params,
        name="core_sum",
    )(own, came)


def column_sum_body(n_in, n_after, *refs):
    in_refs, out_refs = refs[:n_in], refs[n_in + n_after :]
    token_ref = out_refs[-1]
    for j, ref in enumerate(out_refs[:-1]):
        total = in_refs[0][j].astype(jnp.float32)
        for came in in_refs[1:]:
            total = total + came[j].astype(jnp.float32)
        ref[...] = total.astype(ref.dtype)
    token_ref[...] = jnp.zeros(token_ref.shape, token_ref.dtype)


def column_sum(parts, *after):
    nz = parts[0].shape[0]
    shapes = [
        jax.ShapeDtypeStruct(parts[0].shape[1:], jnp.float32 if j == 0 else jnp.bfloat16)
        for j in range(nz)
    ]
    return pl.pallas_call(
        functools.partial(column_sum_body, len(parts), len(after)),
        in_specs=[in_vmem] * (len(parts) + len(after)),
        out_specs=[in_vmem] * (nz + 1),
        out_shape=shapes + [token_shape],
        compiler_params=params,
        name="column_sum",
    )(*parts, *after)


def finish_body(n_chunks, n_terms, n_blocks, *refs):
    terms = refs[2 : 2 + n_chunks * n_terms]
    targets = refs[2 + n_chunks * n_terms : 4 + n_chunks * n_terms]
    edges, sem = refs[4 + n_chunks * n_terms :]
    at = 0
    for c in range(n_chunks):
        near, *mine = terms[c * n_terms : (c + 1) * n_terms]
        total = mine[0][...]
        for term in mine[1:]:
            total = total + term[...].astype(jnp.float32)
        to = pl.ds(at, near.shape[1])
        for row in range(2 * n_blocks):
            tile = near[row * EDGE : (row + 1) * EDGE, :]
            more = total[row * SUMMARY : (row + 1) * SUMMARY]
            edge = jnp.concatenate([tile[: EDGE - SUMMARY], tile[EDGE - SUMMARY :] + more], axis=0)
            edges[row, :, to] = edge.astype(jnp.bfloat16)
        at += near.shape[1]
    copies = [
        pltpu.make_async_copy(
            edges.at[row],
            targets[row // n_blocks].at[pl.ds((row % n_blocks + 1) * BLOCK - EDGE, EDGE), :],
            sem.at[row],
        )
        for row in range(2 * n_blocks)
    ]
    for copy in copies:
        copy.start()
    for copy in copies:
        copy.wait()


def finish(dk, dv, chunks):
    tokens, width = dk.shape
    n_blocks = tokens // BLOCK
    n_terms = len(chunks[0])
    terms = [term for chunk in chunks for term in chunk]
    anywhere = pl.BlockSpec(memory_space=pl.ANY)
    return pl.pallas_call(
        functools.partial(finish_body, len(chunks), n_terms, n_blocks),
        in_specs=[anywhere] * 2 + [in_vmem] * len(terms),
        out_specs=[anywhere] * 2,
        out_shape=[jax.ShapeDtypeStruct(dk.shape, dk.dtype)] * 2,
        scratch_shapes=[
            pltpu.VMEM((2 * n_blocks, EDGE, width), jnp.bfloat16),
            pltpu.SemaphoreType.DMA((2 * n_blocks,)),
        ],
        input_output_aliases={0: 0, 1: 1},
        compiler_params=params,
        name="finish",
    )(dk, dv, *terms)


def on_device(n_seq, nz, queries, keys_in, values_in, cotangent):
    n_cols = n_seq // 2

    def over_z(array, bits):
        return lax.ppermute(array, "head", [(i, i ^ bits) for i in range(nz)])

    def over_seq(array, bits):
        return lax.ppermute(array, "seq", [(i, i ^ bits) for i in range(n_seq)])

    def spread_z(piece):
        return [over_z(piece, j) for j in reversed(range(1, nz))][::-1]

    def spread_columns(line):
        return [over_seq(line, 2 * c) for c in reversed(range(1, n_cols))][::-1]

    place = jnp.stack([lax.axis_index("seq"), lax.axis_index("head")]).astype(jnp.int32)
    n_chunks = len(chunk_heads)
    firsts = [sum(chunk_heads[:c]) for c in range(n_chunks)]
    pieces = []
    for first, heads in zip(firsts, chunk_heads):
        width = heads * HEAD_DIM
        start = first * HEAD_DIM
        mine = jnp.concatenate(
            [summary_rows(keys_in, start, width), summary_rows(values_in, start, width)], axis=0
        )
        pieces.append([mine] + spread_z(mine))
    columns = []
    marks = []
    lines = []
    for c in range(n_chunks):
        line, mark = stack_line(pieces[c], *[cols[-1] for cols in columns[-1:]])
        shown = line
        if c + 1 < n_chunks:
            shown, _ = stack_line(pieces[c], *pieces[c + 1][1:])
        marks.append(mark)
        lines.append(shown)
        columns.append([line] + spread_columns(line))

    results = ()
    chunks = []
    cols = columns[0]
    sent, ends, after = None, [], []
    for c in range(n_chunks):
        cols = cols + [over_seq(col, 1) for col in [lines[c] if c == 0 else cols[0]] + cols[1:]]
        more = c + 1 < n_chunks
        *results, near, own, other, mark = attention(
            place, queries, keys_in, values_in, cotangent, cols, results,
            after + marks[c + 1 : c + 2], firsts[c], chunk_heads[c],
        )
        if more:
            cols = list(hold(columns[c + 1], mark))
            (other,) = hold([other], *cols)
        if sent is not None:
            *ends, mark = column_sum(sent[1])
            (other,) = hold([other], mark)
            ends = [ends[0]] + spread_z_back(ends, over_z)
            chunks.append([sent[0]] + ends)
        *sums, mark = core_sum(own, over_seq(other, 1))
        after = [mark]
        back = [over_seq(sums[i], 2 * i) for i in reversed(range(1, n_cols))][::-1]
        sent = near, [sums[0]] + back
    *ends, mark = column_sum(sent[1], *ends[1:])
    chunks.append([sent[0], ends[0]] + spread_z_back(ends, over_z))
    attended, grad_queries, dk, dv = results
    grad_keys, grad_values = finish(dk, dv, chunks)
    return (attended, grad_queries, grad_keys, grad_values)


def spread_z_back(ends, over_z):
    return [over_z(ends[j], j) for j in reversed(range(1, len(ends)))][::-1]


def solution(mesh):
    spec = P(("seq", "head"), None)
    return jax.shard_map(
        functools.partial(on_device, mesh.shape["seq"], mesh.shape["head"]),
        mesh=mesh,
        in_specs=(spec,) * 4,
        out_specs=(spec,) * 4,
        check_vma=False,
    )
```

time: 115 us -> 90.6 us (0.79)
  starting transfers between devices: 46.5 us -> 34.6 us
  local copies, waits for them, and re-layouts: 5.36 us -> 0.85 us
  Pallas kernels: 28.7 us -> 24.7 us
  waiting for transfers between devices: 32.5 us -> 29.4 us
    ppermute x34, starting transfers between devices: 46.5 us -> 34.6 us  [the longest x12 18.3 us: over_z(): return lax.ppermute(array, 'head', [(i, i ^ bits) for i in range(nz)])]
    unnamed x14 -> x0, local copies, waits for them, and re-layouts: 4.12 us -> none
    pallas_call x6 -> x12, Pallas kernels: 27.1 us -> 23.8 us  [the longest x2 20.9 us: attention(): pl.pallas_call(functools.partial(attention_body, rows // 2, n_cols, n_ski...]
    ppermute x34, waiting for transfers between devices: 32.5 us -> 29.4 us  [the longest x12 22.5 us: over_z(): return lax.ppermute(array, 'head', [(i, i ^ bits) for i in range(nz)])]
  transfers between devices with their start and end apart: 34 -> 34, of which waited for: 9 -> 13; matrix products, arithmetic and copies ran while one was open for 1% -> 0% of each run, Pallas kernels for 12% -> 24%
where the time goes in v2:
time: 90.6 us; the launch traced here: 90.3 us
  starting transfers between devices  34.6 us (38%)
  waiting for transfers between devices  29.4 us (32%)
  Pallas kernels  24.7 us (27%)
    ppermute x12, waiting for transfers between devices, over_z(): return lax.ppermute(array, 'head', [(i, i ^ bits) for i in range(nz)])  22.5 us
    pallas_call x2, Pallas kernels, attention(): pl.pallas_call(functools.partial(attention_body, rows // 2, n_cols, n_ski...  20.9 us
    ppermute x12, starting transfers between devices, over_z(): return lax.ppermute(array, 'head', [(i, i ^ bits) for i in range(nz)])  18.3 us
    ppermute x22, starting transfers between devices, over_seq(): return lax.ppermute(array, 'seq', [(i, i ^ bits) for i in range(n_seq)])  16.3 us
    ppermute x22, waiting for transfers between devices, over_seq(): return lax.ppermute(array, 'seq', [(i, i ^ bits) for i in range(n_seq)])  6.88 us
  transfers between devices with their start and end apart: 34, of which 13 were waited for; matrix products, arithmetic and copies ran while one was open for 0% of the time, Pallas kernels for 24%

profile of v2, /device:TPU:0, one launch (start us, length us, event | category | flops | bytes accessed | tf_op | source)
XLA Modules:
  0.0 90.3 jit_solution(7435763068990495866)
XLA Ops:
  1.5 3.1 %collective-permute-start.3 = (bf16[32,1024]{1,0:T(8,128)(2,1)S(1)}, bf16[32,1024]{1,0:T(8,128)(2,1)S(1)}, u32[]{:S(2)}, u32[]{:S(2)}) collective-permute-start(bf16[32,1024]{1,0:T(8,128)(2,1)S(1)} %pad_maximum_fusion.1.refs_0_), channel_id=1, source_target_pairs={{0,1},{1,0},{2,3},{3,2},{4,5},{5,4},{6,7},{7,6},{8,9},{9,8},{10,11... | collective-permute-start | bytes 196616 | tf_op jit(solution)/shard_map/ppermute | solution.py:348
  4.6 2.6 %collective-permute-start.4 = (bf16[32,1024]{1,0:T(8,128)(2,1)S(1)}, bf16[32,1024]{1,0:T(8,128)(2,1)S(1)}, u32[]{:S(2)}, u32[]{:S(2)}) collective-permute-start(bf16[32,1024]{1,0:T(8,128)(2,1)S(1)} %pad_maximum_fusion.1.refs_0_), channel_id=1, source_target_pairs={{0,2},{1,3},{2,0},{3,1},{4,6},{5,7},{6,4},{7,5},{8,10},{9,11},{10,... | collective-permute-start | bytes 196616 | tf_op jit(solution)/shard_map/ppermute | solution.py:348
  7.2 4.7 %collective-permute-done.4.refs_2_ = bf16[32,1024]{1,0:T(8,128)(2,1)S(1)} collective-permute-done((bf16[32,1024]{1,0:T(8,128)(2,1)S(1)}, bf16[32,1024]{1,0:T(8,128)(2,1)S(1)}, u32[]{:S(2)}, u32[]{:S(2)}) %collective-permute-start.4) | collective-permute-done | bytes 65568 | tf_op jit(solution)/shard_map/ppermute | solution.py:348
  11.9 1.4 %collective-permute-done.5.refs_3_ = bf16[32,1024]{1,0:T(8,128)(2,1)S(1)} collective-permute-done((bf16[32,1024]{1,0:T(8,128)(2,1)S(1)}, bf16[32,1024]{1,0:T(8,128)(2,1)S(1)}, u32[]{:S(2)}, u32[]{:S(2)}) %collective-permute-start.5) | collective-permute-done | bytes 65568 | tf_op jit(solution)/shard_map/ppermute | solution.py:348
  13.9 2.4 %collective-permute-start.6 = (bf16[4,32,1024]{2,1,0:T(8,128)(2,1)S(1)}, bf16[4,32,1024]{2,1,0:T(8,128)(2,1)S(1)}, u32[]{:S(2)}, u32[]{:S(2)}) collective-permute-start(bf16[4,32,1024]{2,1,0:T(8,128)(2,1)S(1)} %get-tuple-element.47.refs_5_), channel_id=1, source_target_pairs={{0,24},{4,28},{8,16},{12,20},{16,8},{20,12},{24,0},{28,4},{1,25},{... | collective-permute-start | bytes 786440 | tf_op jit(solution)/shard_map/ppermute | solution.py:351
  17.4 2.3 %collective-permute-start.1 = (bf16[32,1024]{1,0:T(8,128)(2,1)S(1)}, bf16[32,1024]{1,0:T(8,128)(2,1)S(1)}, u32[]{:S(2)}, u32[]{:S(2)}) collective-permute-start(bf16[32,1024]{1,0:T(8,128)(2,1)S(1)} %pad_maximum_fusion.refs_0_), channel_id=1, source_target_pairs={{0,2},{1,3},{2,0},{3,1},{4,6},{5,7},{6,4},{7,5},{8,10},{9,11},{10,... | collective-permute-start | bytes 196616 | tf_op jit(solution)/shard_map/ppermute | solution.py:348
  19.7 1.9 %collective-permute-done.refs_1_.refs_4_ = bf16[32,1024]{1,0:T(8,128)(2,1)S(1)} collective-permute-done((bf16[32,1024]{1,0:T(8,128)(2,1)S(1)}, bf16[32,1024]{1,0:T(8,128)(2,1)S(1)}, u32[]{:S(2)}, u32[]{:S(2)}) %collective-permute-start) | collective-permute-done | bytes 65568 | tf_op jit(solution)/shard_map/ppermute | solution.py:348
  21.6 1.8 %collective-permute-start.2 = (bf16[32,1024]{1,0:T(8,128)(2,1)S(1)}, bf16[32,1024]{1,0:T(8,128)(2,1)S(1)}, u32[]{:S(2)}, u32[]{:S(2)}) collective-permute-start(bf16[32,1024]{1,0:T(8,128)(2,1)S(1)} %pad_maximum_fusion.refs_0_), channel_id=1, source_target_pairs={{0,3},{1,2},{2,1},{3,0},{4,7},{5,6},{6,5},{7,4},{8,11},{9,10},{10,... | collective-permute-start | bytes 196616 | tf_op jit(solution)/shard_map/ppermute | solution.py:348
  23.4 4.3 %collective-permute-done.2.refs_3_.refs_6_ = bf16[32,1024]{1,0:T(8,128)(2,1)S(1)} collective-permute-done((bf16[32,1024]{1,0:T(8,128)(2,1)S(1)}, bf16[32,1024]{1,0:T(8,128)(2,1)S(1)}, u32[]{:S(2)}, u32[]{:S(2)}) %collective-permute-start.2) | collective-permute-done | bytes 65568 | tf_op jit(solution)/shard_map/ppermute | solution.py:348
  29.4 1.6 %collective-permute-start.7 = (bf16[4,32,1024]{2,1,0:T(8,128)(2,1)S(1)}, bf16[4,32,1024]{2,1,0:T(8,128)(2,1)S(1)}, u32[]{:S(2)}, u32[]{:S(2)}) collective-permute-start(bf16[4,32,1024]{2,1,0:T(8,128)(2,1)S(1)} %get-tuple-element.48.refs_0_), channel_id=1, source_target_pairs={{0,8},{4,12},{8,0},{12,4},{16,24},{20,28},{24,16},{28,20},{1,9},{5... | collective-permute-start | bytes 786440 | tf_op jit(solution)/shard_map/ppermute | solution.py:351
  30.9 1.5 %collective-permute-start.8 = (bf16[4,32,1024]{2,1,0:T(8,128)(2,1)S(1)}, bf16[4,32,1024]{2,1,0:T(8,128)(2,1)S(1)}, u32[]{:S(2)}, u32[]{:S(2)}) collective-permute-start(bf16[4,32,1024]{2,1,0:T(8,128)(2,1)S(1)} %get-tuple-element.48.refs_0_), channel_id=1, source_target_pairs={{0,16},{4,20},{8,24},{12,28},{16,0},{20,4},{24,8},{28,12},{1,17},{... | collective-permute-start | bytes 786440 | tf_op jit(solution)/shard_map/ppermute | solution.py:351
  33.0 10.2 %attention.2 = (bf16[256,2048]{1,0:T(8,128)(2,1)}, bf16[256,2048]{1,0:T(8,128)(2,1)}, bf16[256,2048]{1,0:T(8,128)(2,1)}, bf16[256,2048]{1,0:T(8,128)(2,1)}, f32[...) custom-call(s32[2]{0:T(128)S(1)} %pad_add_fusion.refs_0_, ...), custom_call_target="tpu_custom_call" | custom-call | flops 2415919104 | bytes 8388608 | tf_op jit(solution)/shard_map/attention/pallas_call | solution.py:172
  45.6 1.6 %collective-permute-done.20.came_ref = bf16[4,4,32,1024]{3,2,1,0:T(8,128)(2,1)S(1)} collective-permute-done((bf16[4,4,32,1024]{3,2,1,0:T(8,128)(2,1)S(1)}, bf16[4,4,32,1024]{3,2,1,0:T(8,128)(2,1)S(1)}, u32[]{:S(2)}, u32[]{:S(2)}) %collective-permute-start.20) | collective-permute-done | bytes 1048608 | tf_op jit(solution)/shard_map/ppermute | solution.py:351
  51.0 10.8 %attention.3 = (bf16[256,2048]{1,0:T(8,128)(2,1)}, bf16[256,2048]{1,0:T(8,128)(2,1)}, bf16[256,2048]{1,0:T(8,128)(2,1)}, bf16[256,2048]{1,0:T(8,128)(2,1)}, f32[...) custom-call(s32[2]{0:T(128)S(1)} %pad_add_fusion.refs_0_, ...), custom_call_target="tpu_custom_call", output_to_operand_aliasing={{0}: (13, {}), {1}: (14, {}), {2}: (15, {}), {3}: (16, {})} | custom-call | flops 2415919104 | bytes 8388608 | tf_op jit(solution)/shard_map/attention/pallas_call | solution.py:172
  62.7 2.6 %collective-permute-done.27.came_ref = bf16[4,4,32,1024]{3,2,1,0:T(8,128)(2,1)S(1)} collective-permute-done((bf16[4,4,32,1024]{3,2,1,0:T(8,128)(2,1)S(1)}, bf16[4,4,32,1024]{3,2,1,0:T(8,128)(2,1)S(1)}, u32[]{:S(2)}, u32[]{:S(2)}) %collective-permute-start.27) | collective-permute-done | bytes 1048608 | tf_op jit(solution)/shard_map/ppermute | solution.py:351
  66.8 1.5 %collective-permute-start.29 = (bf16[4,32,1024]{2,1,0:T(8,128)(2,1)S(1)}, bf16[4,32,1024]{2,1,0:T(8,128)(2,1)S(1)}, u32[]{:S(2)}, u32[]{:S(2)}) collective-permute-start(bf16[4,32,1024]{2,1,0:T(8,128)(2,1)S(1)} %get-tuple-element.82), channel_id=1, source_target_pairs={{0,16},{4,20},{8,24},{12,28},{16,0},{20,4},{24,8},{28,12},{1,17},{... | collective-permute-start | bytes 786440 | tf_op jit(solution)/shard_map/ppermute | solution.py:351
  69.5 2.3 %collective-permute-start.25 = (bf16[32,1024]{1,0:T(8,128)(2,1)S(1)}, bf16[32,1024]{1,0:T(8,128)(2,1)S(1)}, u32[]{:S(2)}, u32[]{:S(2)}) collective-permute-start(bf16[32,1024]{1,0:T(8,128)(2,1)S(1)} %get-tuple-element.74), channel_id=1, source_target_pairs={{0,2},{1,3},{2,0},{3,1},{4,6},{5,7},{6,4},{7,5},{8,10},{9,11},{10,... | collective-permute-start | bytes 196616 | tf_op jit(solution)/shard_map/ppermute | solution.py:348
  71.8 1.9 %collective-permute-done.24.refs_4_ = bf16[32,1024]{1,0:T(8,128)(2,1)S(1)} collective-permute-done((bf16[32,1024]{1,0:T(8,128)(2,1)S(1)}, bf16[32,1024]{1,0:T(8,128)(2,1)S(1)}, u32[]{:S(2)}, u32[]{:S(2)}) %collective-permute-start.24) | collective-permute-done | bytes 65568 | tf_op jit(solution)/shard_map/ppermute | solution.py:348
  73.7 1.8 %collective-permute-start.26 = (bf16[32,1024]{1,0:T(8,128)(2,1)S(1)}, bf16[32,1024]{1,0:T(8,128)(2,1)S(1)}, u32[]{:S(2)}, u32[]{:S(2)}) collective-permute-start(bf16[32,1024]{1,0:T(8,128)(2,1)S(1)} %get-tuple-element.75), channel_id=1, source_target_pairs={{0,3},{1,2},{2,1},{3,0},{4,7},{5,6},{6,5},{7,4},{8,11},{9,10},{10,... | collective-permute-start | bytes 196616 | tf_op jit(solution)/shard_map/ppermute | solution.py:348
  75.5 4.3 %collective-permute-done.26.refs_6_ = bf16[32,1024]{1,0:T(8,128)(2,1)S(1)} collective-permute-done((bf16[32,1024]{1,0:T(8,128)(2,1)S(1)}, bf16[32,1024]{1,0:T(8,128)(2,1)S(1)}, u32[]{:S(2)}, u32[]{:S(2)}) %collective-permute-start.26) | collective-permute-done | bytes 65568 | tf_op jit(solution)/shard_map/ppermute | solution.py:348
  81.1 2.3 %collective-permute-start.32 = (bf16[32,1024]{1,0:T(8,128)(2,1)S(1)}, bf16[32,1024]{1,0:T(8,128)(2,1)S(1)}, u32[]{:S(2)}, u32[]{:S(2)}) collective-permute-start(bf16[32,1024]{1,0:T(8,128)(2,1)S(1)} %get-tuple-element.86), channel_id=1, source_target_pairs={{0,2},{1,3},{2,0},{3,1},{4,6},{5,7},{6,4},{7,5},{8,10},{9,11},{10,... | collective-permute-start | bytes 196616 | tf_op jit(solution)/shard_map/ppermute | solution.py:348
  83.4 2.0 %collective-permute-start.33 = (bf16[32,1024]{1,0:T(8,128)(2,1)S(1)}, bf16[32,1024]{1,0:T(8,128)(2,1)S(1)}, u32[]{:S(2)}, u32[]{:S(2)}) collective-permute-start(bf16[32,1024]{1,0:T(8,128)(2,1)S(1)} %get-tuple-element.87), channel_id=1, source_target_pairs={{0,3},{1,2},{2,1},{3,0},{4,7},{5,6},{6,5},{7,4},{8,11},{9,10},{10,... | collective-permute-start | bytes 196616 | tf_op jit(solution)/shard_map/ppermute | solution.py:348
  85.5 2.6 %collective-permute-done.32.refs_10_ = bf16[32,1024]{1,0:T(8,128)(2,1)S(1)} collective-permute-done((bf16[32,1024]{1,0:T(8,128)(2,1)S(1)}, bf16[32,1024]{1,0:T(8,128)(2,1)S(1)}, u32[]{:S(2)}, u32[]{:S(2)}) %collective-permute-start.32) | collective-permute-done | bytes 65568 | tf_op jit(solution)/shard_map/ppermute | solution.py:348
  88.1 1.4 %collective-permute-done.33.refs_11_ = bf16[32,1024]{1,0:T(8,128)(2,1)S(1)} collective-permute-done((bf16[32,1024]{1,0:T(8,128)(2,1)S(1)}, bf16[32,1024]{1,0:T(8,128)(2,1)S(1)}, u32[]{:S(2)}, u32[]{:S(2)}) %collective-permute-start.33) | collective-permute-done | bytes 65568 | tf_op jit(solution)/shard_map/ppermute | solution.py:348
  (61 shorter events, 16.6 us)
Async XLA Ops:
  1.5 5.7 %collective-permute-start.3 = (bf16[32,1024]{1,0:T(8,128)(2,1)S(1)}, bf16[32,1024]{1,0:T(8,128)(2,1)S(1)}, u32[]{:S(2)}, u32[]{:S(2)}) collective-permute-start(bf16[32,1024]{1,0:T(8,128)(2,1)S(1)} %pad_maximum_fusion.1.refs_0_), channel_id=1, source_target_pairs={{0,1},{1,0},{2,3},{3,2},{4,5},{5,4},{6,7},{7,6},{8,9},{9,8},{10,11... | collective-permute-start | bytes 196616 | tf_op jit(solution)/shard_map/ppermute | solution.py:348
  4.6 7.3 %collective-permute-start.4 = (bf16[32,1024]{1,0:T(8,128)(2,1)S(1)}, bf16[32,1024]{1,0:T(8,128)(2,1)S(1)}, u32[]{:S(2)}, u32[]{:S(2)}) collective-permute-start(bf16[32,1024]{1,0:T(8,128)(2,1)S(1)} %pad_maximum_fusion.1.refs_0_), channel_id=1, source_target_pairs={{0,2},{1,3},{2,0},{3,1},{4,6},{5,7},{6,4},{7,5},{8,10},{9,11},{10,... | collective-permute-start | bytes 196616 | tf_op jit(solution)/shard_map/ppermute | solution.py:348
  7.2 6.1 %collective-permute-start.5 = (bf16[32,1024]{1,0:T(8,128)(2,1)S(1)}, bf16[32,1024]{1,0:T(8,128)(2,1)S(1)}, u32[]{:S(2)}, u32[]{:S(2)}) collective-permute-start(bf16[32,1024]{1,0:T(8,128)(2,1)S(1)} %pad_maximum_fusion.1.refs_0_), channel_id=1, source_target_pairs={{0,3},{1,2},{2,1},{3,0},{4,7},{5,6},{6,5},{7,4},{8,11},{9,10},{10,... | collective-permute-start | bytes 196616 | tf_op jit(solution)/shard_map/ppermute | solution.py:348
  13.9 14.4 %collective-permute-start.6 = (bf16[4,32,1024]{2,1,0:T(8,128)(2,1)S(1)}, bf16[4,32,1024]{2,1,0:T(8,128)(2,1)S(1)}, u32[]{:S(2)}, u32[]{:S(2)}) collective-permute-start(bf16[4,32,1024]{2,1,0:T(8,128)(2,1)S(1)} %get-tuple-element.47.refs_5_), channel_id=1, source_target_pairs={{0,24},{4,28},{8,16},{12,20},{16,8},{20,12},{24,0},{28,4},{1,25},{... | collective-permute-start | bytes 786440 | tf_op jit(solution)/shard_map/ppermute | solution.py:351
  16.3 12.5 %collective-permute-start.10 = (bf16[4,32,1024]{2,1,0:T(8,128)(2,1)S(1)}, bf16[4,32,1024]{2,1,0:T(8,128)(2,1)S(1)}, u32[]{:S(2)}, u32[]{:S(2)}) collective-permute-start(bf16[4,32,1024]{2,1,0:T(8,128)(2,1)S(1)} %get-tuple-element.47.refs_5_), channel_id=1, source_target_pairs={{0,8},{4,12},{8,0},{12,4},{16,24},{20,28},{24,16},{28,20},{1,9},{5... | collective-permute-start | bytes 786440 | tf_op jit(solution)/shard_map/ppermute | solution.py:351
  16.9 12.0 %collective-permute-start.11 = (bf16[4,32,1024]{2,1,0:T(8,128)(2,1)S(1)}, bf16[4,32,1024]{2,1,0:T(8,128)(2,1)S(1)}, u32[]{:S(2)}, u32[]{:S(2)}) collective-permute-start(bf16[4,32,1024]{2,1,0:T(8,128)(2,1)S(1)} %get-tuple-element.47.refs_5_), channel_id=1, source_target_pairs={{0,16},{4,20},{8,24},{12,28},{16,0},{20,4},{24,8},{28,12},{1,17},{... | collective-permute-start | bytes 786440 | tf_op jit(solution)/shard_map/ppermute | solution.py:351
  17.4 6.0 %collective-permute-start.1 = (bf16[32,1024]{1,0:T(8,128)(2,1)S(1)}, bf16[32,1024]{1,0:T(8,128)(2,1)S(1)}, u32[]{:S(2)}, u32[]{:S(2)}) collective-permute-start(bf16[32,1024]{1,0:T(8,128)(2,1)S(1)} %pad_maximum_fusion.refs_0_), channel_id=1, source_target_pairs={{0,2},{1,3},{2,0},{3,1},{4,6},{5,7},{6,4},{7,5},{8,10},{9,11},{10,... | collective-permute-start | bytes 196616 | tf_op jit(solution)/shard_map/ppermute | solution.py:348
  21.6 6.1 %collective-permute-start.2 = (bf16[32,1024]{1,0:T(8,128)(2,1)S(1)}, bf16[32,1024]{1,0:T(8,128)(2,1)S(1)}, u32[]{:S(2)}, u32[]{:S(2)}) collective-permute-start(bf16[32,1024]{1,0:T(8,128)(2,1)S(1)} %pad_maximum_fusion.refs_0_), channel_id=1, source_target_pairs={{0,3},{1,2},{2,1},{3,0},{4,7},{5,6},{6,5},{7,4},{8,11},{9,10},{10,... | collective-permute-start | bytes 196616 | tf_op jit(solution)/shard_map/ppermute | solution.py:348
  29.4 13.8 %collective-permute-start.7 = (bf16[4,32,1024]{2,1,0:T(8,128)(2,1)S(1)}, bf16[4,32,1024]{2,1,0:T(8,128)(2,1)S(1)}, u32[]{:S(2)}, u32[]{:S(2)}) collective-permute-start(bf16[4,32,1024]{2,1,0:T(8,128)(2,1)S(1)} %get-tuple-element.48.refs_0_), channel_id=1, source_target_pairs={{0,8},{4,12},{8,0},{12,4},{16,24},{20,28},{24,16},{28,20},{1,9},{5... | collective-permute-start | bytes 786440 | tf_op jit(solution)/shard_map/ppermute | solution.py:351
  30.9 13.6 %collective-permute-start.8 = (bf16[4,32,1024]{2,1,0:T(8,128)(2,1)S(1)}, bf16[4,32,1024]{2,1,0:T(8,128)(2,1)S(1)}, u32[]{:S(2)}, u32[]{:S(2)}) collective-permute-start(bf16[4,32,1024]{2,1,0:T(8,128)(2,1)S(1)} %get-tuple-element.48.refs_0_), channel_id=1, source_target_pairs={{0,16},{4,20},{8,24},{12,28},{16,0},{20,4},{24,8},{28,12},{1,17},{... | collective-permute-start | bytes 786440 | tf_op jit(solution)/shard_map/ppermute | solution.py:351
  32.4 12.1 %collective-permute-start.9 = (bf16[4,32,1024]{2,1,0:T(8,128)(2,1)S(1)}, bf16[4,32,1024]{2,1,0:T(8,128)(2,1)S(1)}, u32[]{:S(2)}, u32[]{:S(2)}) collective-permute-start(bf16[4,32,1024]{2,1,0:T(8,128)(2,1)S(1)} %get-tuple-element.48.refs_0_), channel_id=1, source_target_pairs={{0,24},{4,28},{8,16},{12,20},{16,8},{20,12},{24,0},{28,4},{1,25},{... | collective-permute-start | bytes 786440 | tf_op jit(solution)/shard_map/ppermute | solution.py:351
  45.1 4.8 %collective-permute-start.17 = (bf16[4,32,1024]{2,1,0:T(8,128)(2,1)S(1)}, bf16[4,32,1024]{2,1,0:T(8,128)(2,1)S(1)}, u32[]{:S(2)}, u32[]{:S(2)}) collective-permute-start(bf16[4,32,1024]{2,1,0:T(8,128)(2,1)S(1)} %get-tuple-element.53.refs_2_.refs_6_), channel_id=1, source_target_pairs={{0,4},{4,0},{8,12},{12,8},{16,20},{20,16},{24,28},{28,24},{1,5},{5... | collective-permute-start | bytes 786440 | tf_op jit(solution)/shard_map/ppermute | solution.py:351
  45.1 5.9 %collective-permute-start.18 = (bf16[4,32,1024]{2,1,0:T(8,128)(2,1)S(1)}, bf16[4,32,1024]{2,1,0:T(8,128)(2,1)S(1)}, u32[]{:S(2)}, u32[]{:S(2)}) collective-permute-start(bf16[4,32,1024]{2,1,0:T(8,128)(2,1)S(1)} %get-tuple-element.54.refs_3_.refs_7_), channel_id=1, source_target_pairs={{0,4},{4,0},{8,12},{12,8},{16,20},{20,16},{24,28},{28,24},{1,5},{5... | collective-permute-start | bytes 786440 | tf_op jit(solution)/shard_map/ppermute | solution.py:351
  45.6 5.5 %collective-permute-start.19 = (bf16[4,32,1024]{2,1,0:T(8,128)(2,1)S(1)}, bf16[4,32,1024]{2,1,0:T(8,128)(2,1)S(1)}, u32[]{:S(2)}, u32[]{:S(2)}) collective-permute-start(bf16[4,32,1024]{2,1,0:T(8,128)(2,1)S(1)} %get-tuple-element.55.refs_4_.refs_8_), channel_id=1, source_target_pairs={{0,4},{4,0},{8,12},{12,8},{16,20},{20,16},{24,28},{28,24},{1,5},{5... | collective-permute-start | bytes 786440 | tf_op jit(solution)/shard_map/ppermute | solution.py:351
  47.5 14.3 %collective-permute-start.21 = (bf16[4,32,1024]{2,1,0:T(8,128)(2,1)S(1)}, bf16[4,32,1024]{2,1,0:T(8,128)(2,1)S(1)}, u32[]{:S(2)}, u32[]{:S(2)}) collective-permute-start(bf16[4,32,1024]{2,1,0:T(8,128)(2,1)S(1)} %get-tuple-element.69), channel_id=1, source_target_pairs={{0,8},{4,12},{8,0},{12,4},{16,24},{20,28},{24,16},{28,20},{1,9},{5... | collective-permute-start | bytes 786440 | tf_op jit(solution)/shard_map/ppermute | solution.py:351
  48.8 13.1 %collective-permute-start.22 = (bf16[4,32,1024]{2,1,0:T(8,128)(2,1)S(1)}, bf16[4,32,1024]{2,1,0:T(8,128)(2,1)S(1)}, u32[]{:S(2)}, u32[]{:S(2)}) collective-permute-start(bf16[4,32,1024]{2,1,0:T(8,128)(2,1)S(1)} %get-tuple-element.70), channel_id=1, source_target_pairs={{0,16},{4,20},{8,24},{12,28},{16,0},{20,4},{24,8},{28,12},{1,17},{... | collective-permute-start | bytes 786440 | tf_op jit(solution)/shard_map/ppermute | solution.py:351
  49.8 12.6 %collective-permute-start.23 = (bf16[4,32,1024]{2,1,0:T(8,128)(2,1)S(1)}, bf16[4,32,1024]{2,1,0:T(8,128)(2,1)S(1)}, u32[]{:S(2)}, u32[]{:S(2)}) collective-permute-start(bf16[4,32,1024]{2,1,0:T(8,128)(2,1)S(1)} %get-tuple-element.71), channel_id=1, source_target_pairs={{0,24},{4,28},{8,16},{12,20},{16,8},{20,12},{24,0},{28,4},{1,25},{... | collective-permute-start | bytes 786440 | tf_op jit(solution)/shard_map/ppermute | solution.py:351
  66.0 13.8 %collective-permute-start.28 = (bf16[4,32,1024]{2,1,0:T(8,128)(2,1)S(1)}, bf16[4,32,1024]{2,1,0:T(8,128)(2,1)S(1)}, u32[]{:S(2)}, u32[]{:S(2)}) collective-permute-start(bf16[4,32,1024]{2,1,0:T(8,128)(2,1)S(1)} %get-tuple-element.81), channel_id=1, source_target_pairs={{0,8},{4,12},{8,0},{12,4},{16,24},{20,28},{24,16},{28,20},{1,9},{5... | collective-permute-start | bytes 786440 | tf_op jit(solution)/shard_map/ppermute | solution.py:351
  66.8 13.0 %collective-permute-start.29 = (bf16[4,32,1024]{2,1,0:T(8,128)(2,1)S(1)}, bf16[4,32,1024]{2,1,0:T(8,128)(2,1)S(1)}, u32[]{:S(2)}, u32[]{:S(2)}) collective-permute-start(bf16[4,32,1024]{2,1,0:T(8,128)(2,1)S(1)} %get-tuple-element.82), channel_id=1, source_target_pairs={{0,16},{4,20},{8,24},{12,28},{16,0},{20,4},{24,8},{28,12},{1,17},{... | collective-permute-start | bytes 786440 | tf_op jit(solution)/shard_map/ppermute | solution.py:351
  68.3 12.2 %collective-permute-start.30 = (bf16[4,32,1024]{2,1,0:T(8,128)(2,1)S(1)}, bf16[4,32,1024]{2,1,0:T(8,128)(2,1)S(1)}, u32[]{:S(2)}, u32[]{:S(2)}) collective-permute-start(bf16[4,32,1024]{2,1,0:T(8,128)(2,1)S(1)} %get-tuple-element.83), channel_id=1, source_target_pairs={{0,24},{4,28},{8,16},{12,20},{16,8},{20,12},{24,0},{28,4},{1,25},{... | collective-permute-start | bytes 786440 | tf_op jit(solution)/shard_map/ppermute | solution.py:351
  69.5 6.0 %collective-permute-start.25 = (bf16[32,1024]{1,0:T(8,128)(2,1)S(1)}, bf16[32,1024]{1,0:T(8,128)(2,1)S(1)}, u32[]{:S(2)}, u32[]{:S(2)}) collective-permute-start(bf16[32,1024]{1,0:T(8,128)(2,1)S(1)} %get-tuple-element.74), channel_id=1, source_target_pairs={{0,2},{1,3},{2,0},{3,1},{4,6},{5,7},{6,4},{7,5},{8,10},{9,11},{10,... | collective-permute-start | bytes 196616 | tf_op jit(solution)/shard_map/ppermute | solution.py:348
  73.7 6.1 %collective-permute-start.26 = (bf16[32,1024]{1,0:T(8,128)(2,1)S(1)}, bf16[32,1024]{1,0:T(8,128)(2,1)S(1)}, u32[]{:S(2)}, u32[]{:S(2)}) collective-permute-start(bf16[32,1024]{1,0:T(8,128)(2,1)S(1)} %get-tuple-element.75), channel_id=1, source_target_pairs={{0,3},{1,2},{2,1},{3,0},{4,7},{5,6},{6,5},{7,4},{8,11},{9,10},{10,... | collective-permute-start | bytes 196616 | tf_op jit(solution)/shard_map/ppermute | solution.py:348
  81.1 7.0 %collective-permute-start.32 = (bf16[32,1024]{1,0:T(8,128)(2,1)S(1)}, bf16[32,1024]{1,0:T(8,128)(2,1)S(1)}, u32[]{:S(2)}, u32[]{:S(2)}) collective-permute-start(bf16[32,1024]{1,0:T(8,128)(2,1)S(1)} %get-tuple-element.86), channel_id=1, source_target_pairs={{0,2},{1,3},{2,0},{3,1},{4,6},{5,7},{6,4},{7,5},{8,10},{9,11},{10,... | collective-permute-start | bytes 196616 | tf_op jit(solution)/shard_map/ppermute | solution.py:348
  83.4 6.1 %collective-permute-start.33 = (bf16[32,1024]{1,0:T(8,128)(2,1)S(1)}, bf16[32,1024]{1,0:T(8,128)(2,1)S(1)}, u32[]{:S(2)}, u32[]{:S(2)}) collective-permute-start(bf16[32,1024]{1,0:T(8,128)(2,1)S(1)} %get-tuple-element.87), channel_id=1, source_target_pairs={{0,3},{1,2},{2,1},{3,0},{4,7},{5,6},{6,5},{7,4},{8,11},{9,10},{10,... | collective-permute-start | bytes 196616 | tf_op jit(solution)/shard_map/ppermute | solution.py:348
  (10 other events, 37.6 us)

commit v3 on v2

v3 whole, which is shorter than its diff:
```python
import functools
import math

import jax
import jax.numpy as jnp
from jax import lax
from jax.experimental import pallas as pl
from jax.experimental.pallas import tpu as pltpu
from jax.sharding import PartitionSpec as P

HEADS = 16
HEAD_DIM = 128
BLOCK = 128
SUMMARY = 8
EDGE = 16

neg_fill = -1e30
scaling = 1.0 / math.sqrt(HEAD_DIM)
exponent = scaling / math.log(2.0)
chunk_heads = (4, 4)
unroll = 2
vmem_bytes = 40 * 1024 * 1024
in_vmem = pl.BlockSpec(memory_space=pltpu.VMEM)
in_hbm = pl.BlockSpec(memory_space=pltpu.HBM)
in_smem = pl.BlockSpec(memory_space=pltpu.SMEM)
params = pltpu.CompilerParams(vmem_limit_bytes=vmem_bytes)


def dot(left, right, left_dim, right_dim):
    return lax.dot_general(
        left, right, (((left_dim,), (right_dim,)), ((), ())), preferred_element_type=jnp.float32
    )


def block_mask():
    key = lax.broadcasted_iota(jnp.int32, (BLOCK, BLOCK), 1)
    query = lax.broadcasted_iota(jnp.int32, (BLOCK, BLOCK), 0)
    return jnp.where(key <= query, 0.0, neg_fill)


def far_mask(seq_pos, z_pos, n_cols, nz, n_sum, tokens):
    shape = (2 * tokens, n_cols * nz * 2 * n_sum)
    key = lax.broadcasted_iota(jnp.int32, shape, 1)
    query = lax.broadcasted_iota(jnp.int32, shape, 0)
    piece = key // n_sum
    column = piece // (2 * nz)
    source = (seq_pos ^ (2 * column + piece % 2)) * nz + (z_pos ^ ((piece // 2) % nz))
    here = (seq_pos ^ (query // tokens)) * nz + z_pos
    before = (key % n_sum) // SUMMARY < (query % tokens) // BLOCK
    return jnp.where((source < here) | ((source == here) & before), 0.0, neg_fill)


def core_window(place_ref, flip, half, at, size):
    core = (place_ref[0] + flip) % 2
    return pl.ds(pl.multiple_of(core * half + at, HEAD_DIM), size)


def pack_body(place_ref, *refs):
    sources, (mine_ref, other_ref, away_ref, tiles, tile_sem, sem) = refs[:4], refs[4:]
    tokens, width = sources[0].shape
    n_blocks = tokens // BLOCK
    half = width // 2
    copies = []
    for i, source in enumerate(sources[1:3]):
        for b in range(n_blocks):
            row = i * n_blocks + b
            tile = pl.ds((b + 1) * BLOCK - EDGE, EDGE)
            copies.append(pltpu.make_async_copy(source.at[tile, :], tiles.at[row], tile_sem.at[row]))
    columns = [
        pltpu.make_async_copy(
            source.at[:, core_window(place_ref, 1, half, 0, half)], away_ref.at[i], sem.at[i]
        )
        for i, source in enumerate(sources)
    ]
    for copy in copies + columns:
        copy.start()
    for copy in copies:
        copy.wait()
    for flip, target in enumerate((mine_ref, other_ref)):
        to = core_window(place_ref, flip, half, 0, half)
        rows = [tiles[row, EDGE - SUMMARY :, to] for row in range(2 * n_blocks)]
        target[...] = jnp.concatenate(rows, axis=0)
    for copy in columns:
        copy.wait()


def pack(place, arrays):
    tokens, width = arrays[0].shape
    kind = arrays[0].dtype
    n_blocks = tokens // BLOCK
    shape = jax.ShapeDtypeStruct((2 * n_blocks * SUMMARY, width // 2), kind)
    return pl.pallas_call(
        pack_body,
        in_specs=[in_smem] + [in_hbm] * 4,
        out_specs=[in_vmem] * 3,
        out_shape=[shape] * 2 + [jax.ShapeDtypeStruct((4, tokens, width // 2), kind)],
        scratch_shapes=[
            pltpu.VMEM((2 * n_blocks, EDGE, width), kind),
            pltpu.SemaphoreType.DMA((2 * n_blocks,)),
            pltpu.SemaphoreType.DMA((4,)),
        ],
        compiler_params=params,
        name="pack",
    )(place, *[pltpu.with_memory_space_constraint(x, pltpu.HBM) for x in arrays])


def join_body(at, mine_ref, came_ref, *refs):
    ref = refs[-1]
    rows, width = mine_ref.shape[0], ref.shape[1]
    ref[:rows] = mine_ref[:, at : at + width]
    ref[rows:] = came_ref[:, at : at + width]


def join(mine, came, at, size, *after):
    return pl.pallas_call(
        functools.partial(join_body, at),
        in_specs=[in_vmem] * (2 + len(after)),
        out_specs=in_vmem,
        out_shape=jax.ShapeDtypeStruct((2 * mine.shape[0], size), mine.dtype),
        compiler_params=params,
        name="join",
    )(mine, came, *after)


def attention_body(n_sum, n_cols, n_skip, first, heads, *refs):
    place_ref = refs[0]
    sources, came_ref = refs[1:5], refs[5]
    col_refs = refs[6 : 6 + n_cols]
    outs = refs[6 + n_cols + n_skip :]
    targets = outs[:4]
    sent_ref, near_ref = outs[4:6]
    back_refs = outs[6 : 6 + n_cols]
    near_mask, away_mask, loads, stores, load_sem, store_sem = outs[6 + n_cols :]
    tokens, width = sources[0].shape
    nz = col_refs[0].shape[0]
    steps = heads // unroll
    span = unroll * HEAD_DIM

    def window(step):
        return core_window(place_ref, 0, width // 2, first * HEAD_DIM + step * span, span)

    def load(step, i):
        return pltpu.make_async_copy(
            sources[i].at[:, window(step)], loads.at[step, i], load_sem.at[step, i]
        )

    def store(step, i):
        return pltpu.make_async_copy(
            stores.at[step, i], targets[i].at[:, window(step)], store_sem.at[step, i]
        )

    for step in range(steps):
        for i in range(4):
            load(step, i).start()
    n_blocks = tokens // BLOCK
    blocks = [slice(b * BLOCK, (b + 1) * BLOCK) for b in range(2 * n_blocks)]
    near_mask[...] = block_mask()
    away_mask[...] = far_mask(place_ref[0], place_ref[1], n_cols, nz, n_sum, tokens)

    def here(to):
        return pl.ds(pl.multiple_of(first * HEAD_DIM + to.start, HEAD_DIM), HEAD_DIM)

    def far_rows(offset, to):
        parts = []
        for ref in col_refs:
            for j in range(nz):
                for core in range(2):
                    row = 2 * core * n_sum + offset
                    parts.append(ref[j, row : row + n_sum, to])
        return jnp.concatenate(parts, axis=0)

    def keep(step, i, at, to, b, value):
        if b < n_blocks:
            stores[step, i, blocks[b], at] = value
        else:
            sent_ref[i, blocks[b - n_blocks], here(to)] = value

    def head(step, at, to):
        q, k_loc, v_loc, g = (
            jnp.concatenate([loads[step, i, :, at], came_ref[i, :, here(to)]], axis=0) for i in range(4)
        )
        k_far = far_rows(0, to)
        v_far = far_rows(n_sum, to)
        mask = near_mask[...]
        s_loc = jnp.concatenate([dot(q[b], k_loc[b], 1, 1) + mask for b in blocks], axis=0)
        s_far = dot(q, k_far, 1, 1) + away_mask[...]
        high = jnp.maximum(
            jnp.max(s_loc, axis=1, keepdims=True), jnp.max(s_far, axis=1, keepdims=True)
        )
        e_loc = jnp.exp2((s_loc - high) * exponent)
        e_far = jnp.exp2((s_far - high) * exponent)
        norm = jnp.sum(e_loc, axis=1, keepdims=True) + jnp.sum(e_far, axis=1, keepdims=True)
        inv = 1.0 / norm
        eb_loc = e_loc.astype(jnp.bfloat16)
        eb_far = e_far.astype(jnp.bfloat16)
        out = jnp.concatenate([dot(eb_loc[b], v_loc[b], 1, 0) for b in blocks], axis=0) + dot(
            eb_far, v_far, 1, 0
        )
        out = (out * inv).astype(jnp.bfloat16)
        gf = g.astype(jnp.float32)
        delta = jnp.sum(gf * out.astype(jnp.float32), axis=1, keepdims=True)
        factor = inv * scaling
        t_loc = jnp.concatenate([dot(g[b], v_loc[b], 1, 1) for b in blocks], axis=0)
        t_loc = (t_loc - delta) * factor
        t_far = (dot(g, v_far, 1, 1) - delta) * factor
        ds_loc = (eb_loc.astype(jnp.float32) * t_loc).astype(jnp.bfloat16)
        ds_far = (eb_far.astype(jnp.float32) * t_far).astype(jnp.bfloat16)
        dq = jnp.concatenate([dot(ds_loc[b], k_loc[b], 1, 0) for b in blocks], axis=0) + dot(
            ds_far, k_far, 1, 0
        )
        dq = dq.astype(jnp.bfloat16)
        gi = (gf * inv).astype(jnp.bfloat16)
        for n, b in enumerate(blocks):
            keep(step, 0, at, to, n, out[b])
            keep(step, 1, at, to, n, dq[b])
            for i, (left, right) in enumerate(((ds_loc, q), (eb_loc, gi))):
                part = dot(left[b], right[b], 0, 0)
                keep(step, 2 + i, at, to, n, part.astype(jnp.bfloat16))
                t, row = n // n_blocks, (i * n_blocks + n % n_blocks) * EDGE
                near_ref[t, row : row + EDGE, to] = part[BLOCK - EDGE :, :]
        dk_far = dot(q, ds_far, 0, 0).astype(jnp.bfloat16).T
        dv_far = dot(gi, eb_far, 0, 0).astype(jnp.bfloat16).T
        row = 0
        for ref in back_refs:
            for j in range(nz):
                for core in range(2):
                    to_row = 2 * core * n_sum
                    ref[j, to_row : to_row + n_sum, to] = dk_far[row : row + n_sum]
                    ref[j, to_row + n_sum : to_row + 2 * n_sum, to] = dv_far[row : row + n_sum]
                    row += n_sum

    def turn(step, carried):
        for i in range(4):
            load(step, i).wait()
        for u in range(unroll):
            to = pl.ds(pl.multiple_of(step * span + u * HEAD_DIM, HEAD_DIM), HEAD_DIM)
            head(step, slice(u * HEAD_DIM, (u + 1) * HEAD_DIM), to)
        for i in range(4):
            store(step, i).start()
        return carried

    lax.fori_loop(0, steps, turn, 0)
    for step in range(steps):
        for i in range(4):
            store(step, i).wait()


def attention(place, mine, came, cols, earlier, after, first, heads):
    tokens, width = mine[0].shape
    n_cols = len(cols)
    nz, rows, chunk_width = cols[0].shape
    n_sum = rows // 4
    nkeys = n_cols * nz * rows // 2
    n_blocks = tokens // BLOCK
    steps = heads // unroll
    full = jax.ShapeDtypeStruct((tokens, width), jnp.bfloat16)
    n_skip = len(earlier) + len(after)
    rest = [
        jax.ShapeDtypeStruct((4, tokens, width // 2), jnp.bfloat16),
        jax.ShapeDtypeStruct((2, 2 * n_blocks * EDGE, chunk_width), jnp.float32),
    ] + [jax.ShapeDtypeStruct((nz, rows, chunk_width), jnp.bfloat16)] * n_cols
    mine = [pltpu.with_memory_space_constraint(x, pltpu.HBM) for x in mine]
    return pl.pallas_call(
        functools.partial(attention_body, n_sum, n_cols, n_skip, first, heads),
        in_specs=[in_smem]
        + [in_hbm] * 4
        + [in_vmem] * (1 + n_cols)
        + [in_hbm] * len(earlier[:4])
        + [in_vmem] * (len(earlier[4:]) + len(after)),
        out_specs=[in_hbm] * 4 + [in_vmem] * len(rest),
        out_shape=[full] * 4 + rest,
        scratch_shapes=[
            pltpu.VMEM((BLOCK, BLOCK), jnp.float32),
            pltpu.VMEM((2 * tokens, nkeys), jnp.float32),
            pltpu.VMEM((steps, 4, tokens, unroll * HEAD_DIM), jnp.bfloat16),
            pltpu.VMEM((steps, 4, tokens, unroll * HEAD_DIM), jnp.bfloat16),
            pltpu.SemaphoreType.DMA((steps, 4)),
            pltpu.SemaphoreType.DMA((steps, 4)),
        ],
        input_output_aliases={6 + n_cols + i: i for i in range(len(earlier))},
        compiler_params=params,
        cost_estimate=pl.CostEstimate(
            flops=heads * 24 * tokens * (BLOCK + nkeys) * HEAD_DIM,
            bytes_accessed=heads * HEAD_DIM * (32 * tokens + 8 * nkeys),
            transcendentals=heads * 2 * tokens * (BLOCK + nkeys),
        ),
        name="attention",
    )(place, *mine, came, *cols, *earlier, *after)


def hold_body(*refs):
    pass


def hold(arrays, *after):
    return pl.pallas_call(
        hold_body,
        in_specs=[in_vmem] * (len(arrays) + len(after)),
        out_specs=[in_vmem] * len(arrays),
        out_shape=[jax.ShapeDtypeStruct(a.shape, a.dtype) for a in arrays],
        input_output_aliases={i: i for i in range(len(arrays))},
        compiler_params=params,
        name="hold",
    )(*arrays, *after)


def line_body(n_in, *refs):
    for j in range(n_in):
        refs[-1][j] = refs[j][...]


def stack_line(pieces, *after):
    return pl.pallas_call(
        functools.partial(line_body, len(pieces)),
        in_specs=[in_vmem] * (len(pieces) + len(after)),
        out_specs=in_vmem,
        out_shape=jax.ShapeDtypeStruct((len(pieces),) + pieces[0].shape, pieces[0].dtype),
        compiler_params=params,
        name="line",
    )(*pieces, *after)


def column_sum_body(n_in, n_after, *refs):
    in_refs, out_refs = refs[:n_in], refs[n_in + n_after :]
    for j, ref in enumerate(out_refs):
        total = in_refs[0][j].astype(jnp.float32)
        for came in in_refs[1:]:
            total = total + came[j].astype(jnp.float32)
        ref[...] = total.astype(ref.dtype)


def column_sum(parts, *after):
    nz = parts[0].shape[0]
    shapes = [
        jax.ShapeDtypeStruct(parts[0].shape[1:], jnp.float32 if j == 0 else jnp.bfloat16)
        for j in range(nz)
    ]
    return pl.pallas_call(
        functools.partial(column_sum_body, len(parts), len(after)),
        in_specs=[in_vmem] * (len(parts) + len(after)),
        out_specs=[in_vmem] * nz,
        out_shape=shapes,
        compiler_params=params,
        name="column_sum",
    )(*parts, *after)


def edge_body(n_terms, *refs):
    terms, targets = refs[:-2], refs[-2:]
    at = 0
    for c in range(0, len(terms), n_terms):
        near_ref, *ends = terms[c : c + n_terms]
        total = ends[0][...]
        for term in ends[1:]:
            total = total + term[...].astype(jnp.float32)
        rows = total.shape[0] // 2
        to = slice(at, at + total.shape[1])
        at += total.shape[1]
        for t, target in enumerate(targets):
            for n in range(rows // SUMMARY):
                tile = near_ref[t, n * EDGE : (n + 1) * EDGE, :]
                more = total[t * rows + n * SUMMARY : t * rows + (n + 1) * SUMMARY]
                tile = [tile[: EDGE - SUMMARY], tile[EDGE - SUMMARY :] + more]
                tile = jnp.concatenate(tile, axis=0).astype(target.dtype)
                target[n * EDGE : (n + 1) * EDGE, to] = tile


def edge(chunks):
    width = sum(chunk[0].shape[2] for chunk in chunks)
    shape = jax.ShapeDtypeStruct((chunks[0][0].shape[1], width), jnp.bfloat16)
    return pl.pallas_call(
        functools.partial(edge_body, len(chunks[0])),
        in_specs=[in_vmem] * (len(chunks) * len(chunks[0])),
        out_specs=[in_vmem] * 2,
        out_shape=[shape] * 2,
        compiler_params=params,
        name="edge",
    )(*[term for chunk in chunks for term in chunk])


def settle_body(n_came, place_ref, *refs):
    came_refs, targets = refs[:n_came], refs[n_came + 4 : n_came + 8]
    sem = refs[n_came + 8]
    width = targets[0].shape[1]
    copies = []
    at = 0
    for c, came in enumerate(came_refs):
        to = core_window(place_ref, 1, width // 2, at, came.shape[2])
        at += came.shape[2]
        for i, target in enumerate(targets):
            copies.append(pltpu.make_async_copy(came.at[i], target.at[:, to], sem.at[c, i]))
    for copy in copies:
        copy.start()
    for copy in copies:
        copy.wait()


def settle(place, came, results):
    n = len(came)
    return pl.pallas_call(
        functools.partial(settle_body, n),
        in_specs=[in_smem] + [in_vmem] * n + [in_hbm] * 4,
        out_specs=[in_hbm] * 4,
        out_shape=[jax.ShapeDtypeStruct(x.shape, x.dtype) for x in results],
        scratch_shapes=[pltpu.SemaphoreType.DMA((n, 4))],
        input_output_aliases={1 + n + i: i for i in range(4)},
        compiler_params=params,
        name="settle",
    )(place, *came, *results)


def finish_body(n_edges, n_blocks, place_ref, *refs):
    edges = refs[2 : 2 + n_edges]
    targets, sem = refs[2 + n_edges : 4 + n_edges], refs[4 + n_edges]
    width = targets[0].shape[1]
    copies = []
    at = 0
    for e, source in enumerate(edges):
        flip = e % 2
        to = core_window(place_ref, flip, width // 2, at, source.shape[1])
        at += flip * source.shape[1]
        for n in range(2 * n_blocks):
            i, b = divmod(n, n_blocks)
            copies.append(
                pltpu.make_async_copy(
                    source.at[pl.ds(n * EDGE, EDGE)],
                    targets[i].at[pl.ds((b + 1) * BLOCK - EDGE, EDGE), to],
                    sem.at[e, n],
                )
            )
    for copy in copies:
        copy.start()
    for copy in copies:
        copy.wait()


def finish(place, dk, dv, edges):
    n_blocks = dk.shape[0] // BLOCK
    return pl.pallas_call(
        functools.partial(finish_body, len(edges), n_blocks),
        in_specs=[in_smem] + [in_hbm] * 2 + [in_vmem] * len(edges),
        out_specs=[in_hbm] * 2,
        out_shape=[jax.ShapeDtypeStruct(dk.shape, dk.dtype)] * 2,
        scratch_shapes=[pltpu.SemaphoreType.DMA((len(edges), 2 * n_blocks))],
        input_output_aliases={1: 0, 2: 1},
        compiler_params=params,
        name="finish",
    )(place, dk, dv, *edges)


def on_device(n_seq, nz, queries, keys_in, values_in, cotangent):
    n_cols = n_seq // 2
    n_chunks = len(chunk_heads)
    firsts = [sum(chunk_heads[:c]) for c in range(n_chunks)]

    def over_z(array, bits):
        return lax.ppermute(array, "head", [(i, i ^ bits) for i in range(nz)])

    def over_seq(array, bits):
        return lax.ppermute(array, "seq", [(i, i ^ bits) for i in range(n_seq)])

    def swap_z(pieces):
        return [over_z(pieces[j], j) for j in reversed(range(1, nz))][::-1]

    def swap_columns(parts):
        return [over_seq(parts[c], 2 * c) for c in reversed(range(1, n_cols))][::-1]

    place = jnp.stack([lax.axis_index("seq"), lax.axis_index("head")]).astype(jnp.int32)
    arrays = (queries, keys_in, values_in, cotangent)
    mine, other, part = pack(place, arrays)
    came = over_seq(other, 1)
    columns = []
    theirs = None
    for c in range(n_chunks):
        width = chunk_heads[c] * HEAD_DIM
        start = join(mine, came, firsts[c] * HEAD_DIM, width, *([theirs] if c else []))
        pieces = [start] + swap_z([start] * nz)
        if c == 0:
            theirs = over_seq(hold([part], *pieces[1:])[0], 1)
        line = stack_line(pieces, *[cols[-1] for cols in columns[-1:]])
        columns.append([line] + swap_columns([line] * n_cols))

    results = ()
    chunks = []
    back = None
    for c in range(n_chunks):
        made = attention(
            place,
            arrays,
            theirs,
            columns[c],
            results,
            [cols[0] for cols in columns[c + 1 : c + 2]],
            firsts[c],
            chunk_heads[c],
        )
        results, near, parts = made[:5], made[5], list(made[6:])
        waits = columns[c + 1][1:] if c + 1 < n_chunks else []
        if back is not None:
            ends = column_sum(back[1], near)
            waits = waits + list(ends[:1])
        moved = swap_columns(parts[:1] + list(hold(parts[1:], *waits)))
        if back is not None:
            chunks.append([back[0], ends[0]] + swap_z(ends))
        back = near, parts[:1] + moved
    ends = column_sum(back[1], *chunks[-1][2:])
    chunks.append([back[0], ends[0]] + swap_z(ends))
    *results, sent = results
    (sent,) = hold([sent], ends[0])
    results = settle(place, [over_seq(sent, 1)], results)
    own, away = edge(chunks)
    attended, grad_queries, dk, dv = results
    edges = [own, over_seq(away, 1)]
    grad_keys, grad_values = finish(place, dk, dv, edges)
    return (attended, grad_queries, grad_keys, grad_values)


def solution(mesh):
    spec = P(("seq", "head"), None)
    return jax.shard_map(
        functools.partial(on_device, mesh.shape["seq"], mesh.shape["head"]),
        mesh=mesh,
        in_specs=(spec,) * 4,
        out_specs=(spec,) * 4,
        check_vma=False,
    )
```

time: 90.6 us -> 86 us (0.949)
  Pallas kernels: 24.7 us -> 23.2 us
  starting transfers between devices: 34.6 us -> 33.2 us
    ppermute x12, waiting for transfers between devices: 22.5 us -> 18.6 us  [over_z(): return lax.ppermute(array, 'head', [(i, i ^ bits) for i in range(nz)])]
    ppermute x22 -> x16, waiting for transfers between devices: 6.88 us -> 9.87 us  [over_seq(): return lax.ppermute(array, 'seq', [(i, i ^ bits) for i in range(n_seq)])]
    ppermute x22 -> x16, starting transfers between devices: 16.3 us -> 14.8 us  [over_seq(): return lax.ppermute(array, 'seq', [(i, i ^ bits) for i in range(n_seq)])]
    pallas_call x3 -> x2, Pallas kernels: 1.24 us -> 0.04 us  [stack_line(): pl.pallas_call(functools.partial(line_body, len(pieces)), in_specs=[in_vm...]
    pallas_call x5 -> x8, Pallas kernels: 22.7 us -> 22.9 us  [the longest x2 17.3 us: attention(): pl.pallas_call(functools.partial(attention_body, n_sum, n_cols, n_skip, f...]
  transfers between devices with their start and end apart: 34 -> 28, of which waited for: 13 -> 15; matrix products, arithmetic and copies ran while one was open for 0% -> 0% of each run, Pallas kernels for 24% -> 23%
where the time goes in v3:
time: 86 us; the launch traced here: 85.8 us
  starting transfers between devices  33.2 us (39%)
  waiting for transfers between devices  28.5 us (33%)
  Pallas kernels  23.2 us (27%)
    ppermute x12, waiting for transfers between devices, over_z(): return lax.ppermute(array, 'head', [(i, i ^ bits) for i in range(nz)])  18.6 us
    ppermute x12, starting transfers between devices, over_z(): return lax.ppermute(array, 'head', [(i, i ^ bits) for i in range(nz)])  18.4 us
    pallas_call x2, Pallas kernels, attention(): pl.pallas_call(functools.partial(attention_body, n_sum, n_cols, n_skip, f...  17.3 us
    ppermute x16, starting transfers between devices, over_seq(): return lax.ppermute(array, 'seq', [(i, i ^ bits) for i in range(n_seq)])  14.8 us
    ppermute x16, waiting for transfers between devices, over_seq(): return lax.ppermute(array, 'seq', [(i, i ^ bits) for i in range(n_seq)])  9.87 us
    pallas_call x1, Pallas kernels, pack(): pl.pallas_call(pack_body, in_specs=[in_smem] + [in_hbm] * 4, out_specs=[i...  2.24 us
    pallas_call x1, Pallas kernels, settle(): pl.pallas_call(functools.partial(settle_body, n), in_specs=[in_smem] + [i...  1.9 us
  transfers between devices with their start and end apart: 28, of which 15 were waited for; matrix products, arithmetic and copies ran while one was open for 0% of the time, Pallas kernels for 23%

profile of v3, /device:TPU:0, one launch (start us, length us, event | category | flops | bytes accessed | tf_op | source)
XLA Modules:
  0.0 85.8 jit_solution(15685609315758161000)
XLA Ops:
  0.7 2.2 %pack.1 = (bf16[32,1024]{1,0:T(8,128)(2,1)S(1)}, bf16[32,1024]{1,0:T(8,128)(2,1)S(1)}, bf16[4,256,1024]{2,1,0:T(8,128)(2,1)S(1)}) custom-call(s32[2]{0:T(128)S(1)} %pad_add_fusion.place_ref.refs_0_, bf16[256,2048]{1,0:T(8,128)(2,1)} %refs_1_.5, bf16[256,2048]{1,0:T(8,128)(2,1)} %refs_2_.5, bf16[256,2048]{1,0:T(8,128)(2,1)} %refs_3_.5, bf16[256,2048]{1,0:T(8,128)(2,1)} %refs_4_.3), custom_call_target="tpu_custom_call" | custom-call | tf_op jit(solution)/shard_map/pack/pallas_call | solution.py:92
  4.4 4.9 %collective-permute-start.3 = (bf16[64,512]{1,0:T(8,128)(2,1)S(1)}, bf16[64,512]{1,0:T(8,128)(2,1)S(1)}, u32[]{:S(2)}, u32[]{:S(2)}) collective-permute-start(bf16[64,512]{1,0:T(8,128)(2,1)S(1)} %join.2.refs_0_), channel_id=1, source_target_pairs={{0,3},{1,2},{2,1},{3,0},{4,7},{5,6},{6,5},{7,4},{8,11},{9,10},{10,... | collective-permute-start | bytes 196616 | tf_op jit(solution)/shard_map/ppermute | solution.py:457
  10.0 2.0 %collective-permute-done.3.refs_3_ = bf16[64,512]{1,0:T(8,128)(2,1)S(1)} collective-permute-done((bf16[64,512]{1,0:T(8,128)(2,1)S(1)}, bf16[64,512]{1,0:T(8,128)(2,1)S(1)}, u32[]{:S(2)}, u32[]{:S(2)}) %collective-permute-start.3) | collective-permute-done | bytes 65568 | tf_op jit(solution)/shard_map/ppermute | solution.py:457
  12.0 3.2 %collective-permute-done.2.refs_2_ = bf16[64,512]{1,0:T(8,128)(2,1)S(1)} collective-permute-done((bf16[64,512]{1,0:T(8,128)(2,1)S(1)}, bf16[64,512]{1,0:T(8,128)(2,1)S(1)}, u32[]{:S(2)}, u32[]{:S(2)}) %collective-permute-start.2) | collective-permute-done | bytes 65568 | tf_op jit(solution)/shard_map/ppermute | solution.py:457
  15.3 2.5 %collective-permute-start.8 = (bf16[4,64,512]{2,1,0:T(8,128)(2,1)S(1)}, bf16[4,64,512]{2,1,0:T(8,128)(2,1)S(1)}, u32[]{:S(2)}, u32[]{:S(2)}) collective-permute-start(bf16[4,64,512]{2,1,0:T(8,128)(2,1)S(1)} %line.2.refs_6_), channel_id=1, source_target_pairs={{0,24},{4,28},{8,16},{12,20},{16,8},{20,12},{24,0},{28,4},{1,25},{... | collective-permute-start | bytes 786440 | tf_op jit(solution)/shard_map/ppermute | solution.py:460
  19.4 2.5 %collective-permute-start.7 = (bf16[64,512]{1,0:T(8,128)(2,1)S(1)}, bf16[64,512]{1,0:T(8,128)(2,1)S(1)}, u32[]{:S(2)}, u32[]{:S(2)}) collective-permute-start(bf16[64,512]{1,0:T(8,128)(2,1)S(1)} %join.3.refs_0_), channel_id=1, source_target_pairs={{0,3},{1,2},{2,1},{3,0},{4,7},{5,6},{6,5},{7,4},{8,11},{9,10},{10,... | collective-permute-start | bytes 196616 | tf_op jit(solution)/shard_map/ppermute | solution.py:457
  22.0 3.4 %collective-permute-done.8.refs_4_.refs_9_ = bf16[4,64,512]{2,1,0:T(8,128)(2,1)S(1)} collective-permute-done((bf16[4,64,512]{2,1,0:T(8,128)(2,1)S(1)}, bf16[4,64,512]{2,1,0:T(8,128)(2,1)S(1)}, u32[]{:S(2)}, u32[]{:S(2)}) %collective-permute-start.8) | collective-permute-done | bytes 262176 | tf_op jit(solution)/shard_map/ppermute | solution.py:460
  26.5 2.0 %collective-permute-done.6.refs_2_ = bf16[64,512]{1,0:T(8,128)(2,1)S(1)} collective-permute-done((bf16[64,512]{1,0:T(8,128)(2,1)S(1)}, bf16[64,512]{1,0:T(8,128)(2,1)S(1)}, u32[]{:S(2)}, u32[]{:S(2)}) %collective-permute-start.6) | collective-permute-done | bytes 65568 | tf_op jit(solution)/shard_map/ppermute | solution.py:457
  29.9 2.5 %collective-permute-start.11 = (bf16[4,64,512]{2,1,0:T(8,128)(2,1)S(1)}, bf16[4,64,512]{2,1,0:T(8,128)(2,1)S(1)}, u32[]{:S(2)}, u32[]{:S(2)}) collective-permute-start(bf16[4,64,512]{2,1,0:T(8,128)(2,1)S(1)} %line.3.refs_10_.refs_6_), channel_id=1, source_target_pairs={{0,24},{4,28},{8,16},{12,20},{16,8},{20,12},{24,0},{28,4},{1,25},{... | collective-permute-start | bytes 786440 | tf_op jit(solution)/shard_map/ppermute | solution.py:460
  33.4 8.7 %attention.2 = (bf16[256,2048]{1,0:T(8,128)(2,1)}, bf16[256,2048]{1,0:T(8,128)(2,1)}, bf16[256,2048]{1,0:T(8,128)(2,1)}, bf16[256,2048]{1,0:T(8,128)(2,1)}, bf16...) custom-call(s32[2]{0:T(128)S(1)} %pad_add_fusion.place_ref.refs_0_, ...), custom_call_target="tpu_custom_call" | custom-call | flops 2013265920 | bytes 6291456 | tf_op jit(solution)/shard_map/attention/pallas_call | solution.py:263
  42.1 2.1 %collective-permute-done.10.refs_8_.refs_4_ = bf16[4,64,512]{2,1,0:T(8,128)(2,1)S(1)} collective-permute-done((bf16[4,64,512]{2,1,0:T(8,128)(2,1)S(1)}, bf16[4,64,512]{2,1,0:T(8,128)(2,1)S(1)}, u32[]{:S(2)}, u32[]{:S(2)}) %collective-permute-start.10) | collective-permute-done | bytes 262176 | tf_op jit(solution)/shard_map/ppermute | solution.py:460
  44.3 1.5 %collective-permute-start.14 = (bf16[4,64,512]{2,1,0:T(8,128)(2,1)S(1)}, bf16[4,64,512]{2,1,0:T(8,128)(2,1)S(1)}, u32[]{:S(2)}, u32[]{:S(2)}) collective-permute-start(bf16[4,64,512]{2,1,0:T(8,128)(2,1)S(1)} %get-tuple-element.66), channel_id=1, source_target_pairs={{0,8},{4,12},{8,0},{12,4},{16,24},{20,28},{24,16},{28,20},{1,9},{5... | collective-permute-start | bytes 786440 | tf_op jit(solution)/shard_map/ppermute | solution.py:460
  47.8 8.7 %attention.3 = (bf16[256,2048]{1,0:T(8,128)(2,1)}, bf16[256,2048]{1,0:T(8,128)(2,1)}, bf16[256,2048]{1,0:T(8,128)(2,1)}, bf16[256,2048]{1,0:T(8,128)(2,1)}, bf16...) custom-call(s32[2]{0:T(128)S(1)} %pad_add_fusion.place_ref.refs_0_, ...), custom_call_target="tpu_custom_call", output_to_operand_aliasing={{0}: (10, {}), {1}: (11, {}), {2}: (12, {}), {3}: (13, {}),... | custom-call | flops 2013265920 | bytes 6291456 | tf_op jit(solution)/shard_map/attention/pallas_call | solution.py:263
  56.5 2.8 %collective-permute-done.15.refs_2_ = bf16[4,64,512]{2,1,0:T(8,128)(2,1)S(1)} collective-permute-done((bf16[4,64,512]{2,1,0:T(8,128)(2,1)S(1)}, bf16[4,64,512]{2,1,0:T(8,128)(2,1)S(1)}, u32[]{:S(2)}, u32[]{:S(2)}) %collective-permute-start.15) | collective-permute-done | bytes 262176 | tf_op jit(solution)/shard_map/ppermute | solution.py:460
  60.0 1.5 %collective-permute-start.18 = (bf16[4,64,512]{2,1,0:T(8,128)(2,1)S(1)}, bf16[4,64,512]{2,1,0:T(8,128)(2,1)S(1)}, u32[]{:S(2)}, u32[]{:S(2)}) collective-permute-start(bf16[4,64,512]{2,1,0:T(8,128)(2,1)S(1)} %get-tuple-element.72), channel_id=1, source_target_pairs={{0,16},{4,20},{8,24},{12,28},{16,0},{20,4},{24,8},{28,12},{1,17},{... | collective-permute-start | bytes 786440 | tf_op jit(solution)/shard_map/ppermute | solution.py:460
  61.5 1.4 %collective-permute-start.19 = (bf16[4,64,512]{2,1,0:T(8,128)(2,1)S(1)}, bf16[4,64,512]{2,1,0:T(8,128)(2,1)S(1)}, u32[]{:S(2)}, u32[]{:S(2)}) collective-permute-start(bf16[4,64,512]{2,1,0:T(8,128)(2,1)S(1)} %get-tuple-element.73), channel_id=1, source_target_pairs={{0,24},{4,28},{8,16},{12,20},{16,8},{20,12},{24,0},{28,4},{1,25},{... | collective-permute-start | bytes 786440 | tf_op jit(solution)/shard_map/ppermute | solution.py:460
  63.0 2.6 %collective-permute-start.21 = (bf16[64,512]{1,0:T(8,128)(2,1)S(1)}, bf16[64,512]{1,0:T(8,128)(2,1)S(1)}, u32[]{:S(2)}, u32[]{:S(2)}) collective-permute-start(bf16[64,512]{1,0:T(8,128)(2,1)S(1)} %get-tuple-element.75), channel_id=1, source_target_pairs={{0,2},{1,3},{2,0},{3,1},{4,6},{5,7},{6,4},{7,5},{8,10},{9,11},{10,... | collective-permute-start | bytes 196616 | tf_op jit(solution)/shard_map/ppermute | solution.py:457
  65.6 1.6 %collective-permute-done.20.refs_4_.refs_2_ = bf16[64,512]{1,0:T(8,128)(2,1)S(1)} collective-permute-done((bf16[64,512]{1,0:T(8,128)(2,1)S(1)}, bf16[64,512]{1,0:T(8,128)(2,1)S(1)}, u32[]{:S(2)}, u32[]{:S(2)}) %collective-permute-start.20) | collective-permute-done | bytes 65568 | tf_op jit(solution)/shard_map/ppermute | solution.py:457
  67.2 2.1 %collective-permute-start.22 = (bf16[64,512]{1,0:T(8,128)(2,1)S(1)}, bf16[64,512]{1,0:T(8,128)(2,1)S(1)}, u32[]{:S(2)}, u32[]{:S(2)}) collective-permute-start(bf16[64,512]{1,0:T(8,128)(2,1)S(1)} %get-tuple-element.76), channel_id=1, source_target_pairs={{0,3},{1,2},{2,1},{3,0},{4,7},{5,6},{6,5},{7,4},{8,11},{9,10},{10,... | collective-permute-start | bytes 196616 | tf_op jit(solution)/shard_map/ppermute | solution.py:457
  69.3 4.0 %collective-permute-done.22.refs_6_.refs_4_ = bf16[64,512]{1,0:T(8,128)(2,1)S(1)} collective-permute-done((bf16[64,512]{1,0:T(8,128)(2,1)S(1)}, bf16[64,512]{1,0:T(8,128)(2,1)S(1)}, u32[]{:S(2)}, u32[]{:S(2)}) %collective-permute-start.22) | collective-permute-done | bytes 65568 | tf_op jit(solution)/shard_map/ppermute | solution.py:457
  73.6 2.6 %collective-permute-start.25 = (bf16[64,512]{1,0:T(8,128)(2,1)S(1)}, bf16[64,512]{1,0:T(8,128)(2,1)S(1)}, u32[]{:S(2)}, u32[]{:S(2)}) collective-permute-start(bf16[64,512]{1,0:T(8,128)(2,1)S(1)} %get-tuple-element.88), channel_id=1, source_target_pairs={{0,2},{1,3},{2,0},{3,1},{4,6},{5,7},{6,4},{7,5},{8,10},{9,11},{10,... | collective-permute-start | bytes 196616 | tf_op jit(solution)/shard_map/ppermute | solution.py:457
  76.2 1.8 %collective-permute-start.26 = (bf16[64,512]{1,0:T(8,128)(2,1)S(1)}, bf16[64,512]{1,0:T(8,128)(2,1)S(1)}, u32[]{:S(2)}, u32[]{:S(2)}) collective-permute-start(bf16[64,512]{1,0:T(8,128)(2,1)S(1)} %get-tuple-element.89), channel_id=1, source_target_pairs={{0,3},{1,2},{2,1},{3,0},{4,7},{5,6},{6,5},{7,4},{8,11},{9,10},{10,... | collective-permute-start | bytes 196616 | tf_op jit(solution)/shard_map/ppermute | solution.py:457
  79.1 2.4 %collective-permute-done.25.refs_8_ = bf16[64,512]{1,0:T(8,128)(2,1)S(1)} collective-permute-done((bf16[64,512]{1,0:T(8,128)(2,1)S(1)}, bf16[64,512]{1,0:T(8,128)(2,1)S(1)}, u32[]{:S(2)}, u32[]{:S(2)}) %collective-permute-start.25) | collective-permute-done | bytes 65568 | tf_op jit(solution)/shard_map/ppermute | solution.py:457
  82.5 1.9 %settle.1 = (bf16[256,2048]{1,0:T(8,128)(2,1)}, bf16[256,2048]{1,0:T(8,128)(2,1)}, bf16[256,2048]{1,0:T(8,128)(2,1)}, bf16[256,2048]{1,0:T(8,128)(2,1)}) custom-call(s32[2]{0:T(128)S(1)} %pad_add_fusion.place_ref.refs_0_, ...), custom_call_target="tpu_custom_call", output_to_operand_aliasing={{0}: (2, {}), {1}: (3, {}), {2}: (4, {}), {3}: (5, {})} | custom-call | tf_op jit(solution)/shard_map/settle/pallas_call | solution.py:400
  (49 shorter events, 13.9 us)
Async XLA Ops:
  4.4 7.6 %collective-permute-start.3 = (bf16[64,512]{1,0:T(8,128)(2,1)S(1)}, bf16[64,512]{1,0:T(8,128)(2,1)S(1)}, u32[]{:S(2)}, u32[]{:S(2)}) collective-permute-start(bf16[64,512]{1,0:T(8,128)(2,1)S(1)} %join.2.refs_0_), channel_id=1, source_target_pairs={{0,3},{1,2},{2,1},{3,0},{4,7},{5,6},{6,5},{7,4},{8,11},{9,10},{10,... | collective-permute-start | bytes 196616 | tf_op jit(solution)/shard_map/ppermute | solution.py:457
  9.3 5.9 %collective-permute-start.2 = (bf16[64,512]{1,0:T(8,128)(2,1)S(1)}, bf16[64,512]{1,0:T(8,128)(2,1)S(1)}, u32[]{:S(2)}, u32[]{:S(2)}) collective-permute-start(bf16[64,512]{1,0:T(8,128)(2,1)S(1)} %join.2.refs_0_), channel_id=1, source_target_pairs={{0,2},{1,3},{2,0},{3,1},{4,6},{5,7},{6,4},{7,5},{8,10},{9,11},{10,... | collective-permute-start | bytes 196616 | tf_op jit(solution)/shard_map/ppermute | solution.py:457
  9.3 5.9 %collective-permute-start.1 = (bf16[64,512]{1,0:T(8,128)(2,1)S(1)}, bf16[64,512]{1,0:T(8,128)(2,1)S(1)}, u32[]{:S(2)}, u32[]{:S(2)}) collective-permute-start(bf16[64,512]{1,0:T(8,128)(2,1)S(1)} %join.2.refs_0_), channel_id=1, source_target_pairs={{0,1},{1,0},{2,3},{3,2},{4,5},{5,4},{6,7},{7,6},{8,9},{9,8},{10,11... | collective-permute-start | bytes 196616 | tf_op jit(solution)/shard_map/ppermute | solution.py:457
  15.3 10.1 %collective-permute-start.8 = (bf16[4,64,512]{2,1,0:T(8,128)(2,1)S(1)}, bf16[4,64,512]{2,1,0:T(8,128)(2,1)S(1)}, u32[]{:S(2)}, u32[]{:S(2)}) collective-permute-start(bf16[4,64,512]{2,1,0:T(8,128)(2,1)S(1)} %line.2.refs_6_), channel_id=1, source_target_pairs={{0,24},{4,28},{8,16},{12,20},{16,8},{20,12},{24,0},{28,4},{1,25},{... | collective-permute-start | bytes 786440 | tf_op jit(solution)/shard_map/ppermute | solution.py:460
  17.8 15.6 %collective-permute-start.13 = (bf16[4,64,512]{2,1,0:T(8,128)(2,1)S(1)}, bf16[4,64,512]{2,1,0:T(8,128)(2,1)S(1)}, u32[]{:S(2)}, u32[]{:S(2)}) collective-permute-start(bf16[4,64,512]{2,1,0:T(8,128)(2,1)S(1)} %line.2.refs_6_), channel_id=1, source_target_pairs={{0,16},{4,20},{8,24},{12,28},{16,0},{20,4},{24,8},{28,12},{1,17},{... | collective-permute-start | bytes 786440 | tf_op jit(solution)/shard_map/ppermute | solution.py:460
  18.3 15.1 %collective-permute-start.12 = (bf16[4,64,512]{2,1,0:T(8,128)(2,1)S(1)}, bf16[4,64,512]{2,1,0:T(8,128)(2,1)S(1)}, u32[]{:S(2)}, u32[]{:S(2)}) collective-permute-start(bf16[4,64,512]{2,1,0:T(8,128)(2,1)S(1)} %line.2.refs_6_), channel_id=1, source_target_pairs={{0,8},{4,12},{8,0},{12,4},{16,24},{20,28},{24,16},{28,20},{1,9},{5... | collective-permute-start | bytes 786440 | tf_op jit(solution)/shard_map/ppermute | solution.py:460
  19.4 7.1 %collective-permute-start.7 = (bf16[64,512]{1,0:T(8,128)(2,1)S(1)}, bf16[64,512]{1,0:T(8,128)(2,1)S(1)}, u32[]{:S(2)}, u32[]{:S(2)}) collective-permute-start(bf16[64,512]{1,0:T(8,128)(2,1)S(1)} %join.3.refs_0_), channel_id=1, source_target_pairs={{0,3},{1,2},{2,1},{3,0},{4,7},{5,6},{6,5},{7,4},{8,11},{9,10},{10,... | collective-permute-start | bytes 196616 | tf_op jit(solution)/shard_map/ppermute | solution.py:457
  21.9 6.7 %collective-permute-start.6 = (bf16[64,512]{1,0:T(8,128)(2,1)S(1)}, bf16[64,512]{1,0:T(8,128)(2,1)S(1)}, u32[]{:S(2)}, u32[]{:S(2)}) collective-permute-start(bf16[64,512]{1,0:T(8,128)(2,1)S(1)} %join.3.refs_0_), channel_id=1, source_target_pairs={{0,2},{1,3},{2,0},{3,1},{4,6},{5,7},{6,4},{7,5},{8,10},{9,11},{10,... | collective-permute-start | bytes 196616 | tf_op jit(solution)/shard_map/ppermute | solution.py:457
  25.4 4.5 %collective-permute-start.5 = (bf16[64,512]{1,0:T(8,128)(2,1)S(1)}, bf16[64,512]{1,0:T(8,128)(2,1)S(1)}, u32[]{:S(2)}, u32[]{:S(2)}) collective-permute-start(bf16[64,512]{1,0:T(8,128)(2,1)S(1)} %join.3.refs_0_), channel_id=1, source_target_pairs={{0,1},{1,0},{2,3},{3,2},{4,5},{5,4},{6,7},{7,6},{8,9},{9,8},{10,11... | collective-permute-start | bytes 196616 | tf_op jit(solution)/shard_map/ppermute | solution.py:457
  29.9 12.2 %collective-permute-start.11 = (bf16[4,64,512]{2,1,0:T(8,128)(2,1)S(1)}, bf16[4,64,512]{2,1,0:T(8,128)(2,1)S(1)}, u32[]{:S(2)}, u32[]{:S(2)}) collective-permute-start(bf16[4,64,512]{2,1,0:T(8,128)(2,1)S(1)} %line.3.refs_10_.refs_6_), channel_id=1, source_target_pairs={{0,24},{4,28},{8,16},{12,20},{16,8},{20,12},{24,0},{28,4},{1,25},{... | collective-permute-start | bytes 786440 | tf_op jit(solution)/shard_map/ppermute | solution.py:460
  32.4 11.8 %collective-permute-start.10 = (bf16[4,64,512]{2,1,0:T(8,128)(2,1)S(1)}, bf16[4,64,512]{2,1,0:T(8,128)(2,1)S(1)}, u32[]{:S(2)}, u32[]{:S(2)}) collective-permute-start(bf16[4,64,512]{2,1,0:T(8,128)(2,1)S(1)} %line.3.refs_10_.refs_6_), channel_id=1, source_target_pairs={{0,16},{4,20},{8,24},{12,28},{16,0},{20,4},{24,8},{28,12},{1,17},{... | collective-permute-start | bytes 786440 | tf_op jit(solution)/shard_map/ppermute | solution.py:460
  32.9 11.4 %collective-permute-start.9 = (bf16[4,64,512]{2,1,0:T(8,128)(2,1)S(1)}, bf16[4,64,512]{2,1,0:T(8,128)(2,1)S(1)}, u32[]{:S(2)}, u32[]{:S(2)}) collective-permute-start(bf16[4,64,512]{2,1,0:T(8,128)(2,1)S(1)} %line.3.refs_10_.refs_6_), channel_id=1, source_target_pairs={{0,8},{4,12},{8,0},{12,4},{16,24},{20,28},{24,16},{28,20},{1,9},{5... | collective-permute-start | bytes 786440 | tf_op jit(solution)/shard_map/ppermute | solution.py:460
  44.3 12.2 %collective-permute-start.14 = (bf16[4,64,512]{2,1,0:T(8,128)(2,1)S(1)}, bf16[4,64,512]{2,1,0:T(8,128)(2,1)S(1)}, u32[]{:S(2)}, u32[]{:S(2)}) collective-permute-start(bf16[4,64,512]{2,1,0:T(8,128)(2,1)S(1)} %get-tuple-element.66), channel_id=1, source_target_pairs={{0,8},{4,12},{8,0},{12,4},{16,24},{20,28},{24,16},{28,20},{1,9},{5... | collective-permute-start | bytes 786440 | tf_op jit(solution)/shard_map/ppermute | solution.py:460
  45.8 13.5 %collective-permute-start.15 = (bf16[4,64,512]{2,1,0:T(8,128)(2,1)S(1)}, bf16[4,64,512]{2,1,0:T(8,128)(2,1)S(1)}, u32[]{:S(2)}, u32[]{:S(2)}) collective-permute-start(bf16[4,64,512]{2,1,0:T(8,128)(2,1)S(1)} %get-tuple-element.67), channel_id=1, source_target_pairs={{0,16},{4,20},{8,24},{12,28},{16,0},{20,4},{24,8},{28,12},{1,17},{... | collective-permute-start | bytes 786440 | tf_op jit(solution)/shard_map/ppermute | solution.py:460
  46.5 12.7 %collective-permute-start.16 = (bf16[4,64,512]{2,1,0:T(8,128)(2,1)S(1)}, bf16[4,64,512]{2,1,0:T(8,128)(2,1)S(1)}, u32[]{:S(2)}, u32[]{:S(2)}) collective-permute-start(bf16[4,64,512]{2,1,0:T(8,128)(2,1)S(1)} %get-tuple-element.68), channel_id=1, source_target_pairs={{0,24},{4,28},{8,16},{12,20},{16,8},{20,12},{24,0},{28,4},{1,25},{... | collective-permute-start | bytes 786440 | tf_op jit(solution)/shard_map/ppermute | solution.py:460
  59.4 13.9 %collective-permute-start.17 = (bf16[4,64,512]{2,1,0:T(8,128)(2,1)S(1)}, bf16[4,64,512]{2,1,0:T(8,128)(2,1)S(1)}, u32[]{:S(2)}, u32[]{:S(2)}) collective-permute-start(bf16[4,64,512]{2,1,0:T(8,128)(2,1)S(1)} %get-tuple-element.71), channel_id=1, source_target_pairs={{0,8},{4,12},{8,0},{12,4},{16,24},{20,28},{24,16},{28,20},{1,9},{5... | collective-permute-start | bytes 786440 | tf_op jit(solution)/shard_map/ppermute | solution.py:460
  60.0 13.3 %collective-permute-start.18 = (bf16[4,64,512]{2,1,0:T(8,128)(2,1)S(1)}, bf16[4,64,512]{2,1,0:T(8,128)(2,1)S(1)}, u32[]{:S(2)}, u32[]{:S(2)}) collective-permute-start(bf16[4,64,512]{2,1,0:T(8,128)(2,1)S(1)} %get-tuple-element.72), channel_id=1, source_target_pairs={{0,16},{4,20},{8,24},{12,28},{16,0},{20,4},{24,8},{28,12},{1,17},{... | collective-permute-start | bytes 786440 | tf_op jit(solution)/shard_map/ppermute | solution.py:460
  61.5 11.8 %collective-permute-start.19 = (bf16[4,64,512]{2,1,0:T(8,128)(2,1)S(1)}, bf16[4,64,512]{2,1,0:T(8,128)(2,1)S(1)}, u32[]{:S(2)}, u32[]{:S(2)}) collective-permute-start(bf16[4,64,512]{2,1,0:T(8,128)(2,1)S(1)} %get-tuple-element.73), channel_id=1, source_target_pairs={{0,24},{4,28},{8,16},{12,20},{16,8},{20,12},{24,0},{28,4},{1,25},{... | collective-permute-start | bytes 786440 | tf_op jit(solution)/shard_map/ppermute | solution.py:460
  63.0 6.3 %collective-permute-start.21 = (bf16[64,512]{1,0:T(8,128)(2,1)S(1)}, bf16[64,512]{1,0:T(8,128)(2,1)S(1)}, u32[]{:S(2)}, u32[]{:S(2)}) collective-permute-start(bf16[64,512]{1,0:T(8,128)(2,1)S(1)} %get-tuple-element.75), channel_id=1, source_target_pairs={{0,2},{1,3},{2,0},{3,1},{4,6},{5,7},{6,4},{7,5},{8,10},{9,11},{10,... | collective-permute-start | bytes 196616 | tf_op jit(solution)/shard_map/ppermute | solution.py:457
  67.2 6.1 %collective-permute-start.22 = (bf16[64,512]{1,0:T(8,128)(2,1)S(1)}, bf16[64,512]{1,0:T(8,128)(2,1)S(1)}, u32[]{:S(2)}, u32[]{:S(2)}) collective-permute-start(bf16[64,512]{1,0:T(8,128)(2,1)S(1)} %get-tuple-element.76), channel_id=1, source_target_pairs={{0,3},{1,2},{2,1},{3,0},{4,7},{5,6},{6,5},{7,4},{8,11},{9,10},{10,... | collective-permute-start | bytes 196616 | tf_op jit(solution)/shard_map/ppermute | solution.py:457
  73.5 9.1 %collective-permute-start.23 = (bf16[4,256,1024]{2,1,0:T(8,128)(2,1)S(1)}, bf16[4,256,1024]{2,1,0:T(8,128)(2,1)S(1)}, u32[]{:S(2)}, u32[]{:S(2)}) collective-permute-start(bf16[4,256,1024]{2,1,0:T(8,128)(2,1)S(1)} %hold.7), channel_id=1, source_target_pairs={{0,4},{4,0},{8,12},{12,8},{16,20},{20,16},{24,28},{28,24},{1,5},{5... | collective-permute-start | bytes 6291464 | tf_op jit(solution)/shard_map/ppermute | solution.py:460
  73.5 5.6 %collective-permute-start.24 = (bf16[64,512]{1,0:T(8,128)(2,1)S(1)}, bf16[64,512]{1,0:T(8,128)(2,1)S(1)}, u32[]{:S(2)}, u32[]{:S(2)}) collective-permute-start(bf16[64,512]{1,0:T(8,128)(2,1)S(1)} %get-tuple-element.87), channel_id=1, source_target_pairs={{0,1},{1,0},{2,3},{3,2},{4,5},{5,4},{6,7},{7,6},{8,9},{9,8},{10,11... | collective-permute-start | bytes 196616 | tf_op jit(solution)/shard_map/ppermute | solution.py:457
  73.6 8.0 %collective-permute-start.25 = (bf16[64,512]{1,0:T(8,128)(2,1)S(1)}, bf16[64,512]{1,0:T(8,128)(2,1)S(1)}, u32[]{:S(2)}, u32[]{:S(2)}) collective-permute-start(bf16[64,512]{1,0:T(8,128)(2,1)S(1)} %get-tuple-element.88), channel_id=1, source_target_pairs={{0,2},{1,3},{2,0},{3,1},{4,6},{5,7},{6,4},{7,5},{8,10},{9,11},{10,... | collective-permute-start | bytes 196616 | tf_op jit(solution)/shard_map/ppermute | solution.py:457
  76.2 6.1 %collective-permute-start.26 = (bf16[64,512]{1,0:T(8,128)(2,1)S(1)}, bf16[64,512]{1,0:T(8,128)(2,1)S(1)}, u32[]{:S(2)}, u32[]{:S(2)}) collective-permute-start(bf16[64,512]{1,0:T(8,128)(2,1)S(1)} %get-tuple-element.89), channel_id=1, source_target_pairs={{0,3},{1,2},{2,1},{3,0},{4,7},{5,6},{6,5},{7,4},{8,11},{9,10},{10,... | collective-permute-start | bytes 196616 | tf_op jit(solution)/shard_map/ppermute | solution.py:457
  (4 other events, 11.8 us)

commit v4 on v3

--- a/solution.py
+++ b/solution.py
@@ -304,58 +304,69 @@
     )(*arrays, *after)
 
 
-def line_body(n_in, *refs):
-    for j in range(n_in):
-        refs[-1][j] = refs[j][...]
-
-
-def stack_line(pieces, *after):
-    return pl.pallas_call(
-        functools.partial(line_body, len(pieces)),
-        in_specs=[in_vmem] * (len(pieces) + len(after)),
+def line_body(at, n_far, own_ref, pair_ref, *refs):
+    line_ref = refs[-1]
+    line_ref[0] = own_ref[...]
+    line_ref[1] = pair_ref[:, at : at + own_ref.shape[1]]
+    for j in range(n_far):
+        line_ref[2 + j] = refs[j][...]
+
+
+def stack_line(own, pair, far, at, *after):
+    return pl.pallas_call(
+        functools.partial(line_body, at, len(far)),
+        in_specs=[in_vmem] * (2 + len(far) + len(after)),
         out_specs=in_vmem,
-        out_shape=jax.ShapeDtypeStruct((len(pieces),) + pieces[0].shape, pieces[0].dtype),
+        out_shape=jax.ShapeDtypeStruct((2 + len(far),) + own.shape, own.dtype),
         compiler_params=params,
         name="line",
-    )(*pieces, *after)
-
-
-def column_sum_body(n_in, n_after, *refs):
-    in_refs, out_refs = refs[:n_in], refs[n_in + n_after :]
+    )(own, pair, *far, *after)
+
+
+def column_sum_body(n_in, n_pairs, n_after, *refs):
+    in_refs, pair_refs = refs[:n_in], refs[n_in : n_in + n_pairs]
+    out_refs = refs[n_in + n_pairs + n_after :]
     for j, ref in enumerate(out_refs):
         total = in_refs[0][j].astype(jnp.float32)
         for came in in_refs[1:]:
             total = total + came[j].astype(jnp.float32)
-        ref[...] = total.astype(ref.dtype)
-
-
-def column_sum(parts, *after):
-    nz = parts[0].shape[0]
+        at = 0
+        if j == 1:
+            for pair in pair_refs:
+                ref[:, at : at + pair.shape[1]] = pair[...]
+                at += pair.shape[1]
+        ref[:, at : at + total.shape[1]] = total.astype(ref.dtype)
+
+
+def column_sum(parts, pairs, *after):
+    nz, rows, width = parts[0].shape
     shapes = [
-        jax.ShapeDtypeStruct(parts[0].shape[1:], jnp.float32 if j == 0 else jnp.bfloat16)
+        jax.ShapeDtypeStruct((rows, width), jnp.float32 if j == 0 else jnp.bfloat16)
         for j in range(nz)
     ]
-    return pl.pallas_call(
-        functools.partial(column_sum_body, len(parts), len(after)),
-        in_specs=[in_vmem] * (len(parts) + len(after)),
+    wide = width + sum(pair.shape[1] for pair in pairs)
+    shapes[1] = jax.ShapeDtypeStruct((rows, wide), jnp.bfloat16)
+    return pl.pallas_call(
+        functools.partial(column_sum_body, len(parts), len(pairs), len(after)),
+        in_specs=[in_vmem] * (len(parts) + len(pairs) + len(after)),
         out_specs=[in_vmem] * nz,
         out_shape=shapes,
         compiler_params=params,
         name="column_sum",
-    )(*parts, *after)
-
-
-def edge_body(n_terms, *refs):
-    terms, targets = refs[:-2], refs[-2:]
+    )(*parts, *pairs, *after)
+
+
+def edge_body(n_chunks, n_terms, pair_ref, *refs):
+    terms, targets = refs[: n_chunks * n_terms], refs[-2:]
     at = 0
     for c in range(0, len(terms), n_terms):
         near_ref, *ends = terms[c : c + n_terms]
-        total = ends[0][...]
+        to = slice(at, at + near_ref.shape[2])
+        at += near_ref.shape[2]
+        total = ends[0][...] + pair_ref[:, to].astype(jnp.float32)
         for term in ends[1:]:
             total = total + term[...].astype(jnp.float32)
         rows = total.shape[0] // 2
-        to = slice(at, at + total.shape[1])
-        at += total.shape[1]
         for t, target in enumerate(targets):
             for n in range(rows // SUMMARY):
                 tile = near_ref[t, n * EDGE : (n + 1) * EDGE, :]
@@ -365,22 +376,24 @@
                 target[n * EDGE : (n + 1) * EDGE, to] = tile
 
 
-def edge(chunks):
+def edge(pair, chunks, *after):
     width = sum(chunk[0].shape[2] for chunk in chunks)
     shape = jax.ShapeDtypeStruct((chunks[0][0].shape[1], width), jnp.bfloat16)
-    return pl.pallas_call(
-        functools.partial(edge_body, len(chunks[0])),
-        in_specs=[in_vmem] * (len(chunks) * len(chunks[0])),
+    terms = [term for chunk in chunks for term in chunk]
+    return pl.pallas_call(
+        functools.partial(edge_body, len(chunks), len(chunks[0])),
+        in_specs=[in_vmem] * (1 + len(terms) + len(after)),
         out_specs=[in_vmem] * 2,
         out_shape=[shape] * 2,
         compiler_params=params,
         name="edge",
-    )(*[term for chunk in chunks for term in chunk])
+    )(pair, *terms, *after)
 
 
 def settle_body(n_came, place_ref, *refs):
     came_refs, targets = refs[:n_came], refs[n_came + 4 : n_came + 8]
-    sem = refs[n_came + 8]
+    token_ref, sem = refs[n_came + 8 :]
+    token_ref[...] = jnp.zeros(token_ref.shape, token_ref.dtype)
     width = targets[0].shape[1]
     copies = []
     at = 0
@@ -400,8 +413,9 @@
     return pl.pallas_call(
         functools.partial(settle_body, n),
         in_specs=[in_smem] + [in_vmem] * n + [in_hbm] * 4,
-        out_specs=[in_hbm] * 4,
-        out_shape=[jax.ShapeDtypeStruct(x.shape, x.dtype) for x in results],
+        out_specs=[in_hbm] * 4 + [in_vmem],
+        out_shape=[jax.ShapeDtypeStruct(x.shape, x.dtype) for x in results]
+        + [jax.ShapeDtypeStruct((8, 128), jnp.float32)],
         scratch_shapes=[pltpu.SemaphoreType.DMA((n, 4))],
         input_output_aliases={1 + n + i: i for i in range(4)},
         compiler_params=params,
@@ -459,8 +473,8 @@
     def over_seq(array, bits):
         return lax.ppermute(array, "seq", [(i, i ^ bits) for i in range(n_seq)])
 
-    def swap_z(pieces):
-        return [over_z(pieces[j], j) for j in reversed(range(1, nz))][::-1]
+    def swap_far(pieces):
+        return [over_z(pieces[j], j) for j in reversed(range(2, nz))][::-1]
 
     def swap_columns(parts):
         return [over_seq(parts[c], 2 * c) for c in reversed(range(1, n_cols))][::-1]
@@ -469,19 +483,19 @@
     arrays = (queries, keys_in, values_in, cotangent)
     mine, other, part = pack(place, arrays)
     came = over_seq(other, 1)
+    pair = over_z(join(mine, came, 0, mine.shape[1]), 1)
     columns = []
-    theirs = None
+    theirs = over_seq(hold([part], came)[0], 1)
     for c in range(n_chunks):
         width = chunk_heads[c] * HEAD_DIM
-        start = join(mine, came, firsts[c] * HEAD_DIM, width, *([theirs] if c else []))
-        pieces = [start] + swap_z([start] * nz)
-        if c == 0:
-            theirs = over_seq(hold([part], *pieces[1:])[0], 1)
-        line = stack_line(pieces, *[cols[-1] for cols in columns[-1:]])
+        at = firsts[c] * HEAD_DIM
+        own = join(mine, came, at, width, *[cols[0] for cols in columns[-1:]])
+        far = swap_far([own] * nz)
+        line = stack_line(own, pair, far, at, *([cols[-1] for cols in columns[-1:]] or [theirs]))
         columns.append([line] + swap_columns([line] * n_cols))
 
     results = ()
-    chunks = []
+    chunks, pairs = [], []
     back = None
     for c in range(n_chunks):
         made = attention(
@@ -495,20 +509,23 @@
             chunk_heads[c],
         )
         results, near, parts = made[:5], made[5], list(made[6:])
-        waits = columns[c + 1][1:] if c + 1 < n_chunks else []
+        waits = columns[c + 1] if c + 1 < n_chunks else [None] * n_cols
         if back is not None:
-            ends = column_sum(back[1], near)
-            waits = waits + list(ends[:1])
-        moved = swap_columns(parts[:1] + list(hold(parts[1:], *waits)))
+            waits = back[1]
+        moved = [hold([parts[i]], waits[i])[0] for i in range(1, n_cols)]
+        moved = swap_columns(parts[:1] + moved)
         if back is not None:
-            chunks.append([back[0], ends[0]] + swap_z(ends))
+            ends = column_sum(back[1], [], near)
+            pairs.append(ends[1])
+            chunks.append([back[0], ends[0]] + swap_far(ends))
         back = near, parts[:1] + moved
-    ends = column_sum(back[1], *chunks[-1][2:])
-    chunks.append([back[0], ends[0]] + swap_z(ends))
+    ends = column_sum(back[1], pairs, *chunks[-1][2:])
+    pair = over_z(ends[1], 1)
+    chunks.append([back[0], ends[0]] + swap_far(ends))
     *results, sent = results
     (sent,) = hold([sent], ends[0])
-    results = settle(place, [over_seq(sent, 1)], results)
-    own, away = edge(chunks)
+    *results, mark = settle(place, [over_seq(sent, 1)], results)
+    own, away = edge(pair, chunks, mark)
     attended, grad_queries, dk, dv = results
     edges = [own, over_seq(away, 1)]
     grad_keys, grad_values = finish(place, dk, dv, edges)

time: 86 us -> 79.8 us (0.928)
  starting transfers between devices: 33.2 us -> 29.7 us
  waiting for transfers between devices: 28.5 us -> 25.9 us
    ppermute x12 -> x10, starting transfers between devices: 18.4 us -> 14.3 us  [over_z(): return lax.ppermute(array, 'head', [(i, i ^ bits) for i in range(nz)])]
    ppermute x16, waiting for transfers between devices: 9.87 us -> 5.94 us  [over_seq(): return lax.ppermute(array, 'seq', [(i, i ^ bits) for i in range(n_seq)])]
    ppermute x12 -> x10, waiting for transfers between devices: 18.6 us -> 19.9 us  [over_z(): return lax.ppermute(array, 'head', [(i, i ^ bits) for i in range(nz)])]
  transfers between devices with their start and end apart: 28 -> 26, of which waited for: 15 -> 13; matrix products, arithmetic and copies ran while one was open for 0% -> 0% of each run, Pallas kernels for 23% -> 24%
where the time goes in v4:
time: 79.8 us; the launch traced here: 79.6 us
  starting transfers between devices  29.7 us (37%)
  waiting for transfers between devices  25.9 us (32%)
  Pallas kernels  23.2 us (29%)
    ppermute x10, waiting for transfers between devices, over_z(): return lax.ppermute(array, 'head', [(i, i ^ bits) for i in range(nz)])  19.9 us
    pallas_call x2, Pallas kernels, attention(): pl.pallas_call(functools.partial(attention_body, n_sum, n_cols, n_skip, f...  17.3 us
    ppermute x16, starting transfers between devices, over_seq(): return lax.ppermute(array, 'seq', [(i, i ^ bits) for i in range(n_seq)])  15.4 us
    ppermute x10, starting transfers between devices, over_z(): return lax.ppermute(array, 'head', [(i, i ^ bits) for i in range(nz)])  14.3 us
    ppermute x16, waiting for transfers between devices, over_seq(): return lax.ppermute(array, 'seq', [(i, i ^ bits) for i in range(n_seq)])  5.94 us
    pallas_call x1, Pallas kernels, pack(): pl.pallas_call(pack_body, in_specs=[in_smem] + [in_hbm] * 4, out_specs=[i...  2.24 us
    pallas_call x1, Pallas kernels, settle(): pl.pallas_call(functools.partial(settle_body, n), in_specs=[in_smem] + [i...  1.89 us
  transfers between devices with their start and end apart: 26, of which 13 were waited for; matrix products, arithmetic and copies ran while one was open for 0% of the time, Pallas kernels for 24%

profile of v4, /device:TPU:0, one launch (start us, length us, event | category | flops | bytes accessed | tf_op | source)
XLA Modules:
  0.0 79.6 jit_solution(3579324612834451092)
XLA Ops:
  0.7 2.2 %pack.1 = (bf16[32,1024]{1,0:T(8,128)(2,1)S(1)}, bf16[32,1024]{1,0:T(8,128)(2,1)S(1)}, bf16[4,256,1024]{2,1,0:T(8,128)(2,1)S(1)}) custom-call(s32[2]{0:T(128)S(1)} %pad_add_fusion.place_ref.refs_0_, bf16[256,2048]{1,0:T(8,128)(2,1)} %refs_1_.5, bf16[256,2048]{1,0:T(8,128)(2,1)} %refs_2_.5, bf16[256,2048]{1,0:T(8,128)(2,1)} %refs_3_.5, bf16[256,2048]{1,0:T(8,128)(2,1)} %refs_4_.3), custom_call_target="tpu_custom_call" | custom-call | tf_op jit(solution)/shard_map/pack/pallas_call | solution.py:92
  4.7 2.8 %collective-permute-start.2 = (bf16[64,1024]{1,0:T(8,128)(2,1)S(1)}, bf16[64,1024]{1,0:T(8,128)(2,1)S(1)}, u32[]{:S(2)}, u32[]{:S(2)}) collective-permute-start(bf16[64,1024]{1,0:T(8,128)(2,1)S(1)} %join.4), channel_id=1, source_target_pairs={{0,1},{1,0},{2,3},{3,2},{4,5},{5,4},{6,7},{7,6},{8,9},{9,8},{10,11... | collective-permute-start | bytes 393224 | tf_op jit(solution)/shard_map/ppermute | solution.py:471
  7.5 2.5 %collective-permute-start.4 = (bf16[64,512]{1,0:T(8,128)(2,1)S(1)}, bf16[64,512]{1,0:T(8,128)(2,1)S(1)}, u32[]{:S(2)}, u32[]{:S(2)}) collective-permute-start(bf16[64,512]{1,0:T(8,128)(2,1)S(1)} %join.3.own_ref), channel_id=1, source_target_pairs={{0,3},{1,2},{2,1},{3,0},{4,7},{5,6},{6,5},{7,4},{8,11},{9,10},{10,... | collective-permute-start | bytes 196616 | tf_op jit(solution)/shard_map/ppermute | solution.py:471
  10.2 5.6 %collective-permute-done.4.refs_1_ = bf16[64,512]{1,0:T(8,128)(2,1)S(1)} collective-permute-done((bf16[64,512]{1,0:T(8,128)(2,1)S(1)}, bf16[64,512]{1,0:T(8,128)(2,1)S(1)}, u32[]{:S(2)}, u32[]{:S(2)}) %collective-permute-start.4) | collective-permute-done | bytes 65568 | tf_op jit(solution)/shard_map/ppermute | solution.py:471
  15.8 1.7 %collective-permute-done.3.refs_0_ = bf16[64,512]{1,0:T(8,128)(2,1)S(1)} collective-permute-done((bf16[64,512]{1,0:T(8,128)(2,1)S(1)}, bf16[64,512]{1,0:T(8,128)(2,1)S(1)}, u32[]{:S(2)}, u32[]{:S(2)}) %collective-permute-start.3) | collective-permute-done | bytes 65568 | tf_op jit(solution)/shard_map/ppermute | solution.py:471
  17.5 2.5 %collective-permute-start.7 = (bf16[4,64,512]{2,1,0:T(8,128)(2,1)S(1)}, bf16[4,64,512]{2,1,0:T(8,128)(2,1)S(1)}, u32[]{:S(2)}, u32[]{:S(2)}) collective-permute-start(bf16[4,64,512]{2,1,0:T(8,128)(2,1)S(1)} %line.2.refs_0_.refs_6_), channel_id=1, source_target_pairs={{0,24},{4,28},{8,16},{12,20},{16,8},{20,12},{24,0},{28,4},{1,25},{... | collective-permute-start | bytes 786440 | tf_op jit(solution)/shard_map/ppermute | solution.py:474
  21.1 2.0 %collective-permute-start.6 = (bf16[64,512]{1,0:T(8,128)(2,1)S(1)}, bf16[64,512]{1,0:T(8,128)(2,1)S(1)}, u32[]{:S(2)}, u32[]{:S(2)}) collective-permute-start(bf16[64,512]{1,0:T(8,128)(2,1)S(1)} %join.5.own_ref), channel_id=1, source_target_pairs={{0,3},{1,2},{2,1},{3,0},{4,7},{5,6},{6,5},{7,4},{8,11},{9,10},{10,... | collective-permute-start | bytes 196616 | tf_op jit(solution)/shard_map/ppermute | solution.py:471
  23.1 4.1 %collective-permute-done.6.refs_1_ = bf16[64,512]{1,0:T(8,128)(2,1)S(1)} collective-permute-done((bf16[64,512]{1,0:T(8,128)(2,1)S(1)}, bf16[64,512]{1,0:T(8,128)(2,1)S(1)}, u32[]{:S(2)}, u32[]{:S(2)}) %collective-permute-start.6) | collective-permute-done | bytes 65568 | tf_op jit(solution)/shard_map/ppermute | solution.py:471
  27.2 1.5 %collective-permute-done.5.refs_0_ = bf16[64,512]{1,0:T(8,128)(2,1)S(1)} collective-permute-done((bf16[64,512]{1,0:T(8,128)(2,1)S(1)}, bf16[64,512]{1,0:T(8,128)(2,1)S(1)}, u32[]{:S(2)}, u32[]{:S(2)}) %collective-permute-start.5) | collective-permute-done | bytes 65568 | tf_op jit(solution)/shard_map/ppermute | solution.py:471
  28.7 1.6 %collective-permute-start.8 = (bf16[4,64,512]{2,1,0:T(8,128)(2,1)S(1)}, bf16[4,64,512]{2,1,0:T(8,128)(2,1)S(1)}, u32[]{:S(2)}, u32[]{:S(2)}) collective-permute-start(bf16[4,64,512]{2,1,0:T(8,128)(2,1)S(1)} %line.3.refs_10_.refs_6_), channel_id=1, source_target_pairs={{0,8},{4,12},{8,0},{12,4},{16,24},{20,28},{24,16},{28,20},{1,9},{5... | collective-permute-start | bytes 786440 | tf_op jit(solution)/shard_map/ppermute | solution.py:474
  30.3 1.5 %collective-permute-start.9 = (bf16[4,64,512]{2,1,0:T(8,128)(2,1)S(1)}, bf16[4,64,512]{2,1,0:T(8,128)(2,1)S(1)}, u32[]{:S(2)}, u32[]{:S(2)}) collective-permute-start(bf16[4,64,512]{2,1,0:T(8,128)(2,1)S(1)} %line.3.refs_10_.refs_6_), channel_id=1, source_target_pairs={{0,16},{4,20},{8,24},{12,28},{16,0},{20,4},{24,8},{28,12},{1,17},{... | collective-permute-start | bytes 786440 | tf_op jit(solution)/shard_map/ppermute | solution.py:474
  32.8 8.7 %attention.2 = (bf16[256,2048]{1,0:T(8,128)(2,1)}, bf16[256,2048]{1,0:T(8,128)(2,1)}, bf16[256,2048]{1,0:T(8,128)(2,1)}, bf16[256,2048]{1,0:T(8,128)(2,1)}, bf16...) custom-call(s32[2]{0:T(128)S(1)} %pad_add_fusion.place_ref.refs_0_, ...), custom_call_target="tpu_custom_call" | custom-call | flops 2013265920 | bytes 6291456 | tf_op jit(solution)/shard_map/attention/pallas_call | solution.py:263
  41.5 1.6 %collective-permute-start.13 = (bf16[4,64,512]{2,1,0:T(8,128)(2,1)S(1)}, bf16[4,64,512]{2,1,0:T(8,128)(2,1)S(1)}, u32[]{:S(2)}, u32[]{:S(2)}) collective-permute-start(bf16[4,64,512]{2,1,0:T(8,128)(2,1)S(1)} %hold.9), channel_id=1, source_target_pairs={{0,8},{4,12},{8,0},{12,4},{16,24},{20,28},{24,16},{28,20},{1,9},{5... | collective-permute-start | bytes 786440 | tf_op jit(solution)/shard_map/ppermute | solution.py:474
  43.3 1.5 %collective-permute-start.15 = (bf16[4,64,512]{2,1,0:T(8,128)(2,1)S(1)}, bf16[4,64,512]{2,1,0:T(8,128)(2,1)S(1)}, u32[]{:S(2)}, u32[]{:S(2)}) collective-permute-start(bf16[4,64,512]{2,1,0:T(8,128)(2,1)S(1)} %hold.11), channel_id=1, source_target_pairs={{0,16},{4,20},{8,24},{12,28},{16,0},{20,4},{24,8},{28,12},{1,17},{... | collective-permute-start | bytes 786440 | tf_op jit(solution)/shard_map/ppermute | solution.py:474
  45.5 8.6 %attention.3 = (bf16[256,2048]{1,0:T(8,128)(2,1)}, bf16[256,2048]{1,0:T(8,128)(2,1)}, bf16[256,2048]{1,0:T(8,128)(2,1)}, bf16[256,2048]{1,0:T(8,128)(2,1)}, bf16...) custom-call(s32[2]{0:T(128)S(1)} %pad_add_fusion.place_ref.refs_0_, ...), custom_call_target="tpu_custom_call", output_to_operand_aliasing={{0}: (10, {}), {1}: (11, {}), {2}: (12, {}), {3}: (13, {}),... | custom-call | flops 2013265920 | bytes 6291456 | tf_op jit(solution)/shard_map/attention/pallas_call | solution.py:263
  54.2 1.4 %collective-permute-start.14 = (bf16[4,64,512]{2,1,0:T(8,128)(2,1)S(1)}, bf16[4,64,512]{2,1,0:T(8,128)(2,1)S(1)}, u32[]{:S(2)}, u32[]{:S(2)}) collective-permute-start(bf16[4,64,512]{2,1,0:T(8,128)(2,1)S(1)} %hold.10), channel_id=1, source_target_pairs={{0,8},{4,12},{8,0},{12,4},{16,24},{20,28},{24,16},{28,20},{1,9},{5... | collective-permute-start | bytes 786440 | tf_op jit(solution)/shard_map/ppermute | solution.py:474
  55.6 1.4 %collective-permute-start.16 = (bf16[4,64,512]{2,1,0:T(8,128)(2,1)S(1)}, bf16[4,64,512]{2,1,0:T(8,128)(2,1)S(1)}, u32[]{:S(2)}, u32[]{:S(2)}) collective-permute-start(bf16[4,64,512]{2,1,0:T(8,128)(2,1)S(1)} %hold.12), channel_id=1, source_target_pairs={{0,16},{4,20},{8,24},{12,28},{16,0},{20,4},{24,8},{28,12},{1,17},{... | collective-permute-start | bytes 786440 | tf_op jit(solution)/shard_map/ppermute | solution.py:474
  58.3 2.0 %collective-permute-start.20 = (bf16[64,512]{1,0:T(8,128)(2,1)S(1)}, bf16[64,512]{1,0:T(8,128)(2,1)S(1)}, u32[]{:S(2)}, u32[]{:S(2)}) collective-permute-start(bf16[64,512]{1,0:T(8,128)(2,1)S(1)} %get-tuple-element.64), channel_id=1, source_target_pairs={{0,3},{1,2},{2,1},{3,0},{4,7},{5,6},{6,5},{7,4},{8,11},{9,10},{10,... | collective-permute-start | bytes 196616 | tf_op jit(solution)/shard_map/ppermute | solution.py:471
  60.3 3.0 %collective-permute-done.19.refs_5_.refs_2_ = bf16[64,512]{1,0:T(8,128)(2,1)S(1)} collective-permute-done((bf16[64,512]{1,0:T(8,128)(2,1)S(1)}, bf16[64,512]{1,0:T(8,128)(2,1)S(1)}, u32[]{:S(2)}, u32[]{:S(2)}) %collective-permute-start.19) | collective-permute-done | bytes 65568 | tf_op jit(solution)/shard_map/ppermute | solution.py:471
  64.4 2.9 %collective-permute-done.16.refs_2_ = bf16[4,64,512]{2,1,0:T(8,128)(2,1)S(1)} collective-permute-done((bf16[4,64,512]{2,1,0:T(8,128)(2,1)S(1)}, bf16[4,64,512]{2,1,0:T(8,128)(2,1)S(1)}, u32[]{:S(2)}, u32[]{:S(2)}) %collective-permute-start.16) | collective-permute-done | bytes 262176 | tf_op jit(solution)/shard_map/ppermute | solution.py:474
  67.6 2.7 %collective-permute-start.23 = (bf16[64,512]{1,0:T(8,128)(2,1)S(1)}, bf16[64,512]{1,0:T(8,128)(2,1)S(1)}, u32[]{:S(2)}, u32[]{:S(2)}) collective-permute-start(bf16[64,512]{1,0:T(8,128)(2,1)S(1)} %get-tuple-element.77), channel_id=1, source_target_pairs={{0,2},{1,3},{2,0},{3,1},{4,6},{5,7},{6,4},{7,5},{8,10},{9,11},{10,... | collective-permute-start | bytes 196616 | tf_op jit(solution)/shard_map/ppermute | solution.py:471
  70.3 1.7 %collective-permute-start.24 = (bf16[64,512]{1,0:T(8,128)(2,1)S(1)}, bf16[64,512]{1,0:T(8,128)(2,1)S(1)}, u32[]{:S(2)}, u32[]{:S(2)}) collective-permute-start(bf16[64,512]{1,0:T(8,128)(2,1)S(1)} %get-tuple-element.78), channel_id=1, source_target_pairs={{0,3},{1,2},{2,1},{3,0},{4,7},{5,6},{6,5},{7,4},{8,11},{9,10},{10,... | collective-permute-start | bytes 196616 | tf_op jit(solution)/shard_map/ppermute | solution.py:471
  72.0 1.9 %settle.1 = (bf16[256,2048]{1,0:T(8,128)(2,1)}, bf16[256,2048]{1,0:T(8,128)(2,1)}, bf16[256,2048]{1,0:T(8,128)(2,1)}, bf16[256,2048]{1,0:T(8,128)(2,1)}, f32[8,128]{1,0:T(8,128)S(1)}) custom-call(s32[2]{0:T(128)S(1)} %pad_add_fusion.place_ref.refs_0_, ...), custom_call_target="tpu_custom_call", output_to_operand_aliasing={{0}: (2, {}), {1}: (3, {}), {2}: (4, {}), {3}: (5, {})} | custom-call | tf_op jit(solution)/shard_map/settle/pallas_call | solution.py:413
  73.9 2.8 %collective-permute-done.24.refs_7_ = bf16[64,512]{1,0:T(8,128)(2,1)S(1)} collective-permute-done((bf16[64,512]{1,0:T(8,128)(2,1)S(1)}, bf16[64,512]{1,0:T(8,128)(2,1)S(1)}, u32[]{:S(2)}, u32[]{:S(2)}) %collective-permute-start.24) | collective-permute-done | bytes 65568 | tf_op jit(solution)/shard_map/ppermute | solution.py:471
  (50 shorter events, 10.6 us)
Async XLA Ops:
  4.4 13.1 %collective-permute-start.1 = (bf16[4,256,1024]{2,1,0:T(8,128)(2,1)S(1)}, bf16[4,256,1024]{2,1,0:T(8,128)(2,1)S(1)}, u32[]{:S(2)}, u32[]{:S(2)}) collective-permute-start(bf16[4,256,1024]{2,1,0:T(8,128)(2,1)S(1)} %hold.8), channel_id=1, source_target_pairs={{0,4},{4,0},{8,12},{12,8},{16,20},{20,16},{24,28},{28,24},{1,5},{5... | collective-permute-start | bytes 6291464 | tf_op jit(solution)/shard_map/ppermute | solution.py:474
  4.7 12.7 %collective-permute-start.2 = (bf16[64,1024]{1,0:T(8,128)(2,1)S(1)}, bf16[64,1024]{1,0:T(8,128)(2,1)S(1)}, u32[]{:S(2)}, u32[]{:S(2)}) collective-permute-start(bf16[64,1024]{1,0:T(8,128)(2,1)S(1)} %join.4), channel_id=1, source_target_pairs={{0,1},{1,0},{2,3},{3,2},{4,5},{5,4},{6,7},{7,6},{8,9},{9,8},{10,11... | collective-permute-start | bytes 393224 | tf_op jit(solution)/shard_map/ppermute | solution.py:471
  7.5 8.3 %collective-permute-start.4 = (bf16[64,512]{1,0:T(8,128)(2,1)S(1)}, bf16[64,512]{1,0:T(8,128)(2,1)S(1)}, u32[]{:S(2)}, u32[]{:S(2)}) collective-permute-start(bf16[64,512]{1,0:T(8,128)(2,1)S(1)} %join.3.own_ref), channel_id=1, source_target_pairs={{0,3},{1,2},{2,1},{3,0},{4,7},{5,6},{6,5},{7,4},{8,11},{9,10},{10,... | collective-permute-start | bytes 196616 | tf_op jit(solution)/shard_map/ppermute | solution.py:471
  10.0 7.4 %collective-permute-start.3 = (bf16[64,512]{1,0:T(8,128)(2,1)S(1)}, bf16[64,512]{1,0:T(8,128)(2,1)S(1)}, u32[]{:S(2)}, u32[]{:S(2)}) collective-permute-start(bf16[64,512]{1,0:T(8,128)(2,1)S(1)} %join.3.own_ref), channel_id=1, source_target_pairs={{0,2},{1,3},{2,0},{3,1},{4,6},{5,7},{6,4},{7,5},{8,10},{9,11},{10,... | collective-permute-start | bytes 196616 | tf_op jit(solution)/shard_map/ppermute | solution.py:471
  17.5 11.2 %collective-permute-start.7 = (bf16[4,64,512]{2,1,0:T(8,128)(2,1)S(1)}, bf16[4,64,512]{2,1,0:T(8,128)(2,1)S(1)}, u32[]{:S(2)}, u32[]{:S(2)}) collective-permute-start(bf16[4,64,512]{2,1,0:T(8,128)(2,1)S(1)} %line.2.refs_0_.refs_6_), channel_id=1, source_target_pairs={{0,24},{4,28},{8,16},{12,20},{16,8},{20,12},{24,0},{28,4},{1,25},{... | collective-permute-start | bytes 786440 | tf_op jit(solution)/shard_map/ppermute | solution.py:474
  20.0 12.3 %collective-permute-start.12 = (bf16[4,64,512]{2,1,0:T(8,128)(2,1)S(1)}, bf16[4,64,512]{2,1,0:T(8,128)(2,1)S(1)}, u32[]{:S(2)}, u32[]{:S(2)}) collective-permute-start(bf16[4,64,512]{2,1,0:T(8,128)(2,1)S(1)} %line.2.refs_0_.refs_6_), channel_id=1, source_target_pairs={{0,16},{4,20},{8,24},{12,28},{16,0},{20,4},{24,8},{28,12},{1,17},{... | collective-permute-start | bytes 786440 | tf_op jit(solution)/shard_map/ppermute | solution.py:474
  20.5 12.3 %collective-permute-start.11 = (bf16[4,64,512]{2,1,0:T(8,128)(2,1)S(1)}, bf16[4,64,512]{2,1,0:T(8,128)(2,1)S(1)}, u32[]{:S(2)}, u32[]{:S(2)}) collective-permute-start(bf16[4,64,512]{2,1,0:T(8,128)(2,1)S(1)} %line.2.refs_0_.refs_6_), channel_id=1, source_target_pairs={{0,8},{4,12},{8,0},{12,4},{16,24},{20,28},{24,16},{28,20},{1,9},{5... | collective-permute-start | bytes 786440 | tf_op jit(solution)/shard_map/ppermute | solution.py:474
  21.1 6.2 %collective-permute-start.6 = (bf16[64,512]{1,0:T(8,128)(2,1)S(1)}, bf16[64,512]{1,0:T(8,128)(2,1)S(1)}, u32[]{:S(2)}, u32[]{:S(2)}) collective-permute-start(bf16[64,512]{1,0:T(8,128)(2,1)S(1)} %join.5.own_ref), channel_id=1, source_target_pairs={{0,3},{1,2},{2,1},{3,0},{4,7},{5,6},{6,5},{7,4},{8,11},{9,10},{10,... | collective-permute-start | bytes 196616 | tf_op jit(solution)/shard_map/ppermute | solution.py:471
  23.1 5.6 %collective-permute-start.5 = (bf16[64,512]{1,0:T(8,128)(2,1)S(1)}, bf16[64,512]{1,0:T(8,128)(2,1)S(1)}, u32[]{:S(2)}, u32[]{:S(2)}) collective-permute-start(bf16[64,512]{1,0:T(8,128)(2,1)S(1)} %join.5.own_ref), channel_id=1, source_target_pairs={{0,2},{1,3},{2,0},{3,1},{4,6},{5,7},{6,4},{7,5},{8,10},{9,11},{10,... | collective-permute-start | bytes 196616 | tf_op jit(solution)/shard_map/ppermute | solution.py:471
  28.7 12.8 %collective-permute-start.8 = (bf16[4,64,512]{2,1,0:T(8,128)(2,1)S(1)}, bf16[4,64,512]{2,1,0:T(8,128)(2,1)S(1)}, u32[]{:S(2)}, u32[]{:S(2)}) collective-permute-start(bf16[4,64,512]{2,1,0:T(8,128)(2,1)S(1)} %line.3.refs_10_.refs_6_), channel_id=1, source_target_pairs={{0,8},{4,12},{8,0},{12,4},{16,24},{20,28},{24,16},{28,20},{1,9},{5... | collective-permute-start | bytes 786440 | tf_op jit(solution)/shard_map/ppermute | solution.py:474
  30.3 13.0 %collective-permute-start.9 = (bf16[4,64,512]{2,1,0:T(8,128)(2,1)S(1)}, bf16[4,64,512]{2,1,0:T(8,128)(2,1)S(1)}, u32[]{:S(2)}, u32[]{:S(2)}) collective-permute-start(bf16[4,64,512]{2,1,0:T(8,128)(2,1)S(1)} %line.3.refs_10_.refs_6_), channel_id=1, source_target_pairs={{0,16},{4,20},{8,24},{12,28},{16,0},{20,4},{24,8},{28,12},{1,17},{... | collective-permute-start | bytes 786440 | tf_op jit(solution)/shard_map/ppermute | solution.py:474
  31.8 13.0 %collective-permute-start.10 = (bf16[4,64,512]{2,1,0:T(8,128)(2,1)S(1)}, bf16[4,64,512]{2,1,0:T(8,128)(2,1)S(1)}, u32[]{:S(2)}, u32[]{:S(2)}) collective-permute-start(bf16[4,64,512]{2,1,0:T(8,128)(2,1)S(1)} %line.3.refs_10_.refs_6_), channel_id=1, source_target_pairs={{0,24},{4,28},{8,16},{12,20},{16,8},{20,12},{24,0},{28,4},{1,25},{... | collective-permute-start | bytes 786440 | tf_op jit(solution)/shard_map/ppermute | solution.py:474
  41.5 12.6 %collective-permute-start.13 = (bf16[4,64,512]{2,1,0:T(8,128)(2,1)S(1)}, bf16[4,64,512]{2,1,0:T(8,128)(2,1)S(1)}, u32[]{:S(2)}, u32[]{:S(2)}) collective-permute-start(bf16[4,64,512]{2,1,0:T(8,128)(2,1)S(1)} %hold.9), channel_id=1, source_target_pairs={{0,8},{4,12},{8,0},{12,4},{16,24},{20,28},{24,16},{28,20},{1,9},{5... | collective-permute-start | bytes 786440 | tf_op jit(solution)/shard_map/ppermute | solution.py:474
  43.3 12.3 %collective-permute-start.15 = (bf16[4,64,512]{2,1,0:T(8,128)(2,1)S(1)}, bf16[4,64,512]{2,1,0:T(8,128)(2,1)S(1)}, u32[]{:S(2)}, u32[]{:S(2)}) collective-permute-start(bf16[4,64,512]{2,1,0:T(8,128)(2,1)S(1)} %hold.11), channel_id=1, source_target_pairs={{0,16},{4,20},{8,24},{12,28},{16,0},{20,4},{24,8},{28,12},{1,17},{... | collective-permute-start | bytes 786440 | tf_op jit(solution)/shard_map/ppermute | solution.py:474
  44.8 12.2 %collective-permute-start.17 = (bf16[4,64,512]{2,1,0:T(8,128)(2,1)S(1)}, bf16[4,64,512]{2,1,0:T(8,128)(2,1)S(1)}, u32[]{:S(2)}, u32[]{:S(2)}) collective-permute-start(bf16[4,64,512]{2,1,0:T(8,128)(2,1)S(1)} %hold.13), channel_id=1, source_target_pairs={{0,24},{4,28},{8,16},{12,20},{16,8},{20,12},{24,0},{28,4},{1,25},{... | collective-permute-start | bytes 786440 | tf_op jit(solution)/shard_map/ppermute | solution.py:474
  54.2 10.3 %collective-permute-start.14 = (bf16[4,64,512]{2,1,0:T(8,128)(2,1)S(1)}, bf16[4,64,512]{2,1,0:T(8,128)(2,1)S(1)}, u32[]{:S(2)}, u32[]{:S(2)}) collective-permute-start(bf16[4,64,512]{2,1,0:T(8,128)(2,1)S(1)} %hold.10), channel_id=1, source_target_pairs={{0,8},{4,12},{8,0},{12,4},{16,24},{20,28},{24,16},{28,20},{1,9},{5... | collective-permute-start | bytes 786440 | tf_op jit(solution)/shard_map/ppermute | solution.py:474
  55.6 11.7 %collective-permute-start.16 = (bf16[4,64,512]{2,1,0:T(8,128)(2,1)S(1)}, bf16[4,64,512]{2,1,0:T(8,128)(2,1)S(1)}, u32[]{:S(2)}, u32[]{:S(2)}) collective-permute-start(bf16[4,64,512]{2,1,0:T(8,128)(2,1)S(1)} %hold.12), channel_id=1, source_target_pairs={{0,16},{4,20},{8,24},{12,28},{16,0},{20,4},{24,8},{28,12},{1,17},{... | collective-permute-start | bytes 786440 | tf_op jit(solution)/shard_map/ppermute | solution.py:474
  57.1 10.2 %collective-permute-start.18 = (bf16[4,64,512]{2,1,0:T(8,128)(2,1)S(1)}, bf16[4,64,512]{2,1,0:T(8,128)(2,1)S(1)}, u32[]{:S(2)}, u32[]{:S(2)}) collective-permute-start(bf16[4,64,512]{2,1,0:T(8,128)(2,1)S(1)} %hold.14), channel_id=1, source_target_pairs={{0,24},{4,28},{8,16},{12,20},{16,8},{20,12},{24,0},{28,4},{1,25},{... | collective-permute-start | bytes 786440 | tf_op jit(solution)/shard_map/ppermute | solution.py:474
  57.9 5.4 %collective-permute-start.19 = (bf16[64,512]{1,0:T(8,128)(2,1)S(1)}, bf16[64,512]{1,0:T(8,128)(2,1)S(1)}, u32[]{:S(2)}, u32[]{:S(2)}) collective-permute-start(bf16[64,512]{1,0:T(8,128)(2,1)S(1)} %get-tuple-element.63), channel_id=1, source_target_pairs={{0,2},{1,3},{2,0},{3,1},{4,6},{5,7},{6,4},{7,5},{8,10},{9,11},{10,... | collective-permute-start | bytes 196616 | tf_op jit(solution)/shard_map/ppermute | solution.py:471
  58.3 6.2 %collective-permute-start.20 = (bf16[64,512]{1,0:T(8,128)(2,1)S(1)}, bf16[64,512]{1,0:T(8,128)(2,1)S(1)}, u32[]{:S(2)}, u32[]{:S(2)}) collective-permute-start(bf16[64,512]{1,0:T(8,128)(2,1)S(1)} %get-tuple-element.64), channel_id=1, source_target_pairs={{0,3},{1,2},{2,1},{3,0},{4,7},{5,6},{6,5},{7,4},{8,11},{9,10},{10,... | collective-permute-start | bytes 196616 | tf_op jit(solution)/shard_map/ppermute | solution.py:471
  67.4 4.5 %collective-permute-start.21 = (bf16[4,256,1024]{2,1,0:T(8,128)(2,1)S(1)}, bf16[4,256,1024]{2,1,0:T(8,128)(2,1)S(1)}, u32[]{:S(2)}, u32[]{:S(2)}) collective-permute-start(bf16[4,256,1024]{2,1,0:T(8,128)(2,1)S(1)} %hold.15), channel_id=1, source_target_pairs={{0,4},{4,0},{8,12},{12,8},{16,20},{20,16},{24,28},{28,24},{1,5},{5... | collective-permute-start | bytes 6291464 | tf_op jit(solution)/shard_map/ppermute | solution.py:474
  67.5 9.2 %collective-permute-start.22 = (bf16[64,1024]{1,0:T(8,128)(2,1)S(1)}, bf16[64,1024]{1,0:T(8,128)(2,1)S(1)}, u32[]{:S(2)}, u32[]{:S(2)}) collective-permute-start(bf16[64,1024]{1,0:T(8,128)(2,1)S(1)} %get-tuple-element.74), channel_id=1, source_target_pairs={{0,1},{1,0},{2,3},{3,2},{4,5},{5,4},{6,7},{7,6},{8,9},{9,8},{10,11... | collective-permute-start | bytes 393224 | tf_op jit(solution)/shard_map/ppermute | solution.py:471
  67.6 6.3 %collective-permute-start.23 = (bf16[64,512]{1,0:T(8,128)(2,1)S(1)}, bf16[64,512]{1,0:T(8,128)(2,1)S(1)}, u32[]{:S(2)}, u32[]{:S(2)}) collective-permute-start(bf16[64,512]{1,0:T(8,128)(2,1)S(1)} %get-tuple-element.77), channel_id=1, source_target_pairs={{0,2},{1,3},{2,0},{3,1},{4,6},{5,7},{6,4},{7,5},{8,10},{9,11},{10,... | collective-permute-start | bytes 196616 | tf_op jit(solution)/shard_map/ppermute | solution.py:471
  70.3 6.4 %collective-permute-start.24 = (bf16[64,512]{1,0:T(8,128)(2,1)S(1)}, bf16[64,512]{1,0:T(8,128)(2,1)S(1)}, u32[]{:S(2)}, u32[]{:S(2)}) collective-permute-start(bf16[64,512]{1,0:T(8,128)(2,1)S(1)} %get-tuple-element.78), channel_id=1, source_target_pairs={{0,3},{1,2},{2,1},{3,0},{4,7},{5,6},{6,5},{7,4},{8,11},{9,10},{10,... | collective-permute-start | bytes 196616 | tf_op jit(solution)/shard_map/ppermute | solution.py:471
  (2 other events, 2.8 us)

commit v5 on v4

--- a/solution.py
+++ b/solution.py
@@ -122,40 +122,56 @@
     )(mine, came, *after)
 
 
+def stage_body(n_cols, nz, n_sum, place_ref, *refs):
+    sources, (out_ref, mask_ref, sem) = refs[:4], refs[4:]
+    tokens, width = sources[0].shape
+    half = width // 2
+    copies = [
+        pltpu.make_async_copy(
+            source.at[:, core_window(place_ref, 0, half, 0, half)], out_ref.at[i], sem.at[i]
+        )
+        for i, source in enumerate(sources)
+    ]
+    for copy in copies:
+        copy.start()
+    mask_ref[...] = far_mask(place_ref[0], place_ref[1], n_cols, nz, n_sum, tokens)
+    for copy in copies:
+        copy.wait()
+
+
+def stage(place, arrays, n_cols, nz):
+    tokens, width = arrays[0].shape
+    n_sum = tokens // BLOCK * SUMMARY
+    nkeys = 2 * n_cols * nz * n_sum
+    return pl.pallas_call(
+        functools.partial(stage_body, n_cols, nz, n_sum),
+        in_specs=[in_smem] + [in_hbm] * 4,
+        out_specs=[in_vmem] * 2,
+        out_shape=[
+            jax.ShapeDtypeStruct((4, tokens, width // 2), arrays[0].dtype),
+            jax.ShapeDtypeStruct((2 * tokens, nkeys), jnp.float32),
+        ],
+        scratch_shapes=[pltpu.SemaphoreType.DMA((4,))],
+        compiler_params=params,
+        cost_estimate=pl.CostEstimate(
+            flops=0, bytes_accessed=8 * tokens * width, transcendentals=0
+        ),
+        name="stage",
+    )(place, *[pltpu.with_memory_space_constraint(x, pltpu.HBM) for x in arrays])
+
+
 def attention_body(n_sum, n_cols, n_skip, first, heads, *refs):
-    place_ref = refs[0]
-    sources, came_ref = refs[1:5], refs[5]
-    col_refs = refs[6 : 6 + n_cols]
-    outs = refs[6 + n_cols + n_skip :]
-    targets = outs[:4]
-    sent_ref, near_ref = outs[4:6]
-    back_refs = outs[6 : 6 + n_cols]
-    near_mask, away_mask, loads, stores, load_sem, store_sem = outs[6 + n_cols :]
-    tokens, width = sources[0].shape
+    mine_ref, came_ref, away_mask = refs[:3]
+    col_refs = refs[3 : 3 + n_cols]
+    outs = refs[3 + n_cols + n_skip :]
+    own_ref, sent_ref, near_ref = outs[:3]
+    back_refs = outs[3 : 4 + n_cols]
+    near_mask = outs[4 + n_cols]
+    tokens = mine_ref.shape[1]
     nz = col_refs[0].shape[0]
-    steps = heads // unroll
-    span = unroll * HEAD_DIM
-
-    def window(step):
-        return core_window(place_ref, 0, width // 2, first * HEAD_DIM + step * span, span)
-
-    def load(step, i):
-        return pltpu.make_async_copy(
-            sources[i].at[:, window(step)], loads.at[step, i], load_sem.at[step, i]
-        )
-
-    def store(step, i):
-        return pltpu.make_async_copy(
-            stores.at[step, i], targets[i].at[:, window(step)], store_sem.at[step, i]
-        )
-
-    for step in range(steps):
-        for i in range(4):
-            load(step, i).start()
     n_blocks = tokens // BLOCK
     blocks = [slice(b * BLOCK, (b + 1) * BLOCK) for b in range(2 * n_blocks)]
     near_mask[...] = block_mask()
-    away_mask[...] = far_mask(place_ref[0], place_ref[1], n_cols, nz, n_sum, tokens)
 
     def here(to):
         return pl.ds(pl.multiple_of(first * HEAD_DIM + to.start, HEAD_DIM), HEAD_DIM)
@@ -169,15 +185,16 @@
                     parts.append(ref[j, row : row + n_sum, to])
         return jnp.concatenate(parts, axis=0)
 
-    def keep(step, i, at, to, b, value):
+    def keep(i, to, b, value):
         if b < n_blocks:
-            stores[step, i, blocks[b], at] = value
+            own_ref[i, blocks[b], here(to)] = value
         else:
             sent_ref[i, blocks[b - n_blocks], here(to)] = value
 
-    def head(step, at, to):
+    def head(to):
         q, k_loc, v_loc, g = (
-            jnp.concatenate([loads[step, i, :, at], came_ref[i, :, here(to)]], axis=0) for i in range(4)
+            jnp.concatenate([ref[i, :, here(to)] for ref in (mine_ref, came_ref)], axis=0)
+            for i in range(4)
         )
         k_far = far_rows(0, to)
         v_far = far_rows(n_sum, to)
@@ -211,73 +228,55 @@
         dq = dq.astype(jnp.bfloat16)
         gi = (gf * inv).astype(jnp.bfloat16)
         for n, b in enumerate(blocks):
-            keep(step, 0, at, to, n, out[b])
-            keep(step, 1, at, to, n, dq[b])
+            keep(0, to, n, out[b])
+            keep(1, to, n, dq[b])
             for i, (left, right) in enumerate(((ds_loc, q), (eb_loc, gi))):
                 part = dot(left[b], right[b], 0, 0)
-                keep(step, 2 + i, at, to, n, part.astype(jnp.bfloat16))
+                keep(2 + i, to, n, part.astype(jnp.bfloat16))
                 t, row = n // n_blocks, (i * n_blocks + n % n_blocks) * EDGE
                 near_ref[t, row : row + EDGE, to] = part[BLOCK - EDGE :, :]
         dk_far = dot(q, ds_far, 0, 0).astype(jnp.bfloat16).T
         dv_far = dot(gi, eb_far, 0, 0).astype(jnp.bfloat16).T
         row = 0
-        for ref in back_refs:
+        for c in range(n_cols):
             for j in range(nz):
+                ref, place = back_refs[c], j
+                if c == n_cols - 1:
+                    ref, place = back_refs[c + j % 2], j // 2
                 for core in range(2):
                     to_row = 2 * core * n_sum
-                    ref[j, to_row : to_row + n_sum, to] = dk_far[row : row + n_sum]
-                    ref[j, to_row + n_sum : to_row + 2 * n_sum, to] = dv_far[row : row + n_sum]
+                    ref[place, to_row : to_row + n_sum, to] = dk_far[row : row + n_sum]
+                    ref[place, to_row + n_sum : to_row + 2 * n_sum, to] = dv_far[row : row + n_sum]
                     row += n_sum
 
     def turn(step, carried):
-        for i in range(4):
-            load(step, i).wait()
         for u in range(unroll):
-            to = pl.ds(pl.multiple_of(step * span + u * HEAD_DIM, HEAD_DIM), HEAD_DIM)
-            head(step, slice(u * HEAD_DIM, (u + 1) * HEAD_DIM), to)
-        for i in range(4):
-            store(step, i).start()
+            h = step * unroll + u
+            head(pl.ds(pl.multiple_of(h * HEAD_DIM, HEAD_DIM), HEAD_DIM))
         return carried
 
-    lax.fori_loop(0, steps, turn, 0)
-    for step in range(steps):
-        for i in range(4):
-            store(step, i).wait()
-
-
-def attention(place, mine, came, cols, earlier, after, first, heads):
-    tokens, width = mine[0].shape
+    lax.fori_loop(0, heads // unroll, turn, 0)
+
+
+def attention(mine, came, mask, cols, earlier, after, first, heads):
+    tokens = mine.shape[1]
     n_cols = len(cols)
     nz, rows, chunk_width = cols[0].shape
     n_sum = rows // 4
-    nkeys = n_cols * nz * rows // 2
+    nkeys = mask.shape[1]
     n_blocks = tokens // BLOCK
-    steps = heads // unroll
-    full = jax.ShapeDtypeStruct((tokens, width), jnp.bfloat16)
+    results = jax.ShapeDtypeStruct(mine.shape, mine.dtype)
+    near = jax.ShapeDtypeStruct((2, 2 * n_blocks * EDGE, chunk_width), jnp.float32)
+    back = jax.ShapeDtypeStruct((nz, rows, chunk_width), jnp.bfloat16)
+    half = jax.ShapeDtypeStruct((nz // 2, rows, chunk_width), jnp.bfloat16)
     n_skip = len(earlier) + len(after)
-    rest = [
-        jax.ShapeDtypeStruct((4, tokens, width // 2), jnp.bfloat16),
-        jax.ShapeDtypeStruct((2, 2 * n_blocks * EDGE, chunk_width), jnp.float32),
-    ] + [jax.ShapeDtypeStruct((nz, rows, chunk_width), jnp.bfloat16)] * n_cols
-    mine = [pltpu.with_memory_space_constraint(x, pltpu.HBM) for x in mine]
     return pl.pallas_call(
         functools.partial(attention_body, n_sum, n_cols, n_skip, first, heads),
-        in_specs=[in_smem]
-        + [in_hbm] * 4
-        + [in_vmem] * (1 + n_cols)
-        + [in_hbm] * len(earlier[:4])
-        + [in_vmem] * (len(earlier[4:]) + len(after)),
-        out_specs=[in_hbm] * 4 + [in_vmem] * len(rest),
-        out_shape=[full] * 4 + rest,
-        scratch_shapes=[
-            pltpu.VMEM((BLOCK, BLOCK), jnp.float32),
-            pltpu.VMEM((2 * tokens, nkeys), jnp.float32),
-            pltpu.VMEM((steps, 4, tokens, unroll * HEAD_DIM), jnp.bfloat16),
-            pltpu.VMEM((steps, 4, tokens, unroll * HEAD_DIM), jnp.bfloat16),
-            pltpu.SemaphoreType.DMA((steps, 4)),
-            pltpu.SemaphoreType.DMA((steps, 4)),
-        ],
-        input_output_aliases={6 + n_cols + i: i for i in range(len(earlier))},
+        in_specs=[in_vmem] * (3 + n_cols + n_skip),
+        out_specs=[in_vmem] * (4 + n_cols),
+        out_shape=[results, results, near] + [back] * (n_cols - 1) + [half] * 2,
+        scratch_shapes=[pltpu.VMEM((BLOCK, BLOCK), jnp.float32)],
+        input_output_aliases={3 + n_cols + i: i for i in range(len(earlier))},
         compiler_params=params,
         cost_estimate=pl.CostEstimate(
             flops=heads * 24 * tokens * (BLOCK + nkeys) * HEAD_DIM,
@@ -285,7 +284,7 @@
             transcendentals=heads * 2 * tokens * (BLOCK + nkeys),
         ),
         name="attention",
-    )(place, *mine, came, *cols, *earlier, *after)
+    )(mine, came, mask, *cols, *earlier, *after)
 
 
 def hold_body(*refs):
@@ -323,49 +322,101 @@
     )(own, pair, *far, *after)
 
 
-def column_sum_body(n_in, n_pairs, n_after, *refs):
-    in_refs, pair_refs = refs[:n_in], refs[n_in : n_in + n_pairs]
-    out_refs = refs[n_in + n_pairs + n_after :]
-    for j, ref in enumerate(out_refs):
+def pair_sum_body(keep_ref, came_ref, *refs):
+    total = keep_ref[...].astype(jnp.float32) + came_ref[...].astype(jnp.float32)
+    refs[-1][...] = total.astype(refs[-1].dtype)
+
+
+def pair_sum(keep, came, *after):
+    return pl.pallas_call(
+        pair_sum_body,
+        in_specs=[in_vmem] * (2 + len(after)),
+        out_specs=in_vmem,
+        out_shape=jax.ShapeDtypeStruct(keep.shape, keep.dtype),
+        compiler_params=params,
+        name="pair_sum",
+    )(keep, came, *after)
+
+
+def store_places(totals, out_refs, apart):
+    if apart:
+        for ref, total in zip(out_refs, totals):
+            ref[...] = total.astype(ref.dtype)
+        return
+    for j, total in enumerate(totals):
+        if j % 2 == 0:
+            out_refs[j // 2][...] = total.astype(out_refs[j // 2].dtype)
+        else:
+            out_refs[-1][j // 2] = total.astype(out_refs[-1].dtype)
+
+
+def places_shapes(n, rows, width, apart):
+    kinds = [jnp.float32] + [jnp.bfloat16] * (n - 1)
+    if apart:
+        return [jax.ShapeDtypeStruct((rows, width), kind) for kind in kinds]
+    shapes = [jax.ShapeDtypeStruct((rows, width), kind) for kind in kinds[0::2]]
+    return shapes + [jax.ShapeDtypeStruct((n // 2, rows, width), jnp.bfloat16)]
+
+
+def column_sum_body(n_in, n_after, apart, *refs):
+    in_refs, out_refs = refs[:n_in], refs[n_in + n_after :]
+    totals = []
+    for j in range(in_refs[0].shape[0]):
         total = in_refs[0][j].astype(jnp.float32)
-        for came in in_refs[1:]:
+        for came in in_refs[1:-1]:
             total = total + came[j].astype(jnp.float32)
-        at = 0
-        if j == 1:
-            for pair in pair_refs:
-                ref[:, at : at + pair.shape[1]] = pair[...]
-                at += pair.shape[1]
-        ref[:, at : at + total.shape[1]] = total.astype(ref.dtype)
-
-
-def column_sum(parts, pairs, *after):
+        if j % 2 == 0:
+            total = total + in_refs[-1][j // 2].astype(jnp.float32)
+        totals.append(total)
+    store_places(totals, out_refs, apart)
+
+
+def column_sum(parts, apart, *after):
     nz, rows, width = parts[0].shape
-    shapes = [
-        jax.ShapeDtypeStruct((rows, width), jnp.float32 if j == 0 else jnp.bfloat16)
-        for j in range(nz)
+    shapes = places_shapes(nz, rows, width, apart)
+    return pl.pallas_call(
+        functools.partial(column_sum_body, len(parts), len(after), apart),
+        in_specs=[in_vmem] * (len(parts) + len(after)),
+        out_specs=[in_vmem] * len(shapes),
+        out_shape=shapes,
+        compiler_params=params,
+        name="column_sum",
+    )(*parts, *after)
+
+
+def fold_body(n, *refs):
+    keeps, came, out_refs = refs[:n], refs[n], refs[n + 1 :]
+    totals = [
+        keep[...].astype(jnp.float32) + came[i].astype(jnp.float32) for i, keep in enumerate(keeps)
     ]
-    wide = width + sum(pair.shape[1] for pair in pairs)
-    shapes[1] = jax.ShapeDtypeStruct((rows, wide), jnp.bfloat16)
-    return pl.pallas_call(
-        functools.partial(column_sum_body, len(parts), len(pairs), len(after)),
-        in_specs=[in_vmem] * (len(parts) + len(pairs) + len(after)),
-        out_specs=[in_vmem] * nz,
+    store_places(totals, out_refs, False)
+
+
+def fold(keeps, came):
+    n = len(keeps)
+    shapes = places_shapes(n, *keeps[0].shape, False)
+    return pl.pallas_call(
+        functools.partial(fold_body, n),
+        in_specs=[in_vmem] * (n + 1),
+        out_specs=[in_vmem] * len(shapes),
         out_shape=shapes,
         compiler_params=params,
-        name="column_sum",
-    )(*parts, *pairs, *after)
-
-
-def edge_body(n_chunks, n_terms, pair_ref, *refs):
-    terms, targets = refs[: n_chunks * n_terms], refs[-2:]
+        name="fold",
+    )(*keeps, came)
+
+
+def edge_body(counts, *refs):
+    targets = refs[-2:]
     at = 0
-    for c in range(0, len(terms), n_terms):
-        near_ref, *ends = terms[c : c + n_terms]
+    start = 0
+    for count in counts:
+        near_ref, *ends = refs[start : start + count]
+        start += count
         to = slice(at, at + near_ref.shape[2])
         at += near_ref.shape[2]
-        total = ends[0][...] + pair_ref[:, to].astype(jnp.float32)
+        total = ends[0][...]
         for term in ends[1:]:
-            total = total + term[...].astype(jnp.float32)
+            total = total + (term[0] if len(term.shape) == 3 else term[...]).astype(jnp.float32)
         rows = total.shape[0] // 2
         for t, target in enumerate(targets):
             for n in range(rows // SUMMARY):
@@ -376,51 +427,49 @@
                 target[n * EDGE : (n + 1) * EDGE, to] = tile
 
 
-def edge(pair, chunks, *after):
+def edge(chunks, *after):
     width = sum(chunk[0].shape[2] for chunk in chunks)
     shape = jax.ShapeDtypeStruct((chunks[0][0].shape[1], width), jnp.bfloat16)
     terms = [term for chunk in chunks for term in chunk]
     return pl.pallas_call(
-        functools.partial(edge_body, len(chunks), len(chunks[0])),
-        in_specs=[in_vmem] * (1 + len(terms) + len(after)),
+        functools.partial(edge_body, [len(chunk) for chunk in chunks]),
+        in_specs=[in_vmem] * (len(terms) + len(after)),
         out_specs=[in_vmem] * 2,
         out_shape=[shape] * 2,
         compiler_params=params,
         name="edge",
-    )(pair, *terms, *after)
-
-
-def settle_body(n_came, place_ref, *refs):
-    came_refs, targets = refs[:n_came], refs[n_came + 4 : n_came + 8]
-    token_ref, sem = refs[n_came + 8 :]
-    token_ref[...] = jnp.zeros(token_ref.shape, token_ref.dtype)
-    width = targets[0].shape[1]
+    )(*terms, *after)
+
+
+def settle_body(place_ref, own_ref, came_ref, *refs):
+    targets, (token_ref, sem) = refs[:4], refs[4:]
+    half = own_ref.shape[2]
     copies = []
-    at = 0
-    for c, came in enumerate(came_refs):
-        to = core_window(place_ref, 1, width // 2, at, came.shape[2])
-        at += came.shape[2]
+    for flip, source in enumerate((own_ref, came_ref)):
+        to = core_window(place_ref, flip, half, 0, half)
         for i, target in enumerate(targets):
-            copies.append(pltpu.make_async_copy(came.at[i], target.at[:, to], sem.at[c, i]))
+            copies.append(
+                pltpu.make_async_copy(source.at[i], target.at[:, to], sem.at[flip, i])
+            )
     for copy in copies:
         copy.start()
+    token_ref[...] = jnp.zeros(token_ref.shape, token_ref.dtype)
     for copy in copies:
         copy.wait()
 
 
-def settle(place, came, results):
-    n = len(came)
-    return pl.pallas_call(
-        functools.partial(settle_body, n),
-        in_specs=[in_smem] + [in_vmem] * n + [in_hbm] * 4,
+def settle(place, own, came):
+    tokens, half = own.shape[1:]
+    return pl.pallas_call(
+        settle_body,
+        in_specs=[in_smem, in_vmem, in_vmem],
         out_specs=[in_hbm] * 4 + [in_vmem],
-        out_shape=[jax.ShapeDtypeStruct(x.shape, x.dtype) for x in results]
+        out_shape=[jax.ShapeDtypeStruct((tokens, 2 * half), own.dtype)] * 4
         + [jax.ShapeDtypeStruct((8, 128), jnp.float32)],
-        scratch_shapes=[pltpu.SemaphoreType.DMA((n, 4))],
-        input_output_aliases={1 + n + i: i for i in range(4)},
+        scratch_shapes=[pltpu.SemaphoreType.DMA((2, 4))],
         compiler_params=params,
         name="settle",
-    )(place, *came, *results)
+    )(place, own, came)
 
 
 def finish_body(n_edges, n_blocks, place_ref, *refs):
@@ -477,13 +526,14 @@
         return [over_z(pieces[j], j) for j in reversed(range(2, nz))][::-1]
 
     def swap_columns(parts):
-        return [over_seq(parts[c], 2 * c) for c in reversed(range(1, n_cols))][::-1]
+        return [over_seq(parts[c], 2 * c) for c in reversed(range(1, len(parts)))][::-1]
 
     place = jnp.stack([lax.axis_index("seq"), lax.axis_index("head")]).astype(jnp.int32)
     arrays = (queries, keys_in, values_in, cotangent)
     mine, other, part = pack(place, arrays)
     came = over_seq(other, 1)
     pair = over_z(join(mine, came, 0, mine.shape[1]), 1)
+    ours, mask = stage(place, arrays, n_cols, nz)
     columns = []
     theirs = over_seq(hold([part], came)[0], 1)
     for c in range(n_chunks):
@@ -491,41 +541,49 @@
         at = firsts[c] * HEAD_DIM
         own = join(mine, came, at, width, *[cols[0] for cols in columns[-1:]])
         far = swap_far([own] * nz)
-        line = stack_line(own, pair, far, at, *([cols[-1] for cols in columns[-1:]] or [theirs]))
+        line = stack_line(own, pair, far, at, *([cols[-1] for cols in columns[-1:]] or [theirs, mask]))
         columns.append([line] + swap_columns([line] * n_cols))
 
     results = ()
-    chunks, pairs = [], []
+    chunks = []
     back = None
     for c in range(n_chunks):
         made = attention(
-            place,
-            arrays,
+            ours,
             theirs,
+            mask,
             columns[c],
             results,
-            [cols[0] for cols in columns[c + 1 : c + 2]],
+            [cols[0] for cols in columns[c + 1 : c + 2]] + ([paired] if c else []),
             firsts[c],
             chunk_heads[c],
         )
-        results, near, parts = made[:5], made[5], list(made[6:])
+        results, near, parts = made[:2], made[2], list(made[3:])
         waits = columns[c + 1] if c + 1 < n_chunks else [None] * n_cols
         if back is not None:
             waits = back[1]
-        moved = [hold([parts[i]], waits[i])[0] for i in range(1, n_cols)]
-        moved = swap_columns(parts[:1] + moved)
+        moved = [hold([parts[i]], waits[i])[0] for i in range(1, n_cols - 1)]
+        give = hold([parts[n_cols]], waits[n_cols - 2])[0] if c else parts[n_cols]
+        after = []
         if back is not None:
-            ends = column_sum(back[1], [], near)
-            pairs.append(ends[1])
-            chunks.append([back[0], ends[0]] + swap_far(ends))
+            *keeps, give_z = column_sum(back[1], False, near)
+            after = keeps[:1]
+        paired = pair_sum(parts[n_cols - 1], over_z(give, 1), *after)
+        last = over_seq(paired, 2 * (n_cols - 1))
+        moved = swap_columns(parts[:1] + moved) + [last]
+        if back is not None:
+            bits = 1
+            while len(keeps) > 1:
+                *keeps, give_z = fold(keeps, over_z(give_z, bits))
+                bits *= 2
+            chunks.append([back[0], keeps[0], over_z(give_z, bits)])
         back = near, parts[:1] + moved
-    ends = column_sum(back[1], pairs, *chunks[-1][2:])
-    pair = over_z(ends[1], 1)
-    chunks.append([back[0], ends[0]] + swap_far(ends))
-    *results, sent = results
+    ends = column_sum(back[1], True, chunks[-1][1])
+    chunks.append([back[0], ends[0], over_z(ends[1], 1)] + swap_far(ends))
+    own, sent = results
     (sent,) = hold([sent], ends[0])
-    *results, mark = settle(place, [over_seq(sent, 1)], results)
-    own, away = edge(pair, chunks, mark)
+    *results, mark = settle(place, own, over_seq(sent, 1))
+    own, away = edge(chunks, mark)
     attended, grad_queries, dk, dv = results
     edges = [own, over_seq(away, 1)]
     grad_keys, grad_values = finish(place, dk, dv, edges)

time: 79.8 us -> 78.2 us (0.980)
  starting transfers between devices: 29.7 us -> 32 us
  Pallas kernels: 23.2 us -> 21.2 us
  waiting for transfers between devices: 25.9 us -> 24 us
    pallas_call x2, Pallas kernels: 17.3 us -> 12.4 us  [attention(): pl.pallas_call(functools.partial(attention_body, n_sum, n_cols, n_skip, f...]
    pallas_call x4 -> x8, Pallas kernels: 2.25 us -> 5.11 us  [the longest x1 2.62 us: settle(): pl.pallas_call(settle_body, in_specs=[in_smem, in_vmem, in_vmem], out_spe...]
    ppermute x10 -> x12, waiting for transfers between devices: 19.9 us -> 17.5 us  [over_z(): return lax.ppermute(array, 'head', [(i, i ^ bits) for i in range(nz)])]
    ppermute x10 -> x12, starting transfers between devices: 14.3 us -> 15.7 us  [over_z(): return lax.ppermute(array, 'head', [(i, i ^ bits) for i in range(nz)])]
    ppermute x16, starting transfers between devices: 15.4 us -> 16.3 us  [over_seq(): return lax.ppermute(array, 'seq', [(i, i ^ bits) for i in range(n_seq)])]
  transfers between devices with their start and end apart: 26 -> 28, of which waited for: 13 -> 13; matrix products, arithmetic and copies ran while one was open for 0% -> 0% of each run, Pallas kernels for 24% -> 22%
where the time goes in v5:
time: 78.2 us; the launch traced here: 78 us
  starting transfers between devices  32 us (41%)
  waiting for transfers between devices  24 us (31%)
  Pallas kernels  21.2 us (27%)
  between operations  0.81 us (1%)
    ppermute x12, waiting for transfers between devices, over_z(): return lax.ppermute(array, 'head', [(i, i ^ bits) for i in range(nz)])  17.5 us
    ppermute x16, starting transfers between devices, over_seq(): return lax.ppermute(array, 'seq', [(i, i ^ bits) for i in range(n_seq)])  16.3 us
    ppermute x12, starting transfers between devices, over_z(): return lax.ppermute(array, 'head', [(i, i ^ bits) for i in range(nz)])  15.7 us
    pallas_call x2, Pallas kernels, attention(): pl.pallas_call(functools.partial(attention_body, n_sum, n_cols, n_skip, f...  12.4 us
    ppermute x16, waiting for transfers between devices, over_seq(): return lax.ppermute(array, 'seq', [(i, i ^ bits) for i in range(n_seq)])  6.48 us
    pallas_call x1, Pallas kernels, settle(): pl.pallas_call(settle_body, in_specs=[in_smem, in_vmem, in_vmem], out_spe...  2.62 us
    pallas_call x1, Pallas kernels, pack(): pl.pallas_call(pack_body, in_specs=[in_smem] + [in_hbm] * 4, out_specs=[i...  2.24 us
    pallas_call x1, Pallas kernels, stage(): pl.pallas_call(functools.partial(stage_body, n_cols, nz, n_sum), in_specs...  2.1 us
  transfers between devices with their start and end apart: 28, of which 13 were waited for; matrix products, arithmetic and copies ran while one was open for 0% of the time, Pallas kernels for 22%

profile of v5, /device:TPU:0, one launch (start us, length us, event | category | flops | bytes accessed | tf_op | source)
XLA Modules:
  0.0 78.0 jit_solution(11476109801529347752)
XLA Ops:
  0.7 2.2 %pack.1 = (bf16[32,1024]{1,0:T(8,128)(2,1)S(1)}, bf16[32,1024]{1,0:T(8,128)(2,1)S(1)}, bf16[4,256,1024]{2,1,0:T(8,128)(2,1)S(1)}) custom-call(s32[2]{0:T(128)S(1)} %pad_add_fusion.place_ref, bf16[256,2048]{1,0:T(8,128)(2,1)} %refs_0_.3, bf16[256,2048]{1,0:T(8,128)(2,1)} %refs_1_.3, bf16[256,2048]{1,0:T(8,128)(2,1)} %refs_2_.3, bf16[256,2048]{1,0:T(8,128)(2,1)} %refs_3_.3), custom_call_target="tpu_custom_call" | custom-call | tf_op jit(solution)/shard_map/pack/pallas_call | solution.py:92
  4.7 2.8 %collective-permute-start.2 = (bf16[64,1024]{1,0:T(8,128)(2,1)S(1)}, bf16[64,1024]{1,0:T(8,128)(2,1)S(1)}, u32[]{:S(2)}, u32[]{:S(2)}) collective-permute-start(bf16[64,1024]{1,0:T(8,128)(2,1)S(1)} %join.4), channel_id=1, source_target_pairs={{0,1},{1,0},{2,3},{3,2},{4,5},{5,4},{6,7},{7,6},{8,9},{9,8},{10,11... | collective-permute-start | bytes 393224 | tf_op jit(solution)/shard_map/ppermute | solution.py:520
  7.5 2.5 %collective-permute-start.4 = (bf16[64,512]{1,0:T(8,128)(2,1)S(1)}, bf16[64,512]{1,0:T(8,128)(2,1)S(1)}, u32[]{:S(2)}, u32[]{:S(2)}) collective-permute-start(bf16[64,512]{1,0:T(8,128)(2,1)S(1)} %join.3.own_ref), channel_id=1, source_target_pairs={{0,3},{1,2},{2,1},{3,0},{4,7},{5,6},{6,5},{7,4},{8,11},{9,10},{10,... | collective-permute-start | bytes 196616 | tf_op jit(solution)/shard_map/ppermute | solution.py:520
  10.2 2.1 %stage.1 = (bf16[4,256,1024]{2,1,0:T(8,128)(2,1)S(1)}, f32[512,512]{1,0:T(8,128)S(1)}) custom-call(s32[2]{0:T(128)S(1)} %pad_add_fusion.place_ref, bf16[256,2048]{1,0:T(8,128)(2,1)} %refs_0_.3, bf16[256,2048]{1,0:T(8,128)(2,1)} %refs_1_.3, bf16[256,2048]{1,0:T(8,128)(2,1)} %refs_2_.3, bf16[256,2048]{1,0:T(8,128)(2,1)} %refs_3_.3), custom_call_target="tpu_custom_call" | custom-call | bytes 4194304 | tf_op jit(solution)/shard_map/stage/pallas_call | solution.py:146
  12.3 3.5 %collective-permute-done.4.refs_1_ = bf16[64,512]{1,0:T(8,128)(2,1)S(1)} collective-permute-done((bf16[64,512]{1,0:T(8,128)(2,1)S(1)}, bf16[64,512]{1,0:T(8,128)(2,1)S(1)}, u32[]{:S(2)}, u32[]{:S(2)}) %collective-permute-start.4) | collective-permute-done | bytes 65568 | tf_op jit(solution)/shard_map/ppermute | solution.py:520
  15.8 1.7 %collective-permute-done.3.refs_0_ = bf16[64,512]{1,0:T(8,128)(2,1)S(1)} collective-permute-done((bf16[64,512]{1,0:T(8,128)(2,1)S(1)}, bf16[64,512]{1,0:T(8,128)(2,1)S(1)}, u32[]{:S(2)}, u32[]{:S(2)}) %collective-permute-start.3) | collective-permute-done | bytes 65568 | tf_op jit(solution)/shard_map/ppermute | solution.py:520
  17.5 2.5 %collective-permute-start.7 = (bf16[4,64,512]{2,1,0:T(8,128)(2,1)S(1)}, bf16[4,64,512]{2,1,0:T(8,128)(2,1)S(1)}, u32[]{:S(2)}, u32[]{:S(2)}) collective-permute-start(bf16[4,64,512]{2,1,0:T(8,128)(2,1)S(1)} %line.2.refs_0_.refs_3_), channel_id=1, source_target_pairs={{0,24},{4,28},{8,16},{12,20},{16,8},{20,12},{24,0},{28,4},{1,25},{... | collective-permute-start | bytes 786440 | tf_op jit(solution)/shard_map/ppermute | solution.py:523
  21.1 2.0 %collective-permute-start.6 = (bf16[64,512]{1,0:T(8,128)(2,1)S(1)}, bf16[64,512]{1,0:T(8,128)(2,1)S(1)}, u32[]{:S(2)}, u32[]{:S(2)}) collective-permute-start(bf16[64,512]{1,0:T(8,128)(2,1)S(1)} %join.5.own_ref), channel_id=1, source_target_pairs={{0,3},{1,2},{2,1},{3,0},{4,7},{5,6},{6,5},{7,4},{8,11},{9,10},{10,... | collective-permute-start | bytes 196616 | tf_op jit(solution)/shard_map/ppermute | solution.py:520
  23.1 4.1 %collective-permute-done.6.refs_1_ = bf16[64,512]{1,0:T(8,128)(2,1)S(1)} collective-permute-done((bf16[64,512]{1,0:T(8,128)(2,1)S(1)}, bf16[64,512]{1,0:T(8,128)(2,1)S(1)}, u32[]{:S(2)}, u32[]{:S(2)}) %collective-permute-start.6) | collective-permute-done | bytes 65568 | tf_op jit(solution)/shard_map/ppermute | solution.py:520
  27.2 1.5 %collective-permute-done.5.refs_0_ = bf16[64,512]{1,0:T(8,128)(2,1)S(1)} collective-permute-done((bf16[64,512]{1,0:T(8,128)(2,1)S(1)}, bf16[64,512]{1,0:T(8,128)(2,1)S(1)}, u32[]{:S(2)}, u32[]{:S(2)}) %collective-permute-start.5) | collective-permute-done | bytes 65568 | tf_op jit(solution)/shard_map/ppermute | solution.py:520
  28.7 1.6 %collective-permute-start.9 = (bf16[4,64,512]{2,1,0:T(8,128)(2,1)S(1)}, bf16[4,64,512]{2,1,0:T(8,128)(2,1)S(1)}, u32[]{:S(2)}, u32[]{:S(2)}) collective-permute-start(bf16[4,64,512]{2,1,0:T(8,128)(2,1)S(1)} %line.3.refs_7_.refs_3_), channel_id=1, source_target_pairs={{0,16},{4,20},{8,24},{12,28},{16,0},{20,4},{24,8},{28,12},{1,17},{... | collective-permute-start | bytes 786440 | tf_op jit(solution)/shard_map/ppermute | solution.py:523
  30.3 1.5 %collective-permute-start.8 = (bf16[4,64,512]{2,1,0:T(8,128)(2,1)S(1)}, bf16[4,64,512]{2,1,0:T(8,128)(2,1)S(1)}, u32[]{:S(2)}, u32[]{:S(2)}) collective-permute-start(bf16[4,64,512]{2,1,0:T(8,128)(2,1)S(1)} %line.3.refs_7_.refs_3_), channel_id=1, source_target_pairs={{0,8},{4,12},{8,0},{12,4},{16,24},{20,28},{24,16},{28,20},{1,9},{5... | collective-permute-start | bytes 786440 | tf_op jit(solution)/shard_map/ppermute | solution.py:523
  32.3 6.2 %attention.2 = (bf16[4,256,1024]{2,1,0:T(8,128)(2,1)S(1)}, bf16[4,256,1024]{2,1,0:T(8,128)(2,1)S(1)}, f32[2,64,512]{2,1,0:T(8,128)S(1)}, bf16[4,64,512]{2,1,0:T(...) custom-call(bf16[4,256,1024]{2,1,0:T(8,128)(2,1)S(1)} %get-tuple-ele, ...), custom_call_target="tpu_custom_call" | custom-call | flops 2013265920 | bytes 6291456 | tf_op jit(solution)/shard_map/attention/pallas_call | solution.py:273
  41.7 1.9 %collective-permute-done.13.came_ref = bf16[2,64,512]{2,1,0:T(8,128)(2,1)S(1)} collective-permute-done((bf16[2,64,512]{2,1,0:T(8,128)(2,1)S(1)}, bf16[2,64,512]{2,1,0:T(8,128)(2,1)S(1)}, u32[]{:S(2)}, u32[]{:S(2)}) %collective-permute-start.13) | collective-permute-done | bytes 131104 | tf_op jit(solution)/shard_map/ppermute | solution.py:520
  43.6 2.5 %collective-permute-start.19 = (bf16[2,64,512]{2,1,0:T(8,128)(2,1)S(1)}, bf16[2,64,512]{2,1,0:T(8,128)(2,1)S(1)}, u32[]{:S(2)}, u32[]{:S(2)}) collective-permute-start(bf16[2,64,512]{2,1,0:T(8,128)(2,1)S(1)} %pair_sum.2.refs_9_), channel_id=1, source_target_pairs={{0,24},{4,28},{8,16},{12,20},{16,8},{20,12},{24,0},{28,4},{1,25},{... | collective-permute-start | bytes 393224 | tf_op jit(solution)/shard_map/ppermute | solution.py:523
  46.1 6.2 %attention.3 = (bf16[4,256,1024]{2,1,0:T(8,128)(2,1)S(1)}, bf16[4,256,1024]{2,1,0:T(8,128)(2,1)S(1)}, f32[2,64,512]{2,1,0:T(8,128)S(1)}, bf16[4,64,512]{2,1,0:T(...) custom-call(bf16[4,256,1024]{2,1,0:T(8,128)(2,1)S(1)} %get-tuple-ele, ...), custom_call_target="tpu_custom_call", output_to_operand_aliasing={{0}: (7, {}), {1}: (8, {})} | custom-call | flops 2013265920 | bytes 6291456 | tf_op jit(solution)/shard_map/attention/pallas_call | solution.py:273
  53.2 1.4 %collective-permute-start.17 = (bf16[4,64,512]{2,1,0:T(8,128)(2,1)S(1)}, bf16[4,64,512]{2,1,0:T(8,128)(2,1)S(1)}, u32[]{:S(2)}, u32[]{:S(2)}) collective-permute-start(bf16[4,64,512]{2,1,0:T(8,128)(2,1)S(1)} %hold.11), channel_id=1, source_target_pairs={{0,16},{4,20},{8,24},{12,28},{16,0},{20,4},{24,8},{28,12},{1,17},{... | collective-permute-start | bytes 786440 | tf_op jit(solution)/shard_map/ppermute | solution.py:523
  54.7 2.0 %collective-permute-start.21 = (bf16[2,64,512]{2,1,0:T(8,128)(2,1)S(1)}, bf16[2,64,512]{2,1,0:T(8,128)(2,1)S(1)}, u32[]{:S(2)}, u32[]{:S(2)}) collective-permute-start(bf16[2,64,512]{2,1,0:T(8,128)(2,1)S(1)} %get-tuple-element.65), channel_id=1, source_target_pairs={{0,1},{1,0},{2,3},{3,2},{4,5},{5,4},{6,7},{7,6},{8,9},{9,8},{10,11... | collective-permute-start | bytes 393224 | tf_op jit(solution)/shard_map/ppermute | solution.py:520
  61.0 3.0 %collective-permute-done.20.refs_3_ = bf16[2,64,512]{2,1,0:T(8,128)(2,1)S(1)} collective-permute-done((bf16[2,64,512]{2,1,0:T(8,128)(2,1)S(1)}, bf16[2,64,512]{2,1,0:T(8,128)(2,1)S(1)}, u32[]{:S(2)}, u32[]{:S(2)}) %collective-permute-start.20) | collective-permute-done | bytes 131104 | tf_op jit(solution)/shard_map/ppermute | solution.py:523
  65.1 2.1 %collective-permute-start.24 = (bf16[64,512]{1,0:T(8,128)(2,1)S(1)}, bf16[64,512]{1,0:T(8,128)(2,1)S(1)}, u32[]{:S(2)}, u32[]{:S(2)}) collective-permute-start(bf16[64,512]{1,0:T(8,128)(2,1)S(1)} %get-tuple-element.74), channel_id=1, source_target_pairs={{0,1},{1,0},{2,3},{3,2},{4,5},{5,4},{6,7},{7,6},{8,9},{9,8},{10,11... | collective-permute-start | bytes 196616 | tf_op jit(solution)/shard_map/ppermute | solution.py:520
  67.3 2.3 %collective-permute-start.26 = (bf16[64,512]{1,0:T(8,128)(2,1)S(1)}, bf16[64,512]{1,0:T(8,128)(2,1)S(1)}, u32[]{:S(2)}, u32[]{:S(2)}) collective-permute-start(bf16[64,512]{1,0:T(8,128)(2,1)S(1)} %get-tuple-element.76), channel_id=1, source_target_pairs={{0,3},{1,2},{2,1},{3,0},{4,7},{5,6},{6,5},{7,4},{8,11},{9,10},{10,... | collective-permute-start | bytes 196616 | tf_op jit(solution)/shard_map/ppermute | solution.py:520
  69.6 2.6 %settle.1 = (bf16[256,2048]{1,0:T(8,128)(2,1)}, bf16[256,2048]{1,0:T(8,128)(2,1)}, bf16[256,2048]{1,0:T(8,128)(2,1)}, bf16[256,2048]{1,0:T(8,128)(2,1)}, f32[8,128]{1,0:T(8,128)S(1)}) custom-call(s32[2]{0:T(128)S(1)} %pad_add_fusion.place_ref, bf16[4,256,1024]{2,1,0:T(8,128)(2,1)S(1)} %get-tuple-element.52.own_ref, ...), custom_call_target="tpu_custom_call" | custom-call | tf_op jit(solution)/shard_map/settle/pallas_call | solution.py:463
  72.2 3.0 %collective-permute-done.25.refs_6_ = bf16[64,512]{1,0:T(8,128)(2,1)S(1)} collective-permute-done((bf16[64,512]{1,0:T(8,128)(2,1)S(1)}, bf16[64,512]{1,0:T(8,128)(2,1)S(1)}, u32[]{:S(2)}, u32[]{:S(2)}) %collective-permute-start.25) | collective-permute-done | bytes 65568 | tf_op jit(solution)/shard_map/ppermute | solution.py:520
  75.4 1.3 %collective-permute-done.27.refs_3_ = bf16[64,1024]{1,0:T(8,128)(2,1)S(1)} collective-permute-done((bf16[64,1024]{1,0:T(8,128)(2,1)S(1)}, bf16[64,1024]{1,0:T(8,128)(2,1)S(1)}, u32[]{:S(2)}, u32[]{:S(2)}) %collective-permute-start.27) | collective-permute-done | bytes 131104 | tf_op jit(solution)/shard_map/ppermute | solution.py:523
  (57 shorter events, 14.7 us)
Async XLA Ops:
  4.4 13.1 %collective-permute-start.1 = (bf16[4,256,1024]{2,1,0:T(8,128)(2,1)S(1)}, bf16[4,256,1024]{2,1,0:T(8,128)(2,1)S(1)}, u32[]{:S(2)}, u32[]{:S(2)}) collective-permute-start(bf16[4,256,1024]{2,1,0:T(8,128)(2,1)S(1)} %hold.7), channel_id=1, source_target_pairs={{0,4},{4,0},{8,12},{12,8},{16,20},{20,16},{24,28},{28,24},{1,5},{5... | collective-permute-start | bytes 6291464 | tf_op jit(solution)/shard_map/ppermute | solution.py:523
  4.7 12.7 %collective-permute-start.2 = (bf16[64,1024]{1,0:T(8,128)(2,1)S(1)}, bf16[64,1024]{1,0:T(8,128)(2,1)S(1)}, u32[]{:S(2)}, u32[]{:S(2)}) collective-permute-start(bf16[64,1024]{1,0:T(8,128)(2,1)S(1)} %join.4), channel_id=1, source_target_pairs={{0,1},{1,0},{2,3},{3,2},{4,5},{5,4},{6,7},{7,6},{8,9},{9,8},{10,11... | collective-permute-start | bytes 393224 | tf_op jit(solution)/shard_map/ppermute | solution.py:520
  7.5 8.3 %collective-permute-start.4 = (bf16[64,512]{1,0:T(8,128)(2,1)S(1)}, bf16[64,512]{1,0:T(8,128)(2,1)S(1)}, u32[]{:S(2)}, u32[]{:S(2)}) collective-permute-start(bf16[64,512]{1,0:T(8,128)(2,1)S(1)} %join.3.own_ref), channel_id=1, source_target_pairs={{0,3},{1,2},{2,1},{3,0},{4,7},{5,6},{6,5},{7,4},{8,11},{9,10},{10,... | collective-permute-start | bytes 196616 | tf_op jit(solution)/shard_map/ppermute | solution.py:520
  10.0 7.4 %collective-permute-start.3 = (bf16[64,512]{1,0:T(8,128)(2,1)S(1)}, bf16[64,512]{1,0:T(8,128)(2,1)S(1)}, u32[]{:S(2)}, u32[]{:S(2)}) collective-permute-start(bf16[64,512]{1,0:T(8,128)(2,1)S(1)} %join.3.own_ref), channel_id=1, source_target_pairs={{0,2},{1,3},{2,0},{3,1},{4,6},{5,7},{6,4},{7,5},{8,10},{9,11},{10,... | collective-permute-start | bytes 196616 | tf_op jit(solution)/shard_map/ppermute | solution.py:520
  17.5 11.2 %collective-permute-start.7 = (bf16[4,64,512]{2,1,0:T(8,128)(2,1)S(1)}, bf16[4,64,512]{2,1,0:T(8,128)(2,1)S(1)}, u32[]{:S(2)}, u32[]{:S(2)}) collective-permute-start(bf16[4,64,512]{2,1,0:T(8,128)(2,1)S(1)} %line.2.refs_0_.refs_3_), channel_id=1, source_target_pairs={{0,24},{4,28},{8,16},{12,20},{16,8},{20,12},{24,0},{28,4},{1,25},{... | collective-permute-start | bytes 786440 | tf_op jit(solution)/shard_map/ppermute | solution.py:523
  20.0 12.3 %collective-permute-start.12 = (bf16[4,64,512]{2,1,0:T(8,128)(2,1)S(1)}, bf16[4,64,512]{2,1,0:T(8,128)(2,1)S(1)}, u32[]{:S(2)}, u32[]{:S(2)}) collective-permute-start(bf16[4,64,512]{2,1,0:T(8,128)(2,1)S(1)} %line.2.refs_0_.refs_3_), channel_id=1, source_target_pairs={{0,16},{4,20},{8,24},{12,28},{16,0},{20,4},{24,8},{28,12},{1,17},{... | collective-permute-start | bytes 786440 | tf_op jit(solution)/shard_map/ppermute | solution.py:523
  20.5 11.8 %collective-permute-start.11 = (bf16[4,64,512]{2,1,0:T(8,128)(2,1)S(1)}, bf16[4,64,512]{2,1,0:T(8,128)(2,1)S(1)}, u32[]{:S(2)}, u32[]{:S(2)}) collective-permute-start(bf16[4,64,512]{2,1,0:T(8,128)(2,1)S(1)} %line.2.refs_0_.refs_3_), channel_id=1, source_target_pairs={{0,8},{4,12},{8,0},{12,4},{16,24},{20,28},{24,16},{28,20},{1,9},{5... | collective-permute-start | bytes 786440 | tf_op jit(solution)/shard_map/ppermute | solution.py:523
  21.1 6.2 %collective-permute-start.6 = (bf16[64,512]{1,0:T(8,128)(2,1)S(1)}, bf16[64,512]{1,0:T(8,128)(2,1)S(1)}, u32[]{:S(2)}, u32[]{:S(2)}) collective-permute-start(bf16[64,512]{1,0:T(8,128)(2,1)S(1)} %join.5.own_ref), channel_id=1, source_target_pairs={{0,3},{1,2},{2,1},{3,0},{4,7},{5,6},{6,5},{7,4},{8,11},{9,10},{10,... | collective-permute-start | bytes 196616 | tf_op jit(solution)/shard_map/ppermute | solution.py:520
  23.1 5.6 %collective-permute-start.5 = (bf16[64,512]{1,0:T(8,128)(2,1)S(1)}, bf16[64,512]{1,0:T(8,128)(2,1)S(1)}, u32[]{:S(2)}, u32[]{:S(2)}) collective-permute-start(bf16[64,512]{1,0:T(8,128)(2,1)S(1)} %join.5.own_ref), channel_id=1, source_target_pairs={{0,2},{1,3},{2,0},{3,1},{4,6},{5,7},{6,4},{7,5},{8,10},{9,11},{10,... | collective-permute-start | bytes 196616 | tf_op jit(solution)/shard_map/ppermute | solution.py:520
  28.7 10.6 %collective-permute-start.9 = (bf16[4,64,512]{2,1,0:T(8,128)(2,1)S(1)}, bf16[4,64,512]{2,1,0:T(8,128)(2,1)S(1)}, u32[]{:S(2)}, u32[]{:S(2)}) collective-permute-start(bf16[4,64,512]{2,1,0:T(8,128)(2,1)S(1)} %line.3.refs_7_.refs_3_), channel_id=1, source_target_pairs={{0,16},{4,20},{8,24},{12,28},{16,0},{20,4},{24,8},{28,12},{1,17},{... | collective-permute-start | bytes 786440 | tf_op jit(solution)/shard_map/ppermute | solution.py:523
  30.3 10.2 %collective-permute-start.8 = (bf16[4,64,512]{2,1,0:T(8,128)(2,1)S(1)}, bf16[4,64,512]{2,1,0:T(8,128)(2,1)S(1)}, u32[]{:S(2)}, u32[]{:S(2)}) collective-permute-start(bf16[4,64,512]{2,1,0:T(8,128)(2,1)S(1)} %line.3.refs_7_.refs_3_), channel_id=1, source_target_pairs={{0,8},{4,12},{8,0},{12,4},{16,24},{20,28},{24,16},{28,20},{1,9},{5... | collective-permute-start | bytes 786440 | tf_op jit(solution)/shard_map/ppermute | solution.py:523
  31.8 14.3 %collective-permute-start.10 = (bf16[4,64,512]{2,1,0:T(8,128)(2,1)S(1)}, bf16[4,64,512]{2,1,0:T(8,128)(2,1)S(1)}, u32[]{:S(2)}, u32[]{:S(2)}) collective-permute-start(bf16[4,64,512]{2,1,0:T(8,128)(2,1)S(1)} %line.3.refs_7_.refs_3_), channel_id=1, source_target_pairs={{0,24},{4,28},{8,16},{12,20},{16,8},{20,12},{24,0},{28,4},{1,25},{... | collective-permute-start | bytes 786440 | tf_op jit(solution)/shard_map/ppermute | solution.py:523
  39.3 13.0 %collective-permute-start.16 = (bf16[4,64,512]{2,1,0:T(8,128)(2,1)S(1)}, bf16[4,64,512]{2,1,0:T(8,128)(2,1)S(1)}, u32[]{:S(2)}, u32[]{:S(2)}) collective-permute-start(bf16[4,64,512]{2,1,0:T(8,128)(2,1)S(1)} %hold.10), channel_id=1, source_target_pairs={{0,16},{4,20},{8,24},{12,28},{16,0},{20,4},{24,8},{28,12},{1,17},{... | collective-permute-start | bytes 786440 | tf_op jit(solution)/shard_map/ppermute | solution.py:523
  40.5 11.9 %collective-permute-start.14 = (bf16[4,64,512]{2,1,0:T(8,128)(2,1)S(1)}, bf16[4,64,512]{2,1,0:T(8,128)(2,1)S(1)}, u32[]{:S(2)}, u32[]{:S(2)}) collective-permute-start(bf16[4,64,512]{2,1,0:T(8,128)(2,1)S(1)} %hold.8), channel_id=1, source_target_pairs={{0,8},{4,12},{8,0},{12,4},{16,24},{20,28},{24,16},{28,20},{1,9},{5... | collective-permute-start | bytes 786440 | tf_op jit(solution)/shard_map/ppermute | solution.py:523
  43.6 11.0 %collective-permute-start.19 = (bf16[2,64,512]{2,1,0:T(8,128)(2,1)S(1)}, bf16[2,64,512]{2,1,0:T(8,128)(2,1)S(1)}, u32[]{:S(2)}, u32[]{:S(2)}) collective-permute-start(bf16[2,64,512]{2,1,0:T(8,128)(2,1)S(1)} %pair_sum.2.refs_9_), channel_id=1, source_target_pairs={{0,24},{4,28},{8,16},{12,20},{16,8},{20,12},{24,0},{28,4},{1,25},{... | collective-permute-start | bytes 393224 | tf_op jit(solution)/shard_map/ppermute | solution.py:523
  52.4 5.6 %collective-permute-start.18 = (bf16[2,64,512]{2,1,0:T(8,128)(2,1)S(1)}, bf16[2,64,512]{2,1,0:T(8,128)(2,1)S(1)}, u32[]{:S(2)}, u32[]{:S(2)}) collective-permute-start(bf16[2,64,512]{2,1,0:T(8,128)(2,1)S(1)} %hold.12), channel_id=1, source_target_pairs={{0,1},{1,0},{2,3},{3,2},{4,5},{5,4},{6,7},{7,6},{8,9},{9,8},{10,11... | collective-permute-start | bytes 393224 | tf_op jit(solution)/shard_map/ppermute | solution.py:520
  52.5 7.8 %collective-permute-start.15 = (bf16[4,64,512]{2,1,0:T(8,128)(2,1)S(1)}, bf16[4,64,512]{2,1,0:T(8,128)(2,1)S(1)}, u32[]{:S(2)}, u32[]{:S(2)}) collective-permute-start(bf16[4,64,512]{2,1,0:T(8,128)(2,1)S(1)} %hold.9), channel_id=1, source_target_pairs={{0,8},{4,12},{8,0},{12,4},{16,24},{20,28},{24,16},{28,20},{1,9},{5... | collective-permute-start | bytes 786440 | tf_op jit(solution)/shard_map/ppermute | solution.py:523
  53.2 7.8 %collective-permute-start.17 = (bf16[4,64,512]{2,1,0:T(8,128)(2,1)S(1)}, bf16[4,64,512]{2,1,0:T(8,128)(2,1)S(1)}, u32[]{:S(2)}, u32[]{:S(2)}) collective-permute-start(bf16[4,64,512]{2,1,0:T(8,128)(2,1)S(1)} %hold.11), channel_id=1, source_target_pairs={{0,16},{4,20},{8,24},{12,28},{16,0},{20,4},{24,8},{28,12},{1,17},{... | collective-permute-start | bytes 786440 | tf_op jit(solution)/shard_map/ppermute | solution.py:523
  58.0 5.9 %collective-permute-start.20 = (bf16[2,64,512]{2,1,0:T(8,128)(2,1)S(1)}, bf16[2,64,512]{2,1,0:T(8,128)(2,1)S(1)}, u32[]{:S(2)}, u32[]{:S(2)}) collective-permute-start(bf16[2,64,512]{2,1,0:T(8,128)(2,1)S(1)} %pair_sum.3), channel_id=1, source_target_pairs={{0,24},{4,28},{8,16},{12,20},{16,8},{20,12},{24,0},{28,4},{1,25},{... | collective-permute-start | bytes 393224 | tf_op jit(solution)/shard_map/ppermute | solution.py:523
  64.1 5.5 %collective-permute-start.22 = (bf16[4,256,1024]{2,1,0:T(8,128)(2,1)S(1)}, bf16[4,256,1024]{2,1,0:T(8,128)(2,1)S(1)}, u32[]{:S(2)}, u32[]{:S(2)}) collective-permute-start(bf16[4,256,1024]{2,1,0:T(8,128)(2,1)S(1)} %hold.13), channel_id=1, source_target_pairs={{0,4},{4,0},{8,12},{12,8},{16,20},{20,16},{24,28},{28,24},{1,5},{5... | collective-permute-start | bytes 6291464 | tf_op jit(solution)/shard_map/ppermute | solution.py:523
  64.2 8.0 %collective-permute-start.23 = (bf16[1,64,512]{2,1,0:T(8,128)(2,1)S(1)}, bf16[1,64,512]{2,1,0:T(8,128)(2,1)S(1)}, u32[]{:S(2)}, u32[]{:S(2)}) collective-permute-start(bf16[1,64,512]{2,1,0:T(8,128)(2,1)S(1)} %get-tuple-element.73), channel_id=1, source_target_pairs={{0,2},{1,3},{2,0},{3,1},{4,6},{5,7},{6,4},{7,5},{8,10},{9,11},{10,... | collective-permute-start | bytes 196616 | tf_op jit(solution)/shard_map/ppermute | solution.py:520
  65.1 7.1 %collective-permute-start.24 = (bf16[64,512]{1,0:T(8,128)(2,1)S(1)}, bf16[64,512]{1,0:T(8,128)(2,1)S(1)}, u32[]{:S(2)}, u32[]{:S(2)}) collective-permute-start(bf16[64,512]{1,0:T(8,128)(2,1)S(1)} %get-tuple-element.74), channel_id=1, source_target_pairs={{0,1},{1,0},{2,3},{3,2},{4,5},{5,4},{6,7},{7,6},{8,9},{9,8},{10,11... | collective-permute-start | bytes 196616 | tf_op jit(solution)/shard_map/ppermute | solution.py:520
  67.2 8.1 %collective-permute-start.25 = (bf16[64,512]{1,0:T(8,128)(2,1)S(1)}, bf16[64,512]{1,0:T(8,128)(2,1)S(1)}, u32[]{:S(2)}, u32[]{:S(2)}) collective-permute-start(bf16[64,512]{1,0:T(8,128)(2,1)S(1)} %get-tuple-element.75), channel_id=1, source_target_pairs={{0,2},{1,3},{2,0},{3,1},{4,6},{5,7},{6,4},{7,5},{8,10},{9,11},{10,... | collective-permute-start | bytes 196616 | tf_op jit(solution)/shard_map/ppermute | solution.py:520
  67.3 8.0 %collective-permute-start.26 = (bf16[64,512]{1,0:T(8,128)(2,1)S(1)}, bf16[64,512]{1,0:T(8,128)(2,1)S(1)}, u32[]{:S(2)}, u32[]{:S(2)}) collective-permute-start(bf16[64,512]{1,0:T(8,128)(2,1)S(1)} %get-tuple-element.76), channel_id=1, source_target_pairs={{0,3},{1,2},{2,1},{3,0},{4,7},{5,6},{6,5},{7,4},{8,11},{9,10},{10,... | collective-permute-start | bytes 196616 | tf_op jit(solution)/shard_map/ppermute | solution.py:520
  (4 other events, 12.9 us)

commit v6 on v5

--- a/solution.py
+++ b/solution.py
@@ -384,6 +384,24 @@
     )(*parts, *after)
 
 
+def total_body(n, *refs):
+    total = refs[0][...]
+    for ref in refs[1:n]:
+        total = total + ref[...].astype(jnp.float32)
+    refs[-1][...] = total
+
+
+def total_of(parts, *after):
+    return pl.pallas_call(
+        functools.partial(total_body, len(parts)),
+        in_specs=[in_vmem] * (len(parts) + len(after)),
+        out_specs=in_vmem,
+        out_shape=jax.ShapeDtypeStruct(parts[0].shape, jnp.float32),
+        compiler_params=params,
+        name="total",
+    )(*parts, *after)
+
+
 def fold_body(n, *refs):
     keeps, came, out_refs = refs[:n], refs[n], refs[n + 1 :]
     totals = [
@@ -578,12 +596,13 @@
                 bits *= 2
             chunks.append([back[0], keeps[0], over_z(give_z, bits)])
         back = near, parts[:1] + moved
-    ends = column_sum(back[1], True, chunks[-1][1])
-    chunks.append([back[0], ends[0], over_z(ends[1], 1)] + swap_far(ends))
+    ends = column_sum(back[1], True, *chunks[-1][2:])
+    pair, far = over_z(ends[1], 1), swap_far(ends)
     own, sent = results
     (sent,) = hold([sent], ends[0])
     *results, mark = settle(place, own, over_seq(sent, 1))
-    own, away = edge(chunks, mark)
+    chunks.append([back[0], total_of([ends[0]] + far, mark), pair])
+    own, away = edge(chunks)
     attended, grad_queries, dk, dv = results
     edges = [own, over_seq(away, 1)]
     grad_keys, grad_values = finish(place, dk, dv, edges)

time: 78.2 us -> 78 us (level)
  waiting for transfers between devices: 24 us -> 22.1 us
  starting transfers between devices: 32 us -> 33.7 us
    ppermute x16, waiting for transfers between devices: 6.48 us -> 2.27 us  [over_seq(): return lax.ppermute(array, 'seq', [(i, i ^ bits) for i in range(n_seq)])]
    ppermute x12, waiting for transfers between devices: 17.5 us -> 19.8 us  [over_z(): return lax.ppermute(array, 'head', [(i, i ^ bits) for i in range(nz)])]
    ppermute x12, starting transfers between devices: 15.7 us -> 17.4 us  [over_z(): return lax.ppermute(array, 'head', [(i, i ^ bits) for i in range(nz)])]
where the time goes in v6:
time: 78 us; the launch traced here: 77.8 us
  starting transfers between devices  33.7 us (43%)
  waiting for transfers between devices  22.1 us (28%)
  Pallas kernels  21.2 us (27%)
  between operations  0.8 us (1%)
    ppermute x12, waiting for transfers between devices, over_z(): return lax.ppermute(array, 'head', [(i, i ^ bits) for i in range(nz)])  19.8 us
    ppermute x12, starting transfers between devices, over_z(): return lax.ppermute(array, 'head', [(i, i ^ bits) for i in range(nz)])  17.4 us
    ppermute x16, starting transfers between devices, over_seq(): return lax.ppermute(array, 'seq', [(i, i ^ bits) for i in range(n_seq)])  16.3 us
    pallas_call x2, Pallas kernels, attention(): pl.pallas_call(functools.partial(attention_body, n_sum, n_cols, n_skip, f...  12.4 us
    pallas_call x1, Pallas kernels, settle(): pl.pallas_call(settle_body, in_specs=[in_smem, in_vmem, in_vmem], out_spe...  2.62 us
    ppermute x16, waiting for transfers between devices, over_seq(): return lax.ppermute(array, 'seq', [(i, i ^ bits) for i in range(n_seq)])  2.27 us
    pallas_call x1, Pallas kernels, pack(): pl.pallas_call(pack_body, in_specs=[in_smem] + [in_hbm] * 4, out_specs=[i...  2.24 us
    pallas_call x1, Pallas kernels, stage(): pl.pallas_call(functools.partial(stage_body, n_cols, nz, n_sum), in_specs...  2.1 us
  transfers between devices with their start and end apart: 28, of which 13 were waited for; matrix products, arithmetic and copies ran while one was open for 0% of the time, Pallas kernels for 22%

profile of v6, /device:TPU:0, one launch (start us, length us, event | category | flops | bytes accessed | tf_op | source)
XLA Modules:
  0.0 77.8 jit_solution(2764905396960155468)
XLA Ops:
  0.7 2.2 %pack.1 = (bf16[32,1024]{1,0:T(8,128)(2,1)S(1)}, bf16[32,1024]{1,0:T(8,128)(2,1)S(1)}, bf16[4,256,1024]{2,1,0:T(8,128)(2,1)S(1)}) custom-call(s32[2]{0:T(128)S(1)} %pad_add_fusion.place_ref, bf16[256,2048]{1,0:T(8,128)(2,1)} %refs_0_.3, bf16[256,2048]{1,0:T(8,128)(2,1)} %refs_1_.3, bf16[256,2048]{1,0:T(8,128)(2,1)} %refs_2_.3, bf16[256,2048]{1,0:T(8,128)(2,1)} %refs_3_.3), custom_call_target="tpu_custom_call" | custom-call | tf_op jit(solution)/shard_map/pack/pallas_call | solution.py:92
  4.7 2.8 %collective-permute-start.2 = (bf16[64,1024]{1,0:T(8,128)(2,1)S(1)}, bf16[64,1024]{1,0:T(8,128)(2,1)S(1)}, u32[]{:S(2)}, u32[]{:S(2)}) collective-permute-start(bf16[64,1024]{1,0:T(8,128)(2,1)S(1)} %join.4), channel_id=1, source_target_pairs={{0,1},{1,0},{2,3},{3,2},{4,5},{5,4},{6,7},{7,6},{8,9},{9,8},{10,11... | collective-permute-start | bytes 393224 | tf_op jit(solution)/shard_map/ppermute | solution.py:538
  7.5 2.5 %collective-permute-start.4 = (bf16[64,512]{1,0:T(8,128)(2,1)S(1)}, bf16[64,512]{1,0:T(8,128)(2,1)S(1)}, u32[]{:S(2)}, u32[]{:S(2)}) collective-permute-start(bf16[64,512]{1,0:T(8,128)(2,1)S(1)} %join.3.own_ref), channel_id=1, source_target_pairs={{0,3},{1,2},{2,1},{3,0},{4,7},{5,6},{6,5},{7,4},{8,11},{9,10},{10,... | collective-permute-start | bytes 196616 | tf_op jit(solution)/shard_map/ppermute | solution.py:538
  10.2 2.1 %stage.1 = (bf16[4,256,1024]{2,1,0:T(8,128)(2,1)S(1)}, f32[512,512]{1,0:T(8,128)S(1)}) custom-call(s32[2]{0:T(128)S(1)} %pad_add_fusion.place_ref, bf16[256,2048]{1,0:T(8,128)(2,1)} %refs_0_.3, bf16[256,2048]{1,0:T(8,128)(2,1)} %refs_1_.3, bf16[256,2048]{1,0:T(8,128)(2,1)} %refs_2_.3, bf16[256,2048]{1,0:T(8,128)(2,1)} %refs_3_.3), custom_call_target="tpu_custom_call" | custom-call | bytes 4194304 | tf_op jit(solution)/shard_map/stage/pallas_call | solution.py:146
  12.3 3.5 %collective-permute-done.4.refs_1_ = bf16[64,512]{1,0:T(8,128)(2,1)S(1)} collective-permute-done((bf16[64,512]{1,0:T(8,128)(2,1)S(1)}, bf16[64,512]{1,0:T(8,128)(2,1)S(1)}, u32[]{:S(2)}, u32[]{:S(2)}) %collective-permute-start.4) | collective-permute-done | bytes 65568 | tf_op jit(solution)/shard_map/ppermute | solution.py:538
  15.8 1.7 %collective-permute-done.3.refs_0_ = bf16[64,512]{1,0:T(8,128)(2,1)S(1)} collective-permute-done((bf16[64,512]{1,0:T(8,128)(2,1)S(1)}, bf16[64,512]{1,0:T(8,128)(2,1)S(1)}, u32[]{:S(2)}, u32[]{:S(2)}) %collective-permute-start.3) | collective-permute-done | bytes 65568 | tf_op jit(solution)/shard_map/ppermute | solution.py:538
  17.5 2.5 %collective-permute-start.7 = (bf16[4,64,512]{2,1,0:T(8,128)(2,1)S(1)}, bf16[4,64,512]{2,1,0:T(8,128)(2,1)S(1)}, u32[]{:S(2)}, u32[]{:S(2)}) collective-permute-start(bf16[4,64,512]{2,1,0:T(8,128)(2,1)S(1)} %line.2.refs_0_.refs_3_), channel_id=1, source_target_pairs={{0,24},{4,28},{8,16},{12,20},{16,8},{20,12},{24,0},{28,4},{1,25},{... | collective-permute-start | bytes 786440 | tf_op jit(solution)/shard_map/ppermute | solution.py:541
  21.1 2.0 %collective-permute-start.6 = (bf16[64,512]{1,0:T(8,128)(2,1)S(1)}, bf16[64,512]{1,0:T(8,128)(2,1)S(1)}, u32[]{:S(2)}, u32[]{:S(2)}) collective-permute-start(bf16[64,512]{1,0:T(8,128)(2,1)S(1)} %join.5.own_ref), channel_id=1, source_target_pairs={{0,3},{1,2},{2,1},{3,0},{4,7},{5,6},{6,5},{7,4},{8,11},{9,10},{10,... | collective-permute-start | bytes 196616 | tf_op jit(solution)/shard_map/ppermute | solution.py:538
  23.1 4.1 %collective-permute-done.6.refs_1_ = bf16[64,512]{1,0:T(8,128)(2,1)S(1)} collective-permute-done((bf16[64,512]{1,0:T(8,128)(2,1)S(1)}, bf16[64,512]{1,0:T(8,128)(2,1)S(1)}, u32[]{:S(2)}, u32[]{:S(2)}) %collective-permute-start.6) | collective-permute-done | bytes 65568 | tf_op jit(solution)/shard_map/ppermute | solution.py:538
  27.2 1.5 %collective-permute-done.5.refs_0_ = bf16[64,512]{1,0:T(8,128)(2,1)S(1)} collective-permute-done((bf16[64,512]{1,0:T(8,128)(2,1)S(1)}, bf16[64,512]{1,0:T(8,128)(2,1)S(1)}, u32[]{:S(2)}, u32[]{:S(2)}) %collective-permute-start.5) | collective-permute-done | bytes 65568 | tf_op jit(solution)/shard_map/ppermute | solution.py:538
  28.7 1.6 %collective-permute-start.9 = (bf16[4,64,512]{2,1,0:T(8,128)(2,1)S(1)}, bf16[4,64,512]{2,1,0:T(8,128)(2,1)S(1)}, u32[]{:S(2)}, u32[]{:S(2)}) collective-permute-start(bf16[4,64,512]{2,1,0:T(8,128)(2,1)S(1)} %line.3.refs_7_.refs_3_), channel_id=1, source_target_pairs={{0,16},{4,20},{8,24},{12,28},{16,0},{20,4},{24,8},{28,12},{1,17},{... | collective-permute-start | bytes 786440 | tf_op jit(solution)/shard_map/ppermute | solution.py:541
  30.3 1.5 %collective-permute-start.8 = (bf16[4,64,512]{2,1,0:T(8,128)(2,1)S(1)}, bf16[4,64,512]{2,1,0:T(8,128)(2,1)S(1)}, u32[]{:S(2)}, u32[]{:S(2)}) collective-permute-start(bf16[4,64,512]{2,1,0:T(8,128)(2,1)S(1)} %line.3.refs_7_.refs_3_), channel_id=1, source_target_pairs={{0,8},{4,12},{8,0},{12,4},{16,24},{20,28},{24,16},{28,20},{1,9},{5... | collective-permute-start | bytes 786440 | tf_op jit(solution)/shard_map/ppermute | solution.py:541
  32.3 6.2 %attention.2 = (bf16[4,256,1024]{2,1,0:T(8,128)(2,1)S(1)}, bf16[4,256,1024]{2,1,0:T(8,128)(2,1)S(1)}, f32[2,64,512]{2,1,0:T(8,128)S(1)}, bf16[4,64,512]{2,1,0:T(...) custom-call(bf16[4,256,1024]{2,1,0:T(8,128)(2,1)S(1)} %get-tuple-ele, ...), custom_call_target="tpu_custom_call" | custom-call | flops 2013265920 | bytes 6291456 | tf_op jit(solution)/shard_map/attention/pallas_call | solution.py:273
  41.7 1.9 %collective-permute-done.13.came_ref = bf16[2,64,512]{2,1,0:T(8,128)(2,1)S(1)} collective-permute-done((bf16[2,64,512]{2,1,0:T(8,128)(2,1)S(1)}, bf16[2,64,512]{2,1,0:T(8,128)(2,1)S(1)}, u32[]{:S(2)}, u32[]{:S(2)}) %collective-permute-start.13) | collective-permute-done | bytes 131104 | tf_op jit(solution)/shard_map/ppermute | solution.py:538
  43.6 2.5 %collective-permute-start.19 = (bf16[2,64,512]{2,1,0:T(8,128)(2,1)S(1)}, bf16[2,64,512]{2,1,0:T(8,128)(2,1)S(1)}, u32[]{:S(2)}, u32[]{:S(2)}) collective-permute-start(bf16[2,64,512]{2,1,0:T(8,128)(2,1)S(1)} %pair_sum.2.refs_9_), channel_id=1, source_target_pairs={{0,24},{4,28},{8,16},{12,20},{16,8},{20,12},{24,0},{28,4},{1,25},{... | collective-permute-start | bytes 393224 | tf_op jit(solution)/shard_map/ppermute | solution.py:541
  46.1 6.2 %attention.3 = (bf16[4,256,1024]{2,1,0:T(8,128)(2,1)S(1)}, bf16[4,256,1024]{2,1,0:T(8,128)(2,1)S(1)}, f32[2,64,512]{2,1,0:T(8,128)S(1)}, bf16[4,64,512]{2,1,0:T(...) custom-call(bf16[4,256,1024]{2,1,0:T(8,128)(2,1)S(1)} %get-tuple-ele, ...), custom_call_target="tpu_custom_call", output_to_operand_aliasing={{0}: (7, {}), {1}: (8, {})} | custom-call | flops 2013265920 | bytes 6291456 | tf_op jit(solution)/shard_map/attention/pallas_call | solution.py:273
  53.2 1.4 %collective-permute-start.17 = (bf16[4,64,512]{2,1,0:T(8,128)(2,1)S(1)}, bf16[4,64,512]{2,1,0:T(8,128)(2,1)S(1)}, u32[]{:S(2)}, u32[]{:S(2)}) collective-permute-start(bf16[4,64,512]{2,1,0:T(8,128)(2,1)S(1)} %hold.11), channel_id=1, source_target_pairs={{0,16},{4,20},{8,24},{12,28},{16,0},{20,4},{24,8},{28,12},{1,17},{... | collective-permute-start | bytes 786440 | tf_op jit(solution)/shard_map/ppermute | solution.py:541
  54.7 2.0 %collective-permute-start.21 = (bf16[2,64,512]{2,1,0:T(8,128)(2,1)S(1)}, bf16[2,64,512]{2,1,0:T(8,128)(2,1)S(1)}, u32[]{:S(2)}, u32[]{:S(2)}) collective-permute-start(bf16[2,64,512]{2,1,0:T(8,128)(2,1)S(1)} %get-tuple-element.65), channel_id=1, source_target_pairs={{0,1},{1,0},{2,3},{3,2},{4,5},{5,4},{6,7},{7,6},{8,9},{9,8},{10,11... | collective-permute-start | bytes 393224 | tf_op jit(solution)/shard_map/ppermute | solution.py:538
  59.8 2.7 %collective-permute-start.22 = (bf16[1,64,512]{2,1,0:T(8,128)(2,1)S(1)}, bf16[1,64,512]{2,1,0:T(8,128)(2,1)S(1)}, u32[]{:S(2)}, u32[]{:S(2)}) collective-permute-start(bf16[1,64,512]{2,1,0:T(8,128)(2,1)S(1)} %get-tuple-element.66), channel_id=1, source_target_pairs={{0,2},{1,3},{2,0},{3,1},{4,6},{5,7},{6,4},{7,5},{8,10},{9,11},{10,... | collective-permute-start | bytes 196616 | tf_op jit(solution)/shard_map/ppermute | solution.py:538
  62.4 2.6 %collective-permute-done.22.refs_4_.refs_2_ = bf16[1,64,512]{2,1,0:T(8,128)(2,1)S(1)} collective-permute-done((bf16[1,64,512]{2,1,0:T(8,128)(2,1)S(1)}, bf16[1,64,512]{2,1,0:T(8,128)(2,1)S(1)}, u32[]{:S(2)}, u32[]{:S(2)}) %collective-permute-start.22) | collective-permute-done | bytes 65568 | tf_op jit(solution)/shard_map/ppermute | solution.py:538
  65.2 2.7 %collective-permute-start.24 = (bf16[64,512]{1,0:T(8,128)(2,1)S(1)}, bf16[64,512]{1,0:T(8,128)(2,1)S(1)}, u32[]{:S(2)}, u32[]{:S(2)}) collective-permute-start(bf16[64,512]{1,0:T(8,128)(2,1)S(1)} %get-tuple-element.74), channel_id=1, source_target_pairs={{0,2},{1,3},{2,0},{3,1},{4,6},{5,7},{6,4},{7,5},{8,10},{9,11},{10,... | collective-permute-start | bytes 196616 | tf_op jit(solution)/shard_map/ppermute | solution.py:538
  67.9 1.7 %collective-permute-start.25 = (bf16[64,512]{1,0:T(8,128)(2,1)S(1)}, bf16[64,512]{1,0:T(8,128)(2,1)S(1)}, u32[]{:S(2)}, u32[]{:S(2)}) collective-permute-start(bf16[64,512]{1,0:T(8,128)(2,1)S(1)} %get-tuple-element.75), channel_id=1, source_target_pairs={{0,3},{1,2},{2,1},{3,0},{4,7},{5,6},{6,5},{7,4},{8,11},{9,10},{10,... | collective-permute-start | bytes 196616 | tf_op jit(solution)/shard_map/ppermute | solution.py:538
  69.6 2.6 %settle.1 = (bf16[256,2048]{1,0:T(8,128)(2,1)}, bf16[256,2048]{1,0:T(8,128)(2,1)}, bf16[256,2048]{1,0:T(8,128)(2,1)}, bf16[256,2048]{1,0:T(8,128)(2,1)}, f32[8,128]{1,0:T(8,128)S(1)}) custom-call(s32[2]{0:T(128)S(1)} %pad_add_fusion.place_ref, bf16[4,256,1024]{2,1,0:T(8,128)(2,1)S(1)} %get-tuple-element.52.own_ref, ...), custom_call_target="tpu_custom_call" | custom-call | tf_op jit(solution)/shard_map/settle/pallas_call | solution.py:481
  75.2 1.3 %collective-permute-done.27.refs_3_ = bf16[64,1024]{1,0:T(8,128)(2,1)S(1)} collective-permute-done((bf16[64,1024]{1,0:T(8,128)(2,1)S(1)}, bf16[64,1024]{1,0:T(8,128)(2,1)S(1)}, u32[]{:S(2)}, u32[]{:S(2)}) %collective-permute-start.27) | collective-permute-done | bytes 131104 | tf_op jit(solution)/shard_map/ppermute | solution.py:541
  (58 shorter events, 15.3 us)
Async XLA Ops:
  4.4 13.1 %collective-permute-start.1 = (bf16[4,256,1024]{2,1,0:T(8,128)(2,1)S(1)}, bf16[4,256,1024]{2,1,0:T(8,128)(2,1)S(1)}, u32[]{:S(2)}, u32[]{:S(2)}) collective-permute-start(bf16[4,256,1024]{2,1,0:T(8,128)(2,1)S(1)} %hold.7), channel_id=1, source_target_pairs={{0,4},{4,0},{8,12},{12,8},{16,20},{20,16},{24,28},{28,24},{1,5},{5... | collective-permute-start | bytes 6291464 | tf_op jit(solution)/shard_map/ppermute | solution.py:541
  4.7 12.7 %collective-permute-start.2 = (bf16[64,1024]{1,0:T(8,128)(2,1)S(1)}, bf16[64,1024]{1,0:T(8,128)(2,1)S(1)}, u32[]{:S(2)}, u32[]{:S(2)}) collective-permute-start(bf16[64,1024]{1,0:T(8,128)(2,1)S(1)} %join.4), channel_id=1, source_target_pairs={{0,1},{1,0},{2,3},{3,2},{4,5},{5,4},{6,7},{7,6},{8,9},{9,8},{10,11... | collective-permute-start | bytes 393224 | tf_op jit(solution)/shard_map/ppermute | solution.py:538
  7.5 8.3 %collective-permute-start.4 = (bf16[64,512]{1,0:T(8,128)(2,1)S(1)}, bf16[64,512]{1,0:T(8,128)(2,1)S(1)}, u32[]{:S(2)}, u32[]{:S(2)}) collective-permute-start(bf16[64,512]{1,0:T(8,128)(2,1)S(1)} %join.3.own_ref), channel_id=1, source_target_pairs={{0,3},{1,2},{2,1},{3,0},{4,7},{5,6},{6,5},{7,4},{8,11},{9,10},{10,... | collective-permute-start | bytes 196616 | tf_op jit(solution)/shard_map/ppermute | solution.py:538
  10.0 7.4 %collective-permute-start.3 = (bf16[64,512]{1,0:T(8,128)(2,1)S(1)}, bf16[64,512]{1,0:T(8,128)(2,1)S(1)}, u32[]{:S(2)}, u32[]{:S(2)}) collective-permute-start(bf16[64,512]{1,0:T(8,128)(2,1)S(1)} %join.3.own_ref), channel_id=1, source_target_pairs={{0,2},{1,3},{2,0},{3,1},{4,6},{5,7},{6,4},{7,5},{8,10},{9,11},{10,... | collective-permute-start | bytes 196616 | tf_op jit(solution)/shard_map/ppermute | solution.py:538
  17.5 11.2 %collective-permute-start.7 = (bf16[4,64,512]{2,1,0:T(8,128)(2,1)S(1)}, bf16[4,64,512]{2,1,0:T(8,128)(2,1)S(1)}, u32[]{:S(2)}, u32[]{:S(2)}) collective-permute-start(bf16[4,64,512]{2,1,0:T(8,128)(2,1)S(1)} %line.2.refs_0_.refs_3_), channel_id=1, source_target_pairs={{0,24},{4,28},{8,16},{12,20},{16,8},{20,12},{24,0},{28,4},{1,25},{... | collective-permute-start | bytes 786440 | tf_op jit(solution)/shard_map/ppermute | solution.py:541
  20.0 12.3 %collective-permute-start.12 = (bf16[4,64,512]{2,1,0:T(8,128)(2,1)S(1)}, bf16[4,64,512]{2,1,0:T(8,128)(2,1)S(1)}, u32[]{:S(2)}, u32[]{:S(2)}) collective-permute-start(bf16[4,64,512]{2,1,0:T(8,128)(2,1)S(1)} %line.2.refs_0_.refs_3_), channel_id=1, source_target_pairs={{0,16},{4,20},{8,24},{12,28},{16,0},{20,4},{24,8},{28,12},{1,17},{... | collective-permute-start | bytes 786440 | tf_op jit(solution)/shard_map/ppermute | solution.py:541
  20.5 11.8 %collective-permute-start.11 = (bf16[4,64,512]{2,1,0:T(8,128)(2,1)S(1)}, bf16[4,64,512]{2,1,0:T(8,128)(2,1)S(1)}, u32[]{:S(2)}, u32[]{:S(2)}) collective-permute-start(bf16[4,64,512]{2,1,0:T(8,128)(2,1)S(1)} %line.2.refs_0_.refs_3_), channel_id=1, source_target_pairs={{0,8},{4,12},{8,0},{12,4},{16,24},{20,28},{24,16},{28,20},{1,9},{5... | collective-permute-start | bytes 786440 | tf_op jit(solution)/shard_map/ppermute | solution.py:541
  21.1 6.2 %collective-permute-start.6 = (bf16[64,512]{1,0:T(8,128)(2,1)S(1)}, bf16[64,512]{1,0:T(8,128)(2,1)S(1)}, u32[]{:S(2)}, u32[]{:S(2)}) collective-permute-start(bf16[64,512]{1,0:T(8,128)(2,1)S(1)} %join.5.own_ref), channel_id=1, source_target_pairs={{0,3},{1,2},{2,1},{3,0},{4,7},{5,6},{6,5},{7,4},{8,11},{9,10},{10,... | collective-permute-start | bytes 196616 | tf_op jit(solution)/shard_map/ppermute | solution.py:538
  23.1 5.6 %collective-permute-start.5 = (bf16[64,512]{1,0:T(8,128)(2,1)S(1)}, bf16[64,512]{1,0:T(8,128)(2,1)S(1)}, u32[]{:S(2)}, u32[]{:S(2)}) collective-permute-start(bf16[64,512]{1,0:T(8,128)(2,1)S(1)} %join.5.own_ref), channel_id=1, source_target_pairs={{0,2},{1,3},{2,0},{3,1},{4,6},{5,7},{6,4},{7,5},{8,10},{9,11},{10,... | collective-permute-start | bytes 196616 | tf_op jit(solution)/shard_map/ppermute | solution.py:538
  28.7 10.6 %collective-permute-start.9 = (bf16[4,64,512]{2,1,0:T(8,128)(2,1)S(1)}, bf16[4,64,512]{2,1,0:T(8,128)(2,1)S(1)}, u32[]{:S(2)}, u32[]{:S(2)}) collective-permute-start(bf16[4,64,512]{2,1,0:T(8,128)(2,1)S(1)} %line.3.refs_7_.refs_3_), channel_id=1, source_target_pairs={{0,16},{4,20},{8,24},{12,28},{16,0},{20,4},{24,8},{28,12},{1,17},{... | collective-permute-start | bytes 786440 | tf_op jit(solution)/shard_map/ppermute | solution.py:541
  30.3 10.2 %collective-permute-start.8 = (bf16[4,64,512]{2,1,0:T(8,128)(2,1)S(1)}, bf16[4,64,512]{2,1,0:T(8,128)(2,1)S(1)}, u32[]{:S(2)}, u32[]{:S(2)}) collective-permute-start(bf16[4,64,512]{2,1,0:T(8,128)(2,1)S(1)} %line.3.refs_7_.refs_3_), channel_id=1, source_target_pairs={{0,8},{4,12},{8,0},{12,4},{16,24},{20,28},{24,16},{28,20},{1,9},{5... | collective-permute-start | bytes 786440 | tf_op jit(solution)/shard_map/ppermute | solution.py:541
  31.8 14.3 %collective-permute-start.10 = (bf16[4,64,512]{2,1,0:T(8,128)(2,1)S(1)}, bf16[4,64,512]{2,1,0:T(8,128)(2,1)S(1)}, u32[]{:S(2)}, u32[]{:S(2)}) collective-permute-start(bf16[4,64,512]{2,1,0:T(8,128)(2,1)S(1)} %line.3.refs_7_.refs_3_), channel_id=1, source_target_pairs={{0,24},{4,28},{8,16},{12,20},{16,8},{20,12},{24,0},{28,4},{1,25},{... | collective-permute-start | bytes 786440 | tf_op jit(solution)/shard_map/ppermute | solution.py:541
  38.5 5.0 %collective-permute-start.13 = (bf16[2,64,512]{2,1,0:T(8,128)(2,1)S(1)}, bf16[2,64,512]{2,1,0:T(8,128)(2,1)S(1)}, u32[]{:S(2)}, u32[]{:S(2)}) collective-permute-start(bf16[2,64,512]{2,1,0:T(8,128)(2,1)S(1)} %get-tuple-element.51), channel_id=1, source_target_pairs={{0,1},{1,0},{2,3},{3,2},{4,5},{5,4},{6,7},{7,6},{8,9},{9,8},{10,11... | collective-permute-start | bytes 393224 | tf_op jit(solution)/shard_map/ppermute | solution.py:538
  39.3 13.0 %collective-permute-start.16 = (bf16[4,64,512]{2,1,0:T(8,128)(2,1)S(1)}, bf16[4,64,512]{2,1,0:T(8,128)(2,1)S(1)}, u32[]{:S(2)}, u32[]{:S(2)}) collective-permute-start(bf16[4,64,512]{2,1,0:T(8,128)(2,1)S(1)} %hold.10), channel_id=1, source_target_pairs={{0,16},{4,20},{8,24},{12,28},{16,0},{20,4},{24,8},{28,12},{1,17},{... | collective-permute-start | bytes 786440 | tf_op jit(solution)/shard_map/ppermute | solution.py:541
  40.5 11.9 %collective-permute-start.14 = (bf16[4,64,512]{2,1,0:T(8,128)(2,1)S(1)}, bf16[4,64,512]{2,1,0:T(8,128)(2,1)S(1)}, u32[]{:S(2)}, u32[]{:S(2)}) collective-permute-start(bf16[4,64,512]{2,1,0:T(8,128)(2,1)S(1)} %hold.8), channel_id=1, source_target_pairs={{0,8},{4,12},{8,0},{12,4},{16,24},{20,28},{24,16},{28,20},{1,9},{5... | collective-permute-start | bytes 786440 | tf_op jit(solution)/shard_map/ppermute | solution.py:541
  43.6 11.0 %collective-permute-start.19 = (bf16[2,64,512]{2,1,0:T(8,128)(2,1)S(1)}, bf16[2,64,512]{2,1,0:T(8,128)(2,1)S(1)}, u32[]{:S(2)}, u32[]{:S(2)}) collective-permute-start(bf16[2,64,512]{2,1,0:T(8,128)(2,1)S(1)} %pair_sum.2.refs_9_), channel_id=1, source_target_pairs={{0,24},{4,28},{8,16},{12,20},{16,8},{20,12},{24,0},{28,4},{1,25},{... | collective-permute-start | bytes 393224 | tf_op jit(solution)/shard_map/ppermute | solution.py:541
  52.4 5.6 %collective-permute-start.18 = (bf16[2,64,512]{2,1,0:T(8,128)(2,1)S(1)}, bf16[2,64,512]{2,1,0:T(8,128)(2,1)S(1)}, u32[]{:S(2)}, u32[]{:S(2)}) collective-permute-start(bf16[2,64,512]{2,1,0:T(8,128)(2,1)S(1)} %hold.12), channel_id=1, source_target_pairs={{0,1},{1,0},{2,3},{3,2},{4,5},{5,4},{6,7},{7,6},{8,9},{9,8},{10,11... | collective-permute-start | bytes 393224 | tf_op jit(solution)/shard_map/ppermute | solution.py:538
  52.5 12.5 %collective-permute-start.15 = (bf16[4,64,512]{2,1,0:T(8,128)(2,1)S(1)}, bf16[4,64,512]{2,1,0:T(8,128)(2,1)S(1)}, u32[]{:S(2)}, u32[]{:S(2)}) collective-permute-start(bf16[4,64,512]{2,1,0:T(8,128)(2,1)S(1)} %hold.9), channel_id=1, source_target_pairs={{0,8},{4,12},{8,0},{12,4},{16,24},{20,28},{24,16},{28,20},{1,9},{5... | collective-permute-start | bytes 786440 | tf_op jit(solution)/shard_map/ppermute | solution.py:541
  53.2 11.8 %collective-permute-start.17 = (bf16[4,64,512]{2,1,0:T(8,128)(2,1)S(1)}, bf16[4,64,512]{2,1,0:T(8,128)(2,1)S(1)}, u32[]{:S(2)}, u32[]{:S(2)}) collective-permute-start(bf16[4,64,512]{2,1,0:T(8,128)(2,1)S(1)} %hold.11), channel_id=1, source_target_pairs={{0,16},{4,20},{8,24},{12,28},{16,0},{20,4},{24,8},{28,12},{1,17},{... | collective-permute-start | bytes 786440 | tf_op jit(solution)/shard_map/ppermute | solution.py:541
  58.0 7.0 %collective-permute-start.20 = (bf16[2,64,512]{2,1,0:T(8,128)(2,1)S(1)}, bf16[2,64,512]{2,1,0:T(8,128)(2,1)S(1)}, u32[]{:S(2)}, u32[]{:S(2)}) collective-permute-start(bf16[2,64,512]{2,1,0:T(8,128)(2,1)S(1)} %pair_sum.3), channel_id=1, source_target_pairs={{0,24},{4,28},{8,16},{12,20},{16,8},{20,12},{24,0},{28,4},{1,25},{... | collective-permute-start | bytes 393224 | tf_op jit(solution)/shard_map/ppermute | solution.py:541
  59.8 5.2 %collective-permute-start.22 = (bf16[1,64,512]{2,1,0:T(8,128)(2,1)S(1)}, bf16[1,64,512]{2,1,0:T(8,128)(2,1)S(1)}, u32[]{:S(2)}, u32[]{:S(2)}) collective-permute-start(bf16[1,64,512]{2,1,0:T(8,128)(2,1)S(1)} %get-tuple-element.66), channel_id=1, source_target_pairs={{0,2},{1,3},{2,0},{3,1},{4,6},{5,7},{6,4},{7,5},{8,10},{9,11},{10,... | collective-permute-start | bytes 196616 | tf_op jit(solution)/shard_map/ppermute | solution.py:538
  65.2 8.1 %collective-permute-start.24 = (bf16[64,512]{1,0:T(8,128)(2,1)S(1)}, bf16[64,512]{1,0:T(8,128)(2,1)S(1)}, u32[]{:S(2)}, u32[]{:S(2)}) collective-permute-start(bf16[64,512]{1,0:T(8,128)(2,1)S(1)} %get-tuple-element.74), channel_id=1, source_target_pairs={{0,2},{1,3},{2,0},{3,1},{4,6},{5,7},{6,4},{7,5},{8,10},{9,11},{10,... | collective-permute-start | bytes 196616 | tf_op jit(solution)/shard_map/ppermute | solution.py:538
  67.9 6.7 %collective-permute-start.25 = (bf16[64,512]{1,0:T(8,128)(2,1)S(1)}, bf16[64,512]{1,0:T(8,128)(2,1)S(1)}, u32[]{:S(2)}, u32[]{:S(2)}) collective-permute-start(bf16[64,512]{1,0:T(8,128)(2,1)S(1)} %get-tuple-element.75), channel_id=1, source_target_pairs={{0,3},{1,2},{2,1},{3,0},{4,7},{5,6},{6,5},{7,4},{8,11},{9,10},{10,... | collective-permute-start | bytes 196616 | tf_op jit(solution)/shard_map/ppermute | solution.py:538
  69.6 5.5 %collective-permute-start.26 = (bf16[64,512]{1,0:T(8,128)(2,1)S(1)}, bf16[64,512]{1,0:T(8,128)(2,1)S(1)}, u32[]{:S(2)}, u32[]{:S(2)}) collective-permute-start(bf16[64,512]{1,0:T(8,128)(2,1)S(1)} %get-tuple-element.77), channel_id=1, source_target_pairs={{0,1},{1,0},{2,3},{3,2},{4,5},{5,4},{6,7},{7,6},{8,9},{9,8},{10,11... | collective-permute-start | bytes 196616 | tf_op jit(solution)/shard_map/ppermute | solution.py:538
  (4 other events, 12.3 us)

commit v7 on v6

--- a/solution.py
+++ b/solution.py
@@ -55,71 +55,69 @@
     return pl.ds(pl.multiple_of(core * half + at, HEAD_DIM), size)
 
 
-def pack_body(place_ref, *refs):
-    sources, (mine_ref, other_ref, away_ref, tiles, tile_sem, sem) = refs[:4], refs[4:]
-    tokens, width = sources[0].shape
-    n_blocks = tokens // BLOCK
-    half = width // 2
-    copies = []
-    for i, source in enumerate(sources[1:3]):
-        for b in range(n_blocks):
-            row = i * n_blocks + b
-            tile = pl.ds((b + 1) * BLOCK - EDGE, EDGE)
-            copies.append(pltpu.make_async_copy(source.at[tile, :], tiles.at[row], tile_sem.at[row]))
-    columns = [
+def summary_rows(matrix):
+    blocks = range(BLOCK, matrix.shape[0] + 1, BLOCK)
+    return [lax.slice_in_dim(matrix, end - SUMMARY, end) for end in blocks]
+
+
+def away_body(at, place_ref, *refs):
+    sources, (out_ref, side_ref, sem) = refs[:4], refs[-3:]
+    half = sources[0].shape[1] // 2
+    copies = [
         pltpu.make_async_copy(
-            source.at[:, core_window(place_ref, 1, half, 0, half)], away_ref.at[i], sem.at[i]
+            source.at[:, core_window(place_ref, 1, half, at, out_ref.shape[2])],
+            out_ref.at[i],
+            sem.at[i],
         )
         for i, source in enumerate(sources)
     ]
-    for copy in copies + columns:
+    for copy in copies:
         copy.start()
+    side_ref[...] = jnp.full(side_ref.shape, place_ref[0] % 2, jnp.int32).astype(jnp.float32)
     for copy in copies:
         copy.wait()
-    for flip, target in enumerate((mine_ref, other_ref)):
-        to = core_window(place_ref, flip, half, 0, half)
-        rows = [tiles[row, EDGE - SUMMARY :, to] for row in range(2 * n_blocks)]
-        target[...] = jnp.concatenate(rows, axis=0)
-    for copy in columns:
-        copy.wait()
-
-
-def pack(place, arrays):
-    tokens, width = arrays[0].shape
-    kind = arrays[0].dtype
-    n_blocks = tokens // BLOCK
-    shape = jax.ShapeDtypeStruct((2 * n_blocks * SUMMARY, width // 2), kind)
-    return pl.pallas_call(
-        pack_body,
-        in_specs=[in_smem] + [in_hbm] * 4,
-        out_specs=[in_vmem] * 3,
-        out_shape=[shape] * 2 + [jax.ShapeDtypeStruct((4, tokens, width // 2), kind)],
-        scratch_shapes=[
-            pltpu.VMEM((2 * n_blocks, EDGE, width), kind),
-            pltpu.SemaphoreType.DMA((2 * n_blocks,)),
-            pltpu.SemaphoreType.DMA((4,)),
+
+
+def away_heads(place, arrays, at, size, *after):
+    tokens = arrays[0].shape[0]
+    return pl.pallas_call(
+        functools.partial(away_body, at),
+        in_specs=[in_smem] + [in_hbm] * 4 + [in_vmem] * len(after),
+        out_specs=[in_vmem] * 2,
+        out_shape=[
+            jax.ShapeDtypeStruct((4, tokens, size), arrays[0].dtype),
+            jax.ShapeDtypeStruct((8, 128), jnp.float32),
         ],
-        compiler_params=params,
-        name="pack",
-    )(place, *[pltpu.with_memory_space_constraint(x, pltpu.HBM) for x in arrays])
-
-
-def join_body(at, mine_ref, came_ref, *refs):
+        scratch_shapes=[pltpu.SemaphoreType.DMA((4,))],
+        compiler_params=params,
+        cost_estimate=pl.CostEstimate(
+            flops=0, bytes_accessed=16 * tokens * size, transcendentals=0
+        ),
+        name="away_heads",
+    )(place, *[pltpu.with_memory_space_constraint(x, pltpu.HBM) for x in arrays], *after)
+
+
+def join_body(at, side_ref, mine_ref, came_ref, *refs):
     ref = refs[-1]
-    rows, width = mine_ref.shape[0], ref.shape[1]
-    ref[:rows] = mine_ref[:, at : at + width]
-    ref[rows:] = came_ref[:, at : at + width]
-
-
-def join(mine, came, at, size, *after):
+    rows, width = mine_ref.shape
+    second = jnp.broadcast_to(side_ref[:1, :1], (rows, ref.shape[1])) > 0.5
+    for i, source in enumerate((mine_ref, came_ref)):
+        low, high = (
+            source[:, start : start + ref.shape[1]].astype(jnp.float32)
+            for start in (at, width // 2 + at)
+        )
+        ref[i * rows : (i + 1) * rows] = jnp.where(second, high, low).astype(ref.dtype)
+
+
+def join(side, mine, came, at, size, *after):
     return pl.pallas_call(
         functools.partial(join_body, at),
-        in_specs=[in_vmem] * (2 + len(after)),
+        in_specs=[in_vmem] * (3 + len(after)),
         out_specs=in_vmem,
         out_shape=jax.ShapeDtypeStruct((2 * mine.shape[0], size), mine.dtype),
         compiler_params=params,
         name="join",
-    )(mine, came, *after)
+    )(side, mine, came, *after)
 
 
 def stage_body(n_cols, nz, n_sum, place_ref, *refs):
@@ -193,7 +191,7 @@
 
     def head(to):
         q, k_loc, v_loc, g = (
-            jnp.concatenate([ref[i, :, here(to)] for ref in (mine_ref, came_ref)], axis=0)
+            jnp.concatenate([mine_ref[i, :, here(to)], came_ref[i, :, here(to)]], axis=0)
             for i in range(4)
         )
         k_far = far_rows(0, to)
@@ -548,16 +546,17 @@
 
     place = jnp.stack([lax.axis_index("seq"), lax.axis_index("head")]).astype(jnp.int32)
     arrays = (queries, keys_in, values_in, cotangent)
-    mine, other, part = pack(place, arrays)
-    came = over_seq(other, 1)
-    pair = over_z(join(mine, came, 0, mine.shape[1]), 1)
+    mine = jnp.concatenate(summary_rows(keys_in) + summary_rows(values_in), axis=0)
+    came = over_seq(mine, 1)
+    part, side = away_heads(place, arrays, 0, queries.shape[1] // 2)
+    pair = over_z(join(side, mine, came, 0, mine.shape[1] // 2), 1)
     ours, mask = stage(place, arrays, n_cols, nz)
     columns = []
     theirs = over_seq(hold([part], came)[0], 1)
     for c in range(n_chunks):
         width = chunk_heads[c] * HEAD_DIM
         at = firsts[c] * HEAD_DIM
-        own = join(mine, came, at, width, *[cols[0] for cols in columns[-1:]])
+        own = join(side, mine, came, at, width, *[cols[0] for cols in columns[-1:]])
         far = swap_far([own] * nz)
         line = stack_line(own, pair, far, at, *([cols[-1] for cols in columns[-1:]] or [theirs, mask]))
         columns.append([line] + swap_columns([line] * n_cols))

time: 78 us -> 77.7 us (level)
  starting transfers between devices: 33.7 us -> 31.7 us
  local copies, waits for them, and re-layouts: 0 us -> 0.82 us
  waiting for transfers between devices: 22.1 us -> 22.9 us
    ppermute x12, waiting for transfers between devices: 19.8 us -> 21 us  [over_z(): return lax.ppermute(array, 'head', [(i, i ^ bits) for i in range(nz)])]
    ppermute x12, starting transfers between devices: 17.4 us -> 16.4 us  [over_z(): return lax.ppermute(array, 'head', [(i, i ^ bits) for i in range(nz)])]
    ppermute x16, starting transfers between devices: 16.3 us -> 15.3 us  [over_seq(): return lax.ppermute(array, 'seq', [(i, i ^ bits) for i in range(n_seq)])]
    slice x0 -> x1, local copies, waits for them, and re-layouts: none -> 0.82 us  [summary_rows(): return [lax.slice_in_dim(matrix, end - SUMMARY, end) for end in blocks]]
  transfers between devices with their start and end apart: 28 -> 28, of which waited for: 13 -> 12; matrix products, arithmetic and copies ran while one was open for 0% -> 0% of each run, Pallas kernels for 22% -> 25%
where the time goes in v7:
time: 77.7 us; the launch traced here: 77.5 us
  starting transfers between devices  31.7 us (41%)
  waiting for transfers between devices  22.9 us (29%)
  Pallas kernels  21.2 us (27%)
  between operations  0.83 us (1%)
  local copies, waits for them, and re-layouts  0.82 us (1%)
    ppermute x12, waiting for transfers between devices, over_z(): return lax.ppermute(array, 'head', [(i, i ^ bits) for i in range(nz)])  21 us
    ppermute x12, starting transfers between devices, over_z(): return lax.ppermute(array, 'head', [(i, i ^ bits) for i in range(nz)])  16.4 us
    ppermute x16, starting transfers between devices, over_seq(): return lax.ppermute(array, 'seq', [(i, i ^ bits) for i in range(n_seq)])  15.3 us
    pallas_call x2, Pallas kernels, attention(): pl.pallas_call(functools.partial(attention_body, n_sum, n_cols, n_skip, f...  12.4 us
    pallas_call x1, Pallas kernels, settle(): pl.pallas_call(settle_body, in_specs=[in_smem, in_vmem, in_vmem], out_spe...  2.62 us
    pallas_call x1, Pallas kernels, away_heads(): pl.pallas_call(functools.partial(away_body, at), in_specs=[in_smem] + [in...  2.1 us
    pallas_call x1, Pallas kernels, stage(): pl.pallas_call(functools.partial(stage_body, n_cols, nz, n_sum), in_specs...  2.1 us
    ppermute x16, waiting for transfers between devices, over_seq(): return lax.ppermute(array, 'seq', [(i, i ^ bits) for i in range(n_seq)])  1.96 us
  transfers between devices with their start and end apart: 28, of which 12 were waited for; matrix products, arithmetic and copies ran while one was open for 0% of the time, Pallas kernels for 25%

profile of v7, /device:TPU:0, one launch (start us, length us, event | category | flops | bytes accessed | tf_op | source)
XLA Modules:
  0.0 77.5 jit_solution(8168383307294435169)
XLA Ops:
  2.1 2.1 %away_heads.1 = (bf16[4,256,1024]{2,1,0:T(8,128)(2,1)S(1)}, f32[8,128]{1,0:T(8,128)S(1)}) custom-call(s32[2]{0:T(128)S(1)} %pad_add_fusion.place_ref, bf16[256,2048]{1,0:T(8,128)(2,1)} %refs_0_.3, bf16[256,2048]{1,0:T(8,128)(2,1)} %refs_1_.3, bf16[256,2048]{1,0:T(8,128)(2,1)} %refs_2_.3, bf16[256,2048]{1,0:T(8,128)(2,1)} %refs_3_.3), custom_call_target="tpu_custom_call" | custom-call | bytes 4194304 | tf_op jit(solution)/shard_map/away_heads/pallas_call | solution.py:83
  4.4 3.1 %collective-permute-start.2 = (bf16[64,1024]{1,0:T(8,128)(2,1)S(1)}, bf16[64,1024]{1,0:T(8,128)(2,1)S(1)}, u32[]{:S(2)}, u32[]{:S(2)}) collective-permute-start(bf16[64,1024]{1,0:T(8,128)(2,1)S(1)} %join.4), channel_id=1, source_target_pairs={{0,1},{1,0},{2,3},{3,2},{4,5},{5,4},{6,7},{7,6},{8,9},{9,8},{10,11... | collective-permute-start | bytes 393224 | tf_op jit(solution)/shard_map/ppermute | solution.py:536
  7.5 2.5 %collective-permute-start.4 = (bf16[64,512]{1,0:T(8,128)(2,1)S(1)}, bf16[64,512]{1,0:T(8,128)(2,1)S(1)}, u32[]{:S(2)}, u32[]{:S(2)}) collective-permute-start(bf16[64,512]{1,0:T(8,128)(2,1)S(1)} %join.3.own_ref), channel_id=1, source_target_pairs={{0,3},{1,2},{2,1},{3,0},{4,7},{5,6},{6,5},{7,4},{8,11},{9,10},{10,... | collective-permute-start | bytes 196616 | tf_op jit(solution)/shard_map/ppermute | solution.py:536
  10.3 2.1 %stage.1 = (bf16[4,256,1024]{2,1,0:T(8,128)(2,1)S(1)}, f32[512,512]{1,0:T(8,128)S(1)}) custom-call(s32[2]{0:T(128)S(1)} %pad_add_fusion.place_ref, bf16[256,2048]{1,0:T(8,128)(2,1)} %refs_0_.3, bf16[256,2048]{1,0:T(8,128)(2,1)} %refs_1_.3, bf16[256,2048]{1,0:T(8,128)(2,1)} %refs_2_.3, bf16[256,2048]{1,0:T(8,128)(2,1)} %refs_3_.3), custom_call_target="tpu_custom_call" | custom-call | bytes 4194304 | tf_op jit(solution)/shard_map/stage/pallas_call | solution.py:144
  12.4 3.2 %collective-permute-done.4.refs_1_ = bf16[64,512]{1,0:T(8,128)(2,1)S(1)} collective-permute-done((bf16[64,512]{1,0:T(8,128)(2,1)S(1)}, bf16[64,512]{1,0:T(8,128)(2,1)S(1)}, u32[]{:S(2)}, u32[]{:S(2)}) %collective-permute-start.4) | collective-permute-done | bytes 65568 | tf_op jit(solution)/shard_map/ppermute | solution.py:536
  17.0 2.5 %collective-permute-start.7 = (bf16[4,64,512]{2,1,0:T(8,128)(2,1)S(1)}, bf16[4,64,512]{2,1,0:T(8,128)(2,1)S(1)}, u32[]{:S(2)}, u32[]{:S(2)}) collective-permute-start(bf16[4,64,512]{2,1,0:T(8,128)(2,1)S(1)} %line.2.refs_0_.refs_3_), channel_id=1, source_target_pairs={{0,24},{4,28},{8,16},{12,20},{16,8},{20,12},{24,0},{28,4},{1,25},{... | collective-permute-start | bytes 786440 | tf_op jit(solution)/shard_map/ppermute | solution.py:539
  20.6 2.4 %collective-permute-start.6 = (bf16[64,512]{1,0:T(8,128)(2,1)S(1)}, bf16[64,512]{1,0:T(8,128)(2,1)S(1)}, u32[]{:S(2)}, u32[]{:S(2)}) collective-permute-start(bf16[64,512]{1,0:T(8,128)(2,1)S(1)} %join.5.own_ref), channel_id=1, source_target_pairs={{0,3},{1,2},{2,1},{3,0},{4,7},{5,6},{6,5},{7,4},{8,11},{9,10},{10,... | collective-permute-start | bytes 196616 | tf_op jit(solution)/shard_map/ppermute | solution.py:536
  22.9 3.8 %collective-permute-done.6.refs_1_ = bf16[64,512]{1,0:T(8,128)(2,1)S(1)} collective-permute-done((bf16[64,512]{1,0:T(8,128)(2,1)S(1)}, bf16[64,512]{1,0:T(8,128)(2,1)S(1)}, u32[]{:S(2)}, u32[]{:S(2)}) %collective-permute-start.6) | collective-permute-done | bytes 65568 | tf_op jit(solution)/shard_map/ppermute | solution.py:536
  26.7 1.4 %collective-permute-done.5.refs_0_ = bf16[64,512]{1,0:T(8,128)(2,1)S(1)} collective-permute-done((bf16[64,512]{1,0:T(8,128)(2,1)S(1)}, bf16[64,512]{1,0:T(8,128)(2,1)S(1)}, u32[]{:S(2)}, u32[]{:S(2)}) %collective-permute-start.5) | collective-permute-done | bytes 65568 | tf_op jit(solution)/shard_map/ppermute | solution.py:536
  28.1 1.6 %collective-permute-start.9 = (bf16[4,64,512]{2,1,0:T(8,128)(2,1)S(1)}, bf16[4,64,512]{2,1,0:T(8,128)(2,1)S(1)}, u32[]{:S(2)}, u32[]{:S(2)}) collective-permute-start(bf16[4,64,512]{2,1,0:T(8,128)(2,1)S(1)} %line.3.refs_7_.refs_3_), channel_id=1, source_target_pairs={{0,16},{4,20},{8,24},{12,28},{16,0},{20,4},{24,8},{28,12},{1,17},{... | collective-permute-start | bytes 786440 | tf_op jit(solution)/shard_map/ppermute | solution.py:539
  29.7 1.5 %collective-permute-start.8 = (bf16[4,64,512]{2,1,0:T(8,128)(2,1)S(1)}, bf16[4,64,512]{2,1,0:T(8,128)(2,1)S(1)}, u32[]{:S(2)}, u32[]{:S(2)}) collective-permute-start(bf16[4,64,512]{2,1,0:T(8,128)(2,1)S(1)} %line.3.refs_7_.refs_3_), channel_id=1, source_target_pairs={{0,8},{4,12},{8,0},{12,4},{16,24},{20,28},{24,16},{28,20},{1,9},{5... | collective-permute-start | bytes 786440 | tf_op jit(solution)/shard_map/ppermute | solution.py:539
  31.7 6.2 %attention.2 = (bf16[4,256,1024]{2,1,0:T(8,128)(2,1)S(1)}, bf16[4,256,1024]{2,1,0:T(8,128)(2,1)S(1)}, f32[2,64,512]{2,1,0:T(8,128)S(1)}, bf16[4,64,512]{2,1,0:T(...) custom-call(bf16[4,256,1024]{2,1,0:T(8,128)(2,1)S(1)} %get-tuple-ele, ...), custom_call_target="tpu_custom_call" | custom-call | flops 2013265920 | bytes 6291456 | tf_op jit(solution)/shard_map/attention/pallas_call | solution.py:271
  39.6 1.5 %collective-permute-start.14 = (bf16[4,64,512]{2,1,0:T(8,128)(2,1)S(1)}, bf16[4,64,512]{2,1,0:T(8,128)(2,1)S(1)}, u32[]{:S(2)}, u32[]{:S(2)}) collective-permute-start(bf16[4,64,512]{2,1,0:T(8,128)(2,1)S(1)} %hold.8), channel_id=1, source_target_pairs={{0,8},{4,12},{8,0},{12,4},{16,24},{20,28},{24,16},{28,20},{1,9},{5... | collective-permute-start | bytes 786440 | tf_op jit(solution)/shard_map/ppermute | solution.py:539
  41.1 1.9 %collective-permute-done.13.came_ref = bf16[2,64,512]{2,1,0:T(8,128)(2,1)S(1)} collective-permute-done((bf16[2,64,512]{2,1,0:T(8,128)(2,1)S(1)}, bf16[2,64,512]{2,1,0:T(8,128)(2,1)S(1)}, u32[]{:S(2)}, u32[]{:S(2)}) %collective-permute-start.13) | collective-permute-done | bytes 131104 | tf_op jit(solution)/shard_map/ppermute | solution.py:536
  43.0 2.5 %collective-permute-start.19 = (bf16[2,64,512]{2,1,0:T(8,128)(2,1)S(1)}, bf16[2,64,512]{2,1,0:T(8,128)(2,1)S(1)}, u32[]{:S(2)}, u32[]{:S(2)}) collective-permute-start(bf16[2,64,512]{2,1,0:T(8,128)(2,1)S(1)} %pair_sum.2.refs_9_), channel_id=1, source_target_pairs={{0,24},{4,28},{8,16},{12,20},{16,8},{20,12},{24,0},{28,4},{1,25},{... | collective-permute-start | bytes 393224 | tf_op jit(solution)/shard_map/ppermute | solution.py:539
  45.5 6.2 %attention.3 = (bf16[4,256,1024]{2,1,0:T(8,128)(2,1)S(1)}, bf16[4,256,1024]{2,1,0:T(8,128)(2,1)S(1)}, f32[2,64,512]{2,1,0:T(8,128)S(1)}, bf16[4,64,512]{2,1,0:T(...) custom-call(bf16[4,256,1024]{2,1,0:T(8,128)(2,1)S(1)} %get-tuple-ele, ...), custom_call_target="tpu_custom_call", output_to_operand_aliasing={{0}: (7, {}), {1}: (8, {})} | custom-call | flops 2013265920 | bytes 6291456 | tf_op jit(solution)/shard_map/attention/pallas_call | solution.py:271
  52.5 1.5 %collective-permute-start.17 = (bf16[4,64,512]{2,1,0:T(8,128)(2,1)S(1)}, bf16[4,64,512]{2,1,0:T(8,128)(2,1)S(1)}, u32[]{:S(2)}, u32[]{:S(2)}) collective-permute-start(bf16[4,64,512]{2,1,0:T(8,128)(2,1)S(1)} %hold.11), channel_id=1, source_target_pairs={{0,16},{4,20},{8,24},{12,28},{16,0},{20,4},{24,8},{28,12},{1,17},{... | collective-permute-start | bytes 786440 | tf_op jit(solution)/shard_map/ppermute | solution.py:539
  55.1 1.7 %collective-permute-done.18.came_ref = bf16[2,64,512]{2,1,0:T(8,128)(2,1)S(1)} collective-permute-done((bf16[2,64,512]{2,1,0:T(8,128)(2,1)S(1)}, bf16[2,64,512]{2,1,0:T(8,128)(2,1)S(1)}, u32[]{:S(2)}, u32[]{:S(2)}) %collective-permute-start.18) | collective-permute-done | bytes 131104 | tf_op jit(solution)/shard_map/ppermute | solution.py:536
  57.6 2.1 %collective-permute-done.21.refs_2_ = bf16[2,64,512]{2,1,0:T(8,128)(2,1)S(1)} collective-permute-done((bf16[2,64,512]{2,1,0:T(8,128)(2,1)S(1)}, bf16[2,64,512]{2,1,0:T(8,128)(2,1)S(1)}, u32[]{:S(2)}, u32[]{:S(2)}) %collective-permute-start.21) | collective-permute-done | bytes 131104 | tf_op jit(solution)/shard_map/ppermute | solution.py:536
  59.8 2.4 %collective-permute-start.22 = (bf16[1,64,512]{2,1,0:T(8,128)(2,1)S(1)}, bf16[1,64,512]{2,1,0:T(8,128)(2,1)S(1)}, u32[]{:S(2)}, u32[]{:S(2)}) collective-permute-start(bf16[1,64,512]{2,1,0:T(8,128)(2,1)S(1)} %get-tuple-element.64), channel_id=1, source_target_pairs={{0,2},{1,3},{2,0},{3,1},{4,6},{5,7},{6,4},{7,5},{8,10},{9,11},{10,... | collective-permute-start | bytes 196616 | tf_op jit(solution)/shard_map/ppermute | solution.py:536
  62.1 3.3 %collective-permute-done.22.refs_4_.refs_2_ = bf16[1,64,512]{2,1,0:T(8,128)(2,1)S(1)} collective-permute-done((bf16[1,64,512]{2,1,0:T(8,128)(2,1)S(1)}, bf16[1,64,512]{2,1,0:T(8,128)(2,1)S(1)}, u32[]{:S(2)}, u32[]{:S(2)}) %collective-permute-start.22) | collective-permute-done | bytes 65568 | tf_op jit(solution)/shard_map/ppermute | solution.py:536
  65.7 2.0 %collective-permute-start.24 = (bf16[64,512]{1,0:T(8,128)(2,1)S(1)}, bf16[64,512]{1,0:T(8,128)(2,1)S(1)}, u32[]{:S(2)}, u32[]{:S(2)}) collective-permute-start(bf16[64,512]{1,0:T(8,128)(2,1)S(1)} %get-tuple-element.72), channel_id=1, source_target_pairs={{0,2},{1,3},{2,0},{3,1},{4,6},{5,7},{6,4},{7,5},{8,10},{9,11},{10,... | collective-permute-start | bytes 196616 | tf_op jit(solution)/shard_map/ppermute | solution.py:536
  69.8 2.6 %settle.1 = (bf16[256,2048]{1,0:T(8,128)(2,1)}, bf16[256,2048]{1,0:T(8,128)(2,1)}, bf16[256,2048]{1,0:T(8,128)(2,1)}, bf16[256,2048]{1,0:T(8,128)(2,1)}, f32[8,128]{1,0:T(8,128)S(1)}) custom-call(s32[2]{0:T(128)S(1)} %pad_add_fusion.place_ref, bf16[4,256,1024]{2,1,0:T(8,128)(2,1)S(1)} %get-tuple-element.50.own_ref, ...), custom_call_target="tpu_custom_call" | custom-call | tf_op jit(solution)/shard_map/settle/pallas_call | solution.py:479
  72.5 1.9 %collective-permute-done.25.refs_2_ = bf16[64,512]{1,0:T(8,128)(2,1)S(1)} collective-permute-done((bf16[64,512]{1,0:T(8,128)(2,1)S(1)}, bf16[64,512]{1,0:T(8,128)(2,1)S(1)}, u32[]{:S(2)}, u32[]{:S(2)}) %collective-permute-start.25) | collective-permute-done | bytes 65568 | tf_op jit(solution)/shard_map/ppermute | solution.py:536
  (60 shorter events, 14.9 us)
Async XLA Ops:
  4.2 12.7 %collective-permute-start.1 = (bf16[4,256,1024]{2,1,0:T(8,128)(2,1)S(1)}, bf16[4,256,1024]{2,1,0:T(8,128)(2,1)S(1)}, u32[]{:S(2)}, u32[]{:S(2)}) collective-permute-start(bf16[4,256,1024]{2,1,0:T(8,128)(2,1)S(1)} %hold.7), channel_id=1, source_target_pairs={{0,4},{4,0},{8,12},{12,8},{16,20},{20,16},{24,28},{28,24},{1,5},{5... | collective-permute-start | bytes 6291464 | tf_op jit(solution)/shard_map/ppermute | solution.py:539
  4.4 12.5 %collective-permute-start.2 = (bf16[64,1024]{1,0:T(8,128)(2,1)S(1)}, bf16[64,1024]{1,0:T(8,128)(2,1)S(1)}, u32[]{:S(2)}, u32[]{:S(2)}) collective-permute-start(bf16[64,1024]{1,0:T(8,128)(2,1)S(1)} %join.4), channel_id=1, source_target_pairs={{0,1},{1,0},{2,3},{3,2},{4,5},{5,4},{6,7},{7,6},{8,9},{9,8},{10,11... | collective-permute-start | bytes 393224 | tf_op jit(solution)/shard_map/ppermute | solution.py:536
  7.5 8.0 %collective-permute-start.4 = (bf16[64,512]{1,0:T(8,128)(2,1)S(1)}, bf16[64,512]{1,0:T(8,128)(2,1)S(1)}, u32[]{:S(2)}, u32[]{:S(2)}) collective-permute-start(bf16[64,512]{1,0:T(8,128)(2,1)S(1)} %join.3.own_ref), channel_id=1, source_target_pairs={{0,3},{1,2},{2,1},{3,0},{4,7},{5,6},{6,5},{7,4},{8,11},{9,10},{10,... | collective-permute-start | bytes 196616 | tf_op jit(solution)/shard_map/ppermute | solution.py:536
  10.1 6.9 %collective-permute-start.3 = (bf16[64,512]{1,0:T(8,128)(2,1)S(1)}, bf16[64,512]{1,0:T(8,128)(2,1)S(1)}, u32[]{:S(2)}, u32[]{:S(2)}) collective-permute-start(bf16[64,512]{1,0:T(8,128)(2,1)S(1)} %join.3.own_ref), channel_id=1, source_target_pairs={{0,2},{1,3},{2,0},{3,1},{4,6},{5,7},{6,4},{7,5},{8,10},{9,11},{10,... | collective-permute-start | bytes 196616 | tf_op jit(solution)/shard_map/ppermute | solution.py:536
  17.0 11.1 %collective-permute-start.7 = (bf16[4,64,512]{2,1,0:T(8,128)(2,1)S(1)}, bf16[4,64,512]{2,1,0:T(8,128)(2,1)S(1)}, u32[]{:S(2)}, u32[]{:S(2)}) collective-permute-start(bf16[4,64,512]{2,1,0:T(8,128)(2,1)S(1)} %line.2.refs_0_.refs_3_), channel_id=1, source_target_pairs={{0,24},{4,28},{8,16},{12,20},{16,8},{20,12},{24,0},{28,4},{1,25},{... | collective-permute-start | bytes 786440 | tf_op jit(solution)/shard_map/ppermute | solution.py:539
  19.5 12.2 %collective-permute-start.12 = (bf16[4,64,512]{2,1,0:T(8,128)(2,1)S(1)}, bf16[4,64,512]{2,1,0:T(8,128)(2,1)S(1)}, u32[]{:S(2)}, u32[]{:S(2)}) collective-permute-start(bf16[4,64,512]{2,1,0:T(8,128)(2,1)S(1)} %line.2.refs_0_.refs_3_), channel_id=1, source_target_pairs={{0,16},{4,20},{8,24},{12,28},{16,0},{20,4},{24,8},{28,12},{1,17},{... | collective-permute-start | bytes 786440 | tf_op jit(solution)/shard_map/ppermute | solution.py:539
  20.0 11.7 %collective-permute-start.11 = (bf16[4,64,512]{2,1,0:T(8,128)(2,1)S(1)}, bf16[4,64,512]{2,1,0:T(8,128)(2,1)S(1)}, u32[]{:S(2)}, u32[]{:S(2)}) collective-permute-start(bf16[4,64,512]{2,1,0:T(8,128)(2,1)S(1)} %line.2.refs_0_.refs_3_), channel_id=1, source_target_pairs={{0,8},{4,12},{8,0},{12,4},{16,24},{20,28},{24,16},{28,20},{1,9},{5... | collective-permute-start | bytes 786440 | tf_op jit(solution)/shard_map/ppermute | solution.py:539
  20.6 6.1 %collective-permute-start.6 = (bf16[64,512]{1,0:T(8,128)(2,1)S(1)}, bf16[64,512]{1,0:T(8,128)(2,1)S(1)}, u32[]{:S(2)}, u32[]{:S(2)}) collective-permute-start(bf16[64,512]{1,0:T(8,128)(2,1)S(1)} %join.5.own_ref), channel_id=1, source_target_pairs={{0,3},{1,2},{2,1},{3,0},{4,7},{5,6},{6,5},{7,4},{8,11},{9,10},{10,... | collective-permute-start | bytes 196616 | tf_op jit(solution)/shard_map/ppermute | solution.py:536
  22.9 5.2 %collective-permute-start.5 = (bf16[64,512]{1,0:T(8,128)(2,1)S(1)}, bf16[64,512]{1,0:T(8,128)(2,1)S(1)}, u32[]{:S(2)}, u32[]{:S(2)}) collective-permute-start(bf16[64,512]{1,0:T(8,128)(2,1)S(1)} %join.5.own_ref), channel_id=1, source_target_pairs={{0,2},{1,3},{2,0},{3,1},{4,6},{5,7},{6,4},{7,5},{8,10},{9,11},{10,... | collective-permute-start | bytes 196616 | tf_op jit(solution)/shard_map/ppermute | solution.py:536
  28.1 10.9 %collective-permute-start.9 = (bf16[4,64,512]{2,1,0:T(8,128)(2,1)S(1)}, bf16[4,64,512]{2,1,0:T(8,128)(2,1)S(1)}, u32[]{:S(2)}, u32[]{:S(2)}) collective-permute-start(bf16[4,64,512]{2,1,0:T(8,128)(2,1)S(1)} %line.3.refs_7_.refs_3_), channel_id=1, source_target_pairs={{0,16},{4,20},{8,24},{12,28},{16,0},{20,4},{24,8},{28,12},{1,17},{... | collective-permute-start | bytes 786440 | tf_op jit(solution)/shard_map/ppermute | solution.py:539
  29.7 9.9 %collective-permute-start.8 = (bf16[4,64,512]{2,1,0:T(8,128)(2,1)S(1)}, bf16[4,64,512]{2,1,0:T(8,128)(2,1)S(1)}, u32[]{:S(2)}, u32[]{:S(2)}) collective-permute-start(bf16[4,64,512]{2,1,0:T(8,128)(2,1)S(1)} %line.3.refs_7_.refs_3_), channel_id=1, source_target_pairs={{0,8},{4,12},{8,0},{12,4},{16,24},{20,28},{24,16},{28,20},{1,9},{5... | collective-permute-start | bytes 786440 | tf_op jit(solution)/shard_map/ppermute | solution.py:539
  31.2 14.3 %collective-permute-start.10 = (bf16[4,64,512]{2,1,0:T(8,128)(2,1)S(1)}, bf16[4,64,512]{2,1,0:T(8,128)(2,1)S(1)}, u32[]{:S(2)}, u32[]{:S(2)}) collective-permute-start(bf16[4,64,512]{2,1,0:T(8,128)(2,1)S(1)} %line.3.refs_7_.refs_3_), channel_id=1, source_target_pairs={{0,24},{4,28},{8,16},{12,20},{16,8},{20,12},{24,0},{28,4},{1,25},{... | collective-permute-start | bytes 786440 | tf_op jit(solution)/shard_map/ppermute | solution.py:539
  37.9 5.0 %collective-permute-start.13 = (bf16[2,64,512]{2,1,0:T(8,128)(2,1)S(1)}, bf16[2,64,512]{2,1,0:T(8,128)(2,1)S(1)}, u32[]{:S(2)}, u32[]{:S(2)}) collective-permute-start(bf16[2,64,512]{2,1,0:T(8,128)(2,1)S(1)} %get-tuple-element.49), channel_id=1, source_target_pairs={{0,1},{1,0},{2,3},{3,2},{4,5},{5,4},{6,7},{7,6},{8,9},{9,8},{10,11... | collective-permute-start | bytes 393224 | tf_op jit(solution)/shard_map/ppermute | solution.py:536
  39.0 12.7 %collective-permute-start.16 = (bf16[4,64,512]{2,1,0:T(8,128)(2,1)S(1)}, bf16[4,64,512]{2,1,0:T(8,128)(2,1)S(1)}, u32[]{:S(2)}, u32[]{:S(2)}) collective-permute-start(bf16[4,64,512]{2,1,0:T(8,128)(2,1)S(1)} %hold.10), channel_id=1, source_target_pairs={{0,16},{4,20},{8,24},{12,28},{16,0},{20,4},{24,8},{28,12},{1,17},{... | collective-permute-start | bytes 786440 | tf_op jit(solution)/shard_map/ppermute | solution.py:539
  39.6 12.3 %collective-permute-start.14 = (bf16[4,64,512]{2,1,0:T(8,128)(2,1)S(1)}, bf16[4,64,512]{2,1,0:T(8,128)(2,1)S(1)}, u32[]{:S(2)}, u32[]{:S(2)}) collective-permute-start(bf16[4,64,512]{2,1,0:T(8,128)(2,1)S(1)} %hold.8), channel_id=1, source_target_pairs={{0,8},{4,12},{8,0},{12,4},{16,24},{20,28},{24,16},{28,20},{1,9},{5... | collective-permute-start | bytes 786440 | tf_op jit(solution)/shard_map/ppermute | solution.py:539
  43.0 10.9 %collective-permute-start.19 = (bf16[2,64,512]{2,1,0:T(8,128)(2,1)S(1)}, bf16[2,64,512]{2,1,0:T(8,128)(2,1)S(1)}, u32[]{:S(2)}, u32[]{:S(2)}) collective-permute-start(bf16[2,64,512]{2,1,0:T(8,128)(2,1)S(1)} %pair_sum.2.refs_9_), channel_id=1, source_target_pairs={{0,24},{4,28},{8,16},{12,20},{16,8},{20,12},{24,0},{28,4},{1,25},{... | collective-permute-start | bytes 393224 | tf_op jit(solution)/shard_map/ppermute | solution.py:539
  51.9 13.6 %collective-permute-start.15 = (bf16[4,64,512]{2,1,0:T(8,128)(2,1)S(1)}, bf16[4,64,512]{2,1,0:T(8,128)(2,1)S(1)}, u32[]{:S(2)}, u32[]{:S(2)}) collective-permute-start(bf16[4,64,512]{2,1,0:T(8,128)(2,1)S(1)} %hold.9), channel_id=1, source_target_pairs={{0,8},{4,12},{8,0},{12,4},{16,24},{20,28},{24,16},{28,20},{1,9},{5... | collective-permute-start | bytes 786440 | tf_op jit(solution)/shard_map/ppermute | solution.py:539
  52.5 13.0 %collective-permute-start.17 = (bf16[4,64,512]{2,1,0:T(8,128)(2,1)S(1)}, bf16[4,64,512]{2,1,0:T(8,128)(2,1)S(1)}, u32[]{:S(2)}, u32[]{:S(2)}) collective-permute-start(bf16[4,64,512]{2,1,0:T(8,128)(2,1)S(1)} %hold.11), channel_id=1, source_target_pairs={{0,16},{4,20},{8,24},{12,28},{16,0},{20,4},{24,8},{28,12},{1,17},{... | collective-permute-start | bytes 786440 | tf_op jit(solution)/shard_map/ppermute | solution.py:539
  54.0 5.7 %collective-permute-start.21 = (bf16[2,64,512]{2,1,0:T(8,128)(2,1)S(1)}, bf16[2,64,512]{2,1,0:T(8,128)(2,1)S(1)}, u32[]{:S(2)}, u32[]{:S(2)}) collective-permute-start(bf16[2,64,512]{2,1,0:T(8,128)(2,1)S(1)} %get-tuple-element.63), channel_id=1, source_target_pairs={{0,1},{1,0},{2,3},{3,2},{4,5},{5,4},{6,7},{7,6},{8,9},{9,8},{10,11... | collective-permute-start | bytes 393224 | tf_op jit(solution)/shard_map/ppermute | solution.py:536
  56.8 8.6 %collective-permute-start.20 = (bf16[2,64,512]{2,1,0:T(8,128)(2,1)S(1)}, bf16[2,64,512]{2,1,0:T(8,128)(2,1)S(1)}, u32[]{:S(2)}, u32[]{:S(2)}) collective-permute-start(bf16[2,64,512]{2,1,0:T(8,128)(2,1)S(1)} %pair_sum.3), channel_id=1, source_target_pairs={{0,24},{4,28},{8,16},{12,20},{16,8},{20,12},{24,0},{28,4},{1,25},{... | collective-permute-start | bytes 393224 | tf_op jit(solution)/shard_map/ppermute | solution.py:539
  59.8 5.7 %collective-permute-start.22 = (bf16[1,64,512]{2,1,0:T(8,128)(2,1)S(1)}, bf16[1,64,512]{2,1,0:T(8,128)(2,1)S(1)}, u32[]{:S(2)}, u32[]{:S(2)}) collective-permute-start(bf16[1,64,512]{2,1,0:T(8,128)(2,1)S(1)} %get-tuple-element.64), channel_id=1, source_target_pairs={{0,2},{1,3},{2,0},{3,1},{4,6},{5,7},{6,4},{7,5},{8,10},{9,11},{10,... | collective-permute-start | bytes 196616 | tf_op jit(solution)/shard_map/ppermute | solution.py:536
  65.7 6.8 %collective-permute-start.24 = (bf16[64,512]{1,0:T(8,128)(2,1)S(1)}, bf16[64,512]{1,0:T(8,128)(2,1)S(1)}, u32[]{:S(2)}, u32[]{:S(2)}) collective-permute-start(bf16[64,512]{1,0:T(8,128)(2,1)S(1)} %get-tuple-element.72), channel_id=1, source_target_pairs={{0,2},{1,3},{2,0},{3,1},{4,6},{5,7},{6,4},{7,5},{8,10},{9,11},{10,... | collective-permute-start | bytes 196616 | tf_op jit(solution)/shard_map/ppermute | solution.py:536
  67.6 6.7 %collective-permute-start.25 = (bf16[64,512]{1,0:T(8,128)(2,1)S(1)}, bf16[64,512]{1,0:T(8,128)(2,1)S(1)}, u32[]{:S(2)}, u32[]{:S(2)}) collective-permute-start(bf16[64,512]{1,0:T(8,128)(2,1)S(1)} %get-tuple-element.73), channel_id=1, source_target_pairs={{0,3},{1,2},{2,1},{3,0},{4,7},{5,6},{6,5},{7,4},{8,11},{9,10},{10,... | collective-permute-start | bytes 196616 | tf_op jit(solution)/shard_map/ppermute | solution.py:536
  68.0 6.7 %collective-permute-start.26 = (bf16[64,512]{1,0:T(8,128)(2,1)S(1)}, bf16[64,512]{1,0:T(8,128)(2,1)S(1)}, u32[]{:S(2)}, u32[]{:S(2)}) collective-permute-start(bf16[64,512]{1,0:T(8,128)(2,1)S(1)} %get-tuple-element.75), channel_id=1, source_target_pairs={{0,1},{1,0},{2,3},{3,2},{4,5},{5,4},{6,7},{7,6},{8,9},{9,8},{10,11... | collective-permute-start | bytes 196616 | tf_op jit(solution)/shard_map/ppermute | solution.py:536
  (4 other events, 13.4 us)
